TPU v7x, 128 devices: a whole 4x4x4 slice. The times are simulated.
128 devices in a mesh: ctx: 16 (over y, z), head: 8 (over x, core).
Axes of the slice: x: 4, y: 4, z: 4, core: 2. Of those that a mesh axis runs over, the one named last changes fastest.
Arguments:
- queries: bfloat16 [12288, 4096], P(('ctx', 'head')), may hold values from -64 to 64
- keys: bfloat16 [12288, 1024], P(('ctx', 'head')), may hold values from -6 to 6
- values: bfloat16 [12288, 1024], P(('ctx', 'head')), may hold values from -6 to 6
- grad_out: bfloat16 [12288, 4096], P(('ctx', 'head')), may hold values from -6 to 6
- parent: int32 [48], replicated, may hold values from -1 to 46, as said below
- subtree_end: int32 [12288], P('ctx'), may hold values from 0 to 255, as said below
Outputs:
- attn_out: bfloat16 [12288, 4096], P(('ctx', 'head'))
- grad_q: bfloat16 [12288, 4096], P(('ctx', 'head'))
- grad_k: bfloat16 [12288, 1024], P(('ctx', 'head'))
- grad_v: bfloat16 [12288, 1024], P(('ctx', 'head'))
Inputs may be any that keep to these rules, and one draw needn't show every extreme that they name: Device c of ctx holds blocks c * 3 to (c + 1) * 3 - 1. Block 0 is the only root. A block that is not first on its device has its parent among the earlier blocks of its device, and the last block of each device has the block just before it as parent; the first block of device c > 0 has as parent the first block of an earlier device. Along parents, a block meets the first blocks of at most 4 other devices, and some block meets exactly 4: devices 0 to 4 form a chain of first blocks. In each block the positions follow a depth-first order of a token tree whose root is the block's first token: subtree_end[t] is the last in-block position of t's subtree, at least t's own position, and subtrees nest.
All inputs are finite; a program needn't handle non-finite values.
Results may differ from a plain program's by a relative error of at most 0.035.
Values may be sent and summed in bfloat16 or wider, within the bound.
No kernel may reach another device: no remote copies, remote signals or barrier semaphores. Data moves between devices by JAX's collectives and lax.ppermute only.
A program may use at most 64 MiB of HBM per device.

v0:
```python
import jax
import jax.numpy as jnp
from jax import lax
from jax.sharding import PartitionSpec as P

HQ = 32
KVH = 8
HD = 128
BLK = 256
DMAX = 4


def chain_of(parent, start, steps):
    found = []
    current = start
    for _ in range(steps):
        current = jnp.where(current >= 0, parent[jnp.maximum(current, 0)], -1)
        found.append(current)
    return jnp.stack(found, axis=-1)


def local(queries, keys, values, grad_out, parent, subtree_end):
    n_ctx = lax.axis_size("ctx")
    n_head = lax.axis_size("head")
    here = lax.axis_index("ctx")
    rows = queries.shape[0]
    q_width = queries.shape[1] // n_head
    kv_width = keys.shape[1] // n_head
    spread = (
        lax.all_to_all(
            queries.reshape(rows, n_head, q_width), "head", split_axis=1, concat_axis=0, tiled=True
        ),
        lax.all_to_all(
            keys.reshape(rows, n_head, kv_width), "head", split_axis=1, concat_axis=0, tiled=True
        ),
        lax.all_to_all(
            values.reshape(rows, n_head, kv_width), "head", split_axis=1, concat_axis=0, tiled=True
        ),
        lax.all_to_all(
            grad_out.reshape(rows, n_head, q_width), "head", split_axis=1, concat_axis=0, tiled=True
        ),
    )
    span = rows * n_head
    local_q = spread[0].reshape(span, q_width)
    local_k = spread[1].reshape(span, kv_width)
    local_v = spread[2].reshape(span, kv_width)
    local_g = spread[3].reshape(span, q_width)
    blocks = span // BLK
    kv_heads = kv_width // HD
    group = HQ // KVH
    scale = HD ** (-0.5)
    own_ids = here * blocks + jnp.arange(blocks, dtype=jnp.int32)
    steps = blocks - 1 + DMAX
    chains = chain_of(parent, own_ids, steps)
    remote_ids = chains[0, :DMAX]
    sources = jnp.maximum(remote_ids, 0) // blocks
    first = jnp.concatenate([local_k[:BLK], local_v[:BLK]], axis=1)[None]
    arrived = lax.all_gather(first, "ctx", axis=0, tiled=True)
    remote = jnp.take(arrived, sources, axis=0)
    all_keys = jnp.concatenate(
        [local_k, remote[:, :, :kv_width].reshape(DMAX * BLK, kv_width)], axis=0
    ).reshape(-1, kv_heads, HD)
    all_values = jnp.concatenate(
        [local_v, remote[:, :, kv_width:].reshape(DMAX * BLK, kv_width)], axis=0
    ).reshape(-1, kv_heads, HD)
    key_ids = jnp.repeat(
        jnp.concatenate([own_ids, jnp.where(remote_ids >= 0, remote_ids, -2)]), BLK
    )
    positions = jnp.arange(BLK, dtype=jnp.int32)
    key_pos = jnp.tile(positions, blocks + DMAX)
    n_keys = (blocks + DMAX) * BLK

    def attend(carry, inputs):
        key_acc, value_acc = carry
        block_id, chain, q_blk, g_blk, ends = inputs
        own = key_ids == block_id
        related = jnp.any(key_ids[:, None] == chain[None, :], axis=1)
        tree = (key_pos[None, :] <= positions[:, None]) & (
            positions[:, None] <= ends[key_pos][None, :]
        )
        allowed = jnp.where(own[None, :], tree, related[None, :])
        scores = (
            jnp.einsum("qkgd,nkd->kgqn", q_blk, all_keys, preferred_element_type=jnp.float32)
            * scale
        )
        scores = jnp.where(allowed, scores, -1e30)
        peak = jnp.max(scores, axis=-1, keepdims=True)
        weights = jnp.exp(scores - peak)
        probs = weights / jnp.sum(weights, axis=-1, keepdims=True)
        probs_b = probs.astype(jnp.bfloat16)
        attended = jnp.einsum(
            "kgqn,nkd->qkgd", probs_b, all_values, preferred_element_type=jnp.float32
        ).astype(jnp.bfloat16)
        dot_out = jnp.sum(
            g_blk.astype(jnp.float32) * attended.astype(jnp.float32), axis=-1
        ).transpose(1, 2, 0)
        grad_probs = jnp.einsum(
            "qkgd,nkd->kgqn", g_blk, all_values, preferred_element_type=jnp.float32
        )
        grad_scores = (probs * (grad_probs - dot_out[..., None])).astype(jnp.bfloat16)
        q_grad = (
            jnp.einsum("kgqn,nkd->qkgd", grad_scores, all_keys, preferred_element_type=jnp.float32)
            * scale
        ).astype(jnp.bfloat16)
        key_acc = (
            key_acc
            + jnp.einsum("kgqn,qkgd->nkd", grad_scores, q_blk, preferred_element_type=jnp.float32)
            * scale
        )
        value_acc = value_acc + jnp.einsum(
            "kgqn,qkgd->nkd", probs_b, g_blk, preferred_element_type=jnp.float32
        )
        return ((key_acc, value_acc), (attended, q_grad))

    start = (
        jnp.zeros((n_keys, kv_heads, HD), jnp.float32),
        jnp.zeros((n_keys, kv_heads, HD), jnp.float32),
    )
    inputs = (
        own_ids,
        chains,
        local_q.reshape(blocks, BLK, kv_heads, group, HD),
        local_g.reshape(blocks, BLK, kv_heads, group, HD),
        subtree_end.reshape(blocks, BLK),
    )
    (key_grads, value_grads), (outputs, query_grads) = lax.scan(attend, start, inputs)
    n_local = blocks * BLK
    sent = jnp.concatenate(
        [
            key_grads[n_local:].reshape(DMAX, BLK, kv_width),
            value_grads[n_local:].reshape(DMAX, BLK, kv_width),
        ],
        axis=2,
    )
    routing = (
        (sources[:, None] == jnp.arange(n_ctx, dtype=jnp.int32)[None, :])
        & (remote_ids >= 0)[:, None]
    ).astype(jnp.float32)
    terms = jnp.einsum("rc,rbw->cbw", routing, sent, precision=lax.Precision.HIGHEST)
    summed = lax.psum_scatter(terms, "ctx", scatter_dimension=0, tiled=True)[0]
    local_kg = key_grads[:n_local].reshape(n_local, kv_width).at[:BLK].add(summed[:, :kv_width])
    local_vg = value_grads[:n_local].reshape(n_local, kv_width).at[:BLK].add(summed[:, kv_width:])
    back = (
        lax.all_to_all(
            outputs.reshape(span, 1, q_width), "head", split_axis=0, concat_axis=1, tiled=True
        ),
        lax.all_to_all(
            query_grads.reshape(span, 1, q_width), "head", split_axis=0, concat_axis=1, tiled=True
        ),
        lax.all_to_all(
            local_kg.astype(jnp.bfloat16).reshape(span, 1, kv_width),
            "head",
            split_axis=0,
            concat_axis=1,
            tiled=True,
        ),
        lax.all_to_all(
            local_vg.astype(jnp.bfloat16).reshape(span, 1, kv_width),
            "head",
            split_axis=0,
            concat_axis=1,
            tiled=True,
        ),
    )
    attn_out = back[0].reshape(rows, n_head * q_width)
    grad_q = back[1].reshape(rows, n_head * q_width)
    grad_k = back[2].reshape(rows, n_head * kv_width)
    grad_v = back[3].reshape(rows, n_head * kv_width)
    return (attn_out, grad_q, grad_k, grad_v)


def solution(mesh):
    placed = (
        P(("ctx", "head"), None),
        P(("ctx", "head"), None),
        P(("ctx", "head"), None),
        P(("ctx", "head"), None),
        P(),
        P("ctx"),
    )
    return jax.shard_map(
        local,
        mesh=mesh,
        in_specs=placed,
        out_specs=(
            P(("ctx", "head"), None),
            P(("ctx", "head"), None),
            P(("ctx", "head"), None),
            P(("ctx", "head"), None),
        ),
        check_vma=False,
    )
```

profile of v0, /device:TPU:1, one launch (start us, length us, event | category | flops | bytes accessed | tf_op | source)
XLA Modules:
  0.0 323.9 jit_solution(10940964806669678486)
XLA Ops:
  8.8 5.8 %all-to-all-start.1 = ((bf16[96,8,128]{2,0,1:T(8,128)(2,1)}), bf16[96,8,128]{2,0,1:T(8,128)(2,1)S(1)}, u32[]{:S(2)}, u32[]{:S(2)}) async-start(bf16[96,8,128]{2,0,1:T(8,128)(2,1)} %copy_bitcast_fusion.10), calls=%async_computation.1 | async-start | bytes 393216 | tf_op jit(solution)/shard_map/all_to_all | solution.py:33
  14.6 1.6 copy_bitcast_fusion.9
  16.2 4.3 %all-to-all-done.1 = bf16[96,8,128]{2,0,1:T(8,128)(2,1)S(1)} async-done(((bf16[96,8,128]{2,0,1:T(8,128)(2,1)}), bf16[96,8,128]{2,0,1:T(8,128)(2,1)S(1)}, u32[]{:S(2)}, u32[]{:S(2)}) %all-to-all-start.1) | async-done | bytes 196640 | tf_op jit(solution)/shard_map/all_to_all | solution.py:33
  20.5 4.2 %all-to-all-start.2 = ((bf16[96,8,128]{2,0,1:T(8,128)(2,1)}), bf16[96,8,128]{2,0,1:T(8,128)(2,1)S(1)}, u32[]{:S(2)}, u32[]{:S(2)}) async-start(bf16[96,8,128]{2,0,1:T(8,128)(2,1)} %copy_bitcast_fusion.9), calls=%async_computation.2 | async-start | bytes 393216 | tf_op jit(solution)/shard_map/all_to_all | solution.py:36
  24.8 5.9 %all-to-all-done.2 = bf16[96,8,128]{2,0,1:T(8,128)(2,1)S(1)} async-done(((bf16[96,8,128]{2,0,1:T(8,128)(2,1)}), bf16[96,8,128]{2,0,1:T(8,128)(2,1)S(1)}, u32[]{:S(2)}, u32[]{:S(2)}) %all-to-all-start.2) | async-done | bytes 196640 | tf_op jit(solution)/shard_map/all_to_all | solution.py:36
  31.4 2.1 copy.221
  33.5 4.4 %all-to-all-start = ((bf16[96,8,512]{2,0,1:T(8,128)(2,1)}), bf16[96,8,512]{2,0,1:T(8,128)(2,1)S(1)}, u32[]{:S(2)}, u32[]{:S(2)}) async-start(bf16[96,8,512]{2,0,1:T(8,128)(2,1)} %bitcast.303), calls=%async_computation | async-start | bytes 1572864 | tf_op jit(solution)/shard_map/all_to_all | solution.py:30
  37.9 1.3 gather_fusion.1
  39.2 1.3 gather_fusion.2
  40.5 1.3 gather_fusion.3
  44.9 5.2 %all-to-all-done = bf16[96,8,512]{2,0,1:T(8,128)(2,1)S(1)} async-done(((bf16[96,8,512]{2,0,1:T(8,128)(2,1)}), bf16[96,8,512]{2,0,1:T(8,128)(2,1)S(1)}, u32[]{:S(2)}, u32[]{:S(2)}) %all-to-all-start) | async-done | bytes 786464 | tf_op jit(solution)/shard_map/all_to_all | solution.py:30
  50.2 4.3 %all-to-all-start.3 = ((bf16[96,8,512]{2,0,1:T(8,128)(2,1)}), bf16[96,8,512]{2,0,1:T(8,128)(2,1)S(1)}, u32[]{:S(2)}, u32[]{:S(2)}) async-start(bf16[96,8,512]{2,0,1:T(8,128)(2,1)} %bitcast.302), calls=%async_computation.3 | async-start | bytes 1572864 | tf_op jit(solution)/shard_map/all_to_all | solution.py:39
  57.0 9.8 %all-to-all-done.3 = bf16[96,8,512]{2,0,1:T(8,128)(2,1)S(1)} async-done(((bf16[96,8,512]{2,0,1:T(8,128)(2,1)}), bf16[96,8,512]{2,0,1:T(8,128)(2,1)S(1)}, u32[]{:S(2)}, u32[]{:S(2)}) %all-to-all-start.3) | async-done | bytes 786464 | tf_op jit(solution)/shard_map/all_to_all | solution.py:39
  67.0 9.6 %all-gather.3.cloned.1.call-done = bf16[4096,256]{1,0:T(8,128)(2,1)} async-done(((bf16[256,256]{1,0:T(8,128)(2,1)}), bf16[4096,256]{1,0:T(8,128)(2,1)}) %all-gather.3.cloned.1.call-update) | async-done | bytes 2097168 | tf_op jit(solution)/shard_map/all_gather | solution.py:58
  76.6 2.2 gather_fusion.7
  81.0 116.5 %while.22 = (s32[]{:T(128)}, f32[1792,1,128]{0,2,1:T(8,128)}, f32[1792,1,128]{0,2,1:T(8,128)}, bf16[3,256,1,4,128]{4,3,1,0,2:T(4,128)(2,1)}, bf16[3,256,1,4,128]...) while((s32[]{:T(128)}, f32[1792,1,128]{0,2,1:T(8,128)}, ...), condition=%wide.region_5.6_spmd.clone.clone.clone.clone, body=%wide.region_0.5_spmd.clone.clone.clone.clone.sunk | while | flops 2866537728 | bytes 148704144 | solution.py:126
  81.1 1.3 dynamic_slice.54
  83.9 10.9 %gather_fusion = s32[1792]{0:T(1024)S(1)} fusion(s32[256]{0:T(256)S(1)} %bitcast.368, s32[2048]{0:T(1024)S(1)} %pad_clamp_fusion.9), kind=kCustom, calls=%fused_computation.clone.clone.clone.clone.1 | custom fusion | bytes 21504 | tf_op jit(solution)/shard_map/while/body/eval_jaxpr/gather | solution.py:79
  95.7 1.6 fusion.111
  97.4 2.0 fusion.112
  99.4 3.1 fusion.113
  102.4 2.0 copy.241
  104.4 6.8 %fusion.116 = f32[1792,1,128]{0,2,1:T(8,128)} fusion(f32[1792,1,128]{0,2,1:T(8,128)} %get-tuple-element.525, pred[]{:T(512)S(6)} %compare.15, bf16[1,256,1,4,128]{4,3,1,0,2:T(4,128)(2,1)} %copy-done.9, f32[4,256]{1,0:T(4,128)S(1)} %fusion.112, f32[4,256]{1,0:T(4,128)S(1)} %get-tuple-element.503, f32[256,4,1792]{2,0,1:T(8,128)} %copy-done.2, ...), kind=kOutput, calls=%fused_computation.33.clone.1 | convolution fusion | flops 479395840 | bytes 9904129 | tf_op jit(solution)/shard_map/while/body/eval_jaxpr/kgqn,qkgd->nkd/dot_general | solution.py:110
  111.2 3.9 %fusion.114 = bf16[1,4,256,1792]{3,2,1,0:T(8,128)(2,1)S(1)} fusion(f32[4,256]{1,0:T(4,128)S(1)} %bitcast.399, f32[4,256]{1,0:T(4,128)S(1)} %fusion.112, f32[4,256]{1,0:T(4,128)S(1)} %get-tuple-element.503, f32[256,4,1792]{2,0,1:T(8,128)S(1)} %bitcast.370, pred[256,1792]{1,0:T(8,128)(4,1)S(1)} %copy-done.4, bf16[1792,1,128]{0,2,1:T(8,128)(2,1)} %copy-done.23, ...), kind=kOutput, calls=%fused_computation.15.clone.1 | convolution fusion | flops 482607104 | bytes 12201984 | tf_op jit(solution)/shard_map/while/body/eval_jaxpr/qkgd,nkd->kgqn/dot_general | solution.py:97
  115.2 2.3 fusion.117
  118.4 1.2 copy_dynamic-update-slice_fusion.2
  119.7 1.3 dynamic_slice.54
  122.5 10.9 %gather_fusion = s32[1792]{0:T(1024)S(1)} fusion(s32[256]{0:T(256)S(1)} %bitcast.368, s32[2048]{0:T(1024)S(1)} %pad_clamp_fusion.9), kind=kCustom, calls=%fused_computation.clone.clone.clone.clone.1 | custom fusion | bytes 21504 | tf_op jit(solution)/shard_map/while/body/eval_jaxpr/gather | solution.py:79
  134.3 1.6 fusion.111
  136.0 2.0 fusion.112
  138.0 3.1 fusion.113
  141.0 2.0 copy.241
  143.0 7.1 %fusion.116 = f32[1792,1,128]{0,2,1:T(8,128)} fusion(f32[1792,1,128]{0,2,1:T(8,128)} %get-tuple-element.525, pred[]{:T(512)S(6)} %compare.15, bf16[1,256,1,4,128]{4,3,1,0,2:T(4,128)(2,1)} %copy-done.9, f32[4,256]{1,0:T(4,128)S(1)} %fusion.112, f32[4,256]{1,0:T(4,128)S(1)} %get-tuple-element.503, f32[256,4,1792]{2,0,1:T(8,128)} %copy-done.2, ...), kind=kOutput, calls=%fused_computation.33.clone.1 | convolution fusion | flops 479395840 | bytes 9904129 | tf_op jit(solution)/shard_map/while/body/eval_jaxpr/kgqn,qkgd->nkd/dot_general | solution.py:110
  150.1 3.9 %fusion.114 = bf16[1,4,256,1792]{3,2,1,0:T(8,128)(2,1)S(1)} fusion(f32[4,256]{1,0:T(4,128)S(1)} %bitcast.399, f32[4,256]{1,0:T(4,128)S(1)} %fusion.112, f32[4,256]{1,0:T(4,128)S(1)} %get-tuple-element.503, f32[256,4,1792]{2,0,1:T(8,128)S(1)} %bitcast.370, pred[256,1792]{1,0:T(8,128)(4,1)S(1)} %copy-done.4, bf16[1792,1,128]{0,2,1:T(8,128)(2,1)} %copy-done.23, ...), kind=kOutput, calls=%fused_computation.15.clone.1 | convolution fusion | flops 482607104 | bytes 12201984 | tf_op jit(solution)/shard_map/while/body/eval_jaxpr/qkgd,nkd->kgqn/dot_general | solution.py:97
  154.1 2.3 fusion.117
  157.3 1.1 copy_dynamic-update-slice_fusion.2
  158.5 1.3 dynamic_slice.54
  161.4 10.9 %gather_fusion = s32[1792]{0:T(1024)S(1)} fusion(s32[256]{0:T(256)S(1)} %bitcast.368, s32[2048]{0:T(1024)S(1)} %pad_clamp_fusion.9), kind=kCustom, calls=%fused_computation.clone.clone.clone.clone.1 | custom fusion | bytes 21504 | tf_op jit(solution)/shard_map/while/body/eval_jaxpr/gather | solution.py:79
  173.2 1.6 fusion.111
  174.8 2.0 fusion.112
  176.8 3.1 fusion.113
  179.9 2.0 copy.241
  181.9 7.1 %fusion.116 = f32[1792,1,128]{0,2,1:T(8,128)} fusion(f32[1792,1,128]{0,2,1:T(8,128)} %get-tuple-element.525, pred[]{:T(512)S(6)} %compare.15, bf16[1,256,1,4,128]{4,3,1,0,2:T(4,128)(2,1)} %copy-done.9, f32[4,256]{1,0:T(4,128)S(1)} %fusion.112, f32[4,256]{1,0:T(4,128)S(1)} %get-tuple-element.503, f32[256,4,1792]{2,0,1:T(8,128)} %copy-done.2, ...), kind=kOutput, calls=%fused_computation.33.clone.1 | convolution fusion | flops 479395840 | bytes 9904129 | tf_op jit(solution)/shard_map/while/body/eval_jaxpr/kgqn,qkgd->nkd/dot_general | solution.py:110
  189.0 3.9 %fusion.114 = bf16[1,4,256,1792]{3,2,1,0:T(8,128)(2,1)S(1)} fusion(f32[4,256]{1,0:T(4,128)S(1)} %bitcast.399, f32[4,256]{1,0:T(4,128)S(1)} %fusion.112, f32[4,256]{1,0:T(4,128)S(1)} %get-tuple-element.503, f32[256,4,1792]{2,0,1:T(8,128)S(1)} %bitcast.370, pred[256,1792]{1,0:T(8,128)(4,1)S(1)} %copy-done.4, bf16[1792,1,128]{0,2,1:T(8,128)(2,1)} %copy-done.23, ...), kind=kOutput, calls=%fused_computation.15.clone.1 | convolution fusion | flops 482607104 | bytes 12201984 | tf_op jit(solution)/shard_map/while/body/eval_jaxpr/qkgd,nkd->kgqn/dot_general | solution.py:97
  192.9 2.3 fusion.117
  196.2 1.1 copy_dynamic-update-slice_fusion.2
  197.6 1.5 copy.160
  199.4 1.5 copy.163
  201.3 2.2 fusion.68
  203.5 4.4 %copy.166 = f32[16,256,256]{2,1,0:T(8,128)} copy(f32[16,256,256]{2,0,1:T(8,128)S(1)} %fusion.68) | data formatting | bytes 8388608 | tf_op jit(solution)/shard_map/rc,rbw->cbw/dot_general | solution.py:139
  208.8 5.4 %reduce.16 = bf16[768,512]{1,0:T(8,128)(2,1)S(1)} reduce(bf16[768,1,512]{2,1,0:T(2,128)(2,1)S(1)} %reshape.666, bf16[]{:T(256)} %broadcast.772), dimensions={1}, to_apply=%reshape.666.reduce_sub_computation | reduce | bytes 1572866 | tf_op jit(solution)/shard_map/reshape | solution.py:148
  214.3 1.5 reshape.675
  215.7 6.0 %all-to-all-start.5 = ((bf16[8,2,24576]{2,1,0:T(2,128)(2,1)}), bf16[8,2,24576]{2,1,0:T(2,128)(2,1)}, u32[]{:S(2)}, u32[]{:S(2)}) async-start(bf16[8,2,24576]{2,1,0:T(2,128)(2,1)} %reshape.675), calls=%async_computation.5 | async-start | bytes 1572864 | tf_op jit(solution)/shard_map/all_to_all | solution.py:147
  221.7 4.6 %reshape.665 = bf16[768,1,512]{2,1,0:T(2,128)(2,1)S(1)} reshape(bf16[3,256,1,4,128]{4,3,1,0,2:T(4,128)(2,1)} %get-tuple-element.121) | data formatting | bytes 1572864 | tf_op jit(solution)/shard_map/reshape | solution.py:145
  226.3 5.4 %reduce.15 = bf16[768,512]{1,0:T(8,128)(2,1)S(1)} reduce(bf16[768,1,512]{2,1,0:T(2,128)(2,1)S(1)} %reshape.665, bf16[]{:T(256)} %broadcast.772), dimensions={1}, to_apply=%reshape.665.reduce_sub_computation | reduce | bytes 1572866 | tf_op jit(solution)/shard_map/reshape | solution.py:145
  231.8 1.5 reshape.673
  234.1 4.3 %all-to-all-start.4 = ((bf16[8,2,24576]{2,1,0:T(2,128)(2,1)}), bf16[8,2,24576]{2,1,0:T(2,128)(2,1)S(1)}, u32[]{:S(2)}, u32[]{:S(2)}) async-start(bf16[8,2,24576]{2,1,0:T(2,128)(2,1)} %reshape.673), calls=%async_computation.4 | async-start | bytes 1572864 | tf_op jit(solution)/shard_map/all_to_all | solution.py:144
  239.5 45.0 %reduce-scatter.4.cloned.1.call-done = f32[1,256,256]{2,1,0:T(8,128)} async-done(((f32[16,256,256]{2,1,0:T(8,128)}), f32[1,256,256]{2,1,0:T(8,128)}) %reduce-scatter.4.cloned.1.call-update) | async-done | bytes 262160
  287.1 6.5 %all-to-all-start.7 = ((bf16[8,2,6144]{2,1,0:T(2,128)(2,1)}), bf16[8,2,6144]{2,1,0:T(2,128)(2,1)S(1)}, u32[]{:S(2)}, u32[]{:S(2)}) async-start(bf16[8,2,6144]{2,1,0:T(2,128)(2,1)} %reshape.679), calls=%async_computation.7 | async-start | bytes 393216 | tf_op jit(solution)/shard_map/all_to_all | solution.py:157
  295.1 4.4 %all-to-all-done.7 = bf16[8,2,6144]{2,1,0:T(2,128)(2,1)S(1)} async-done(((bf16[8,2,6144]{2,1,0:T(2,128)(2,1)}), bf16[8,2,6144]{2,1,0:T(2,128)(2,1)S(1)}, u32[]{:S(2)}, u32[]{:S(2)}) %all-to-all-start.7) | async-done | bytes 196640 | tf_op jit(solution)/shard_map/all_to_all | solution.py:157
  300.1 4.9 %all-to-all-start.6 = ((bf16[8,2,6144]{2,1,0:T(2,128)(2,1)}), bf16[8,2,6144]{2,1,0:T(2,128)(2,1)}, u32[]{:S(2)}, u32[]{:S(2)}) async-start(bf16[8,2,6144]{2,1,0:T(2,128)(2,1)} %reshape.677), calls=%async_computation.6 | async-start | bytes 393216 | tf_op jit(solution)/shard_map/all_to_all | solution.py:150
  305.0 4.1 %reshape.676 = bf16[768,1,512]{2,1,0:T(2,128)(2,1)S(1)} reshape(bf16[8,2,24576]{2,1,0:T(2,128)(2,1)} %all-to-all-done.5) | data formatting | bytes 1572864
  312.2 1.6 reshape.680
  314.7 1.6 reshape.678
  (271 shorter events, 33.5 us)
Async XLA Ops:
  7.2 34.6 %copy-start.1 = (s32[48]{0:T(128)S(1)}, s32[48]{0:T(128)}, u32[]{:S(2)}) copy-start(s32[48]{0:T(128)} %param.16) | copy-start | bytes 580
  7.2 36.6 %copy-start.20 = (bf16[96,4096]{1,0:T(8,128)(2,1)S(1)}, bf16[96,4096]{1,0:T(8,128)(2,1)}, u32[]{:S(2)}) copy-start(bf16[96,4096]{1,0:T(8,128)(2,1)} %param.15) | copy-start | bytes 2359300
  8.1 47.1 %copy-start.25 = (s32[768]{0:T(1024)S(1)}, s32[768]{0:T(1024)}, u32[]{:S(2)}) copy-start(s32[768]{0:T(1024)} %param.17) | copy-start | bytes 9220
  8.8 11.7 %all-to-all-start.1 = ((bf16[96,8,128]{2,0,1:T(8,128)(2,1)}), bf16[96,8,128]{2,0,1:T(8,128)(2,1)S(1)}, u32[]{:S(2)}, u32[]{:S(2)}) async-start(bf16[96,8,128]{2,0,1:T(8,128)(2,1)} %copy_bitcast_fusion.10), calls=%async_computation.1 | async-start | bytes 393216 | tf_op jit(solution)/shard_map/all_to_all | solution.py:33
  20.5 13.0 %copy-start.19 = (bf16[96,8,128]{2,0,1:T(8,128)(2,1)}, bf16[96,8,128]{2,0,1:T(8,128)(2,1)S(1)}, u32[]{:S(2)}) copy-start(bf16[96,8,128]{2,0,1:T(8,128)(2,1)S(1)} %all-to-all-done.1) | copy-start | bytes 589828
  20.5 10.2 %all-to-all-start.2 = ((bf16[96,8,128]{2,0,1:T(8,128)(2,1)}), bf16[96,8,128]{2,0,1:T(8,128)(2,1)S(1)}, u32[]{:S(2)}, u32[]{:S(2)}) async-start(bf16[96,8,128]{2,0,1:T(8,128)(2,1)} %copy_bitcast_fusion.9), calls=%async_computation.2 | async-start | bytes 393216 | tf_op jit(solution)/shard_map/all_to_all | solution.py:36
  24.8 51.8 %all-gather.3.cloned.1.call-start = ((), (), s32[]{:S(2)}) async-start(), calls=%async_computation.9 | async-start | bytes 2228224 | tf_op jit(solution)/shard_map/all_gather | solution.py:58
  33.5 16.7 %all-to-all-start = ((bf16[96,8,512]{2,0,1:T(8,128)(2,1)}), bf16[96,8,512]{2,0,1:T(8,128)(2,1)S(1)}, u32[]{:S(2)}, u32[]{:S(2)}) async-start(bf16[96,8,512]{2,0,1:T(8,128)(2,1)} %bitcast.303), calls=%async_computation | async-start | bytes 1572864 | tf_op jit(solution)/shard_map/all_to_all | solution.py:30
  43.1 23.7 %copy-start.28 = (s32[3]{0:T(128)}, s32[3]{0:T(128)S(1)}, u32[]{:S(2)}) copy-start(s32[3]{0:T(128)S(1)} %iota_add_fusion.1) | copy-start | bytes 40
  50.2 16.6 %all-to-all-start.3 = ((bf16[96,8,512]{2,0,1:T(8,128)(2,1)}), bf16[96,8,512]{2,0,1:T(8,128)(2,1)S(1)}, u32[]{:S(2)}, u32[]{:S(2)}) async-start(bf16[96,8,512]{2,0,1:T(8,128)(2,1)} %bitcast.302), calls=%async_computation.3 | async-start | bytes 1572864 | tf_op jit(solution)/shard_map/all_to_all | solution.py:39
  54.5 230.0 %reduce-scatter.4.cloned.1.call-start = ((), (), s32[]{:S(2)}) async-start(), calls=%async_computation.10 | async-start | bytes 4456448
  81.0 13.9 %copy-start.14 = (bf16[3,256,1,4,128]{4,3,1,0,2:T(4,128)(2,1)}, bf16[3,256,1,4,128]{4,3,1,0,2:T(4,128)(2,1)S(1)}, u32[]{:S(2)}) copy-start(bf16[3,256,1,4,128]{4,3,1,0,2:T(4,128)(2,1)S(1)} %get-tuple-element.543) | copy-start | bytes 2359300 | tf_op jit(solution)/shard_map/while
  81.1 16.3 %copy-start.12 = (bf16[1792,1,128]{2,0,1:T(8,128)(2,1)}, bf16[1792,1,128]{2,0,1:T(8,128)(2,1)S(1)}, u32[]{:S(2)}) copy-start(bf16[1792,1,128]{2,0,1:T(8,128)(2,1)S(1)} %get-tuple-element.547) | copy-start | bytes 1376260 | tf_op jit(solution)/shard_map/while
  81.1 16.3 %copy-start.16 = (bf16[3,256,1,4,128]{4,3,1,0,2:T(4,128)(2,1)}, bf16[3,256,1,4,128]{4,3,1,0,2:T(4,128)(2,1)S(1)}, u32[]{:S(2)}) copy-start(bf16[3,256,1,4,128]{4,3,1,0,2:T(4,128)(2,1)S(1)} %get-tuple-element.548) | copy-start | bytes 2359300 | tf_op jit(solution)/shard_map/while
  81.1 18.3 %copy-start.23 = (bf16[1792,1,128]{0,2,1:T(8,128)(2,1)}, bf16[1792,1,128]{0,2,1:T(8,128)(2,1)S(1)}, u32[]{:S(2)}) copy-start(bf16[1792,1,128]{0,2,1:T(8,128)(2,1)S(1)} %get-tuple-element.549) | copy-start | bytes 1376260 | tf_op jit(solution)/shard_map/while
  95.0 4.4 %copy-start.9 = (bf16[1,256,1,4,128]{4,3,1,0,2:T(4,128)(2,1)}, bf16[1,256,1,4,128]{4,3,1,0,2:T(4,128)(2,1)S(1)}, u32[]{:S(2)}) copy-start(bf16[1,256,1,4,128]{4,3,1,0,2:T(4,128)(2,1)S(1)} %constant_dynamic-slice_fusion.7) | copy-start | bytes 786436 | tf_op jit(solution)/shard_map/while
  97.4 5.1 %copy-start.2 = (f32[256,4,1792]{2,0,1:T(8,128)}, f32[256,4,1792]{2,0,1:T(8,128)S(1)}, u32[]{:S(2)}) copy-start(f32[256,4,1792]{2,0,1:T(8,128)S(1)} %get-tuple-element.502) | copy-start | bytes 22020100 | tf_op jit(solution)/shard_map/while
  102.4 8.8 %slice-start = ((s8[7340032]{0:T(1024)(128)(4,1)}), s8[3145728]{0:T(1024)(128)(4,1)S(1)}, s32[]{:S(2)}) async-start(s8[7340032]{0:T(1024)(128)(4,1)} %bitcast.369), calls=%async_computation.11 | async-start | bytes 6291456 | tf_op jit(solution)/shard_map/while
  104.4 6.8 %slice-start.1 = ((s8[7340032]{0:T(1024)(128)(4,1)}), s8[4194304]{0:T(1024)(128)(4,1)S(1)}, s32[]{:S(2)}) async-start(s8[7340032]{0:T(1024)(128)(4,1)} %bitcast.369), calls=%async_computation.12 | async-start | bytes 8388608 | tf_op jit(solution)/shard_map/while
  104.4 6.8 %copy-start.4 = (pred[256,1792]{1,0:T(8,128)(4,1)S(1)}, pred[256,1792]{1,0:T(8,128)(4,1)}, u32[]{:S(2)}) copy-start(pred[256,1792]{1,0:T(8,128)(4,1)} %copy-done.3) | copy-start | bytes 1376260 | tf_op jit(solution)/shard_map/while
  104.4 6.8 %copy-start.10 = (bf16[1,256,1,4,128]{4,3,1,0,2:T(4,128)(2,1)S(1)}, bf16[1,256,1,4,128]{4,3,1,0,2:T(4,128)(2,1)}, u32[]{:S(2)}) copy-start(bf16[1,256,1,4,128]{4,3,1,0,2:T(4,128)(2,1)} %copy-done.9) | copy-start | bytes 786436 | tf_op jit(solution)/shard_map/while
  111.2 6.2 %copy-start.6 = (bf16[1,256,1,4,128]{4,3,1,0,2:T(4,128)(2,1)S(1)}, bf16[1,256,1,4,128]{4,3,1,0,2:T(4,128)(2,1)}, u32[]{:S(2)}) copy-start(bf16[1,256,1,4,128]{4,3,1,0,2:T(4,128)(2,1)} %copy-done.5) | copy-start | bytes 786436 | tf_op jit(solution)/shard_map/while
  115.1 4.5 %copy-start.13 = (bf16[1792,1,128]{2,0,1:T(8,128)(2,1)S(1)}, bf16[1792,1,128]{2,0,1:T(8,128)(2,1)}, u32[]{:S(2)}) copy-start(bf16[1792,1,128]{2,0,1:T(8,128)(2,1)} %copy-done.12) | copy-start | bytes 1376260 | tf_op jit(solution)/shard_map/while
  115.2 4.5 %copy-start.15 = (bf16[3,256,1,4,128]{4,3,1,0,2:T(4,128)(2,1)S(1)}, bf16[3,256,1,4,128]{4,3,1,0,2:T(4,128)(2,1)}, u32[]{:S(2)}) copy-start(bf16[3,256,1,4,128]{4,3,1,0,2:T(4,128)(2,1)} %copy-done.14) | copy-start | bytes 2359300 | tf_op jit(solution)/shard_map/while
  115.2 4.4 %copy-start.17 = (bf16[3,256,1,4,128]{4,3,1,0,2:T(4,128)(2,1)S(1)}, bf16[3,256,1,4,128]{4,3,1,0,2:T(4,128)(2,1)}, u32[]{:S(2)}) copy-start(bf16[3,256,1,4,128]{4,3,1,0,2:T(4,128)(2,1)} %copy-done.16) | copy-start | bytes 2359300 | tf_op jit(solution)/shard_map/while
  115.2 4.4 %copy-start.24 = (bf16[1792,1,128]{0,2,1:T(8,128)(2,1)S(1)}, bf16[1792,1,128]{0,2,1:T(8,128)(2,1)}, u32[]{:S(2)}) copy-start(bf16[1792,1,128]{0,2,1:T(8,128)(2,1)} %copy-done.23) | copy-start | bytes 1376260 | tf_op jit(solution)/shard_map/while
  119.6 13.9 %copy-start.14 = (bf16[3,256,1,4,128]{4,3,1,0,2:T(4,128)(2,1)}, bf16[3,256,1,4,128]{4,3,1,0,2:T(4,128)(2,1)S(1)}, u32[]{:S(2)}) copy-start(bf16[3,256,1,4,128]{4,3,1,0,2:T(4,128)(2,1)S(1)} %get-tuple-element.543) | copy-start | bytes 2359300 | tf_op jit(solution)/shard_map/while
  119.7 16.3 %copy-start.12 = (bf16[1792,1,128]{2,0,1:T(8,128)(2,1)}, bf16[1792,1,128]{2,0,1:T(8,128)(2,1)S(1)}, u32[]{:S(2)}) copy-start(bf16[1792,1,128]{2,0,1:T(8,128)(2,1)S(1)} %get-tuple-element.547) | copy-start | bytes 1376260 | tf_op jit(solution)/shard_map/while
  119.7 16.3 %copy-start.16 = (bf16[3,256,1,4,128]{4,3,1,0,2:T(4,128)(2,1)}, bf16[3,256,1,4,128]{4,3,1,0,2:T(4,128)(2,1)S(1)}, u32[]{:S(2)}) copy-start(bf16[3,256,1,4,128]{4,3,1,0,2:T(4,128)(2,1)S(1)} %get-tuple-element.548) | copy-start | bytes 2359300 | tf_op jit(solution)/shard_map/while
  119.7 18.3 %copy-start.23 = (bf16[1792,1,128]{0,2,1:T(8,128)(2,1)}, bf16[1792,1,128]{0,2,1:T(8,128)(2,1)S(1)}, u32[]{:S(2)}) copy-start(bf16[1792,1,128]{0,2,1:T(8,128)(2,1)S(1)} %get-tuple-element.549) | copy-start | bytes 1376260 | tf_op jit(solution)/shard_map/while
  133.6 4.4 %copy-start.9 = (bf16[1,256,1,4,128]{4,3,1,0,2:T(4,128)(2,1)}, bf16[1,256,1,4,128]{4,3,1,0,2:T(4,128)(2,1)S(1)}, u32[]{:S(2)}) copy-start(bf16[1,256,1,4,128]{4,3,1,0,2:T(4,128)(2,1)S(1)} %constant_dynamic-slice_fusion.7) | copy-start | bytes 786436 | tf_op jit(solution)/shard_map/while
  133.7 4.3 %copy-start.5 = (bf16[1,256,1,4,128]{4,3,1,0,2:T(4,128)(2,1)}, bf16[1,256,1,4,128]{4,3,1,0,2:T(4,128)(2,1)S(1)}, u32[]{:S(2)}) copy-start(bf16[1,256,1,4,128]{4,3,1,0,2:T(4,128)(2,1)S(1)} %constant_dynamic-slice_fusion.9) | copy-start | bytes 786436 | tf_op jit(solution)/shard_map/while
  136.0 5.1 %copy-start.2 = (f32[256,4,1792]{2,0,1:T(8,128)}, f32[256,4,1792]{2,0,1:T(8,128)S(1)}, u32[]{:S(2)}) copy-start(f32[256,4,1792]{2,0,1:T(8,128)S(1)} %get-tuple-element.502) | copy-start | bytes 22020100 | tf_op jit(solution)/shard_map/while
  141.0 9.1 %slice-start = ((s8[7340032]{0:T(1024)(128)(4,1)}), s8[3145728]{0:T(1024)(128)(4,1)S(1)}, s32[]{:S(2)}) async-start(s8[7340032]{0:T(1024)(128)(4,1)} %bitcast.369), calls=%async_computation.11 | async-start | bytes 6291456 | tf_op jit(solution)/shard_map/while
  143.0 7.1 %slice-start.1 = ((s8[7340032]{0:T(1024)(128)(4,1)}), s8[4194304]{0:T(1024)(128)(4,1)S(1)}, s32[]{:S(2)}) async-start(s8[7340032]{0:T(1024)(128)(4,1)} %bitcast.369), calls=%async_computation.12 | async-start | bytes 8388608 | tf_op jit(solution)/shard_map/while
  143.0 7.1 %copy-start.4 = (pred[256,1792]{1,0:T(8,128)(4,1)S(1)}, pred[256,1792]{1,0:T(8,128)(4,1)}, u32[]{:S(2)}) copy-start(pred[256,1792]{1,0:T(8,128)(4,1)} %copy-done.3) | copy-start | bytes 1376260 | tf_op jit(solution)/shard_map/while
  143.0 7.1 %copy-start.10 = (bf16[1,256,1,4,128]{4,3,1,0,2:T(4,128)(2,1)S(1)}, bf16[1,256,1,4,128]{4,3,1,0,2:T(4,128)(2,1)}, u32[]{:S(2)}) copy-start(bf16[1,256,1,4,128]{4,3,1,0,2:T(4,128)(2,1)} %copy-done.9) | copy-start | bytes 786436 | tf_op jit(solution)/shard_map/while
  150.1 6.2 %copy-start.6 = (bf16[1,256,1,4,128]{4,3,1,0,2:T(4,128)(2,1)S(1)}, bf16[1,256,1,4,128]{4,3,1,0,2:T(4,128)(2,1)}, u32[]{:S(2)}) copy-start(bf16[1,256,1,4,128]{4,3,1,0,2:T(4,128)(2,1)} %copy-done.5) | copy-start | bytes 786436 | tf_op jit(solution)/shard_map/while
  154.0 4.4 %copy-start.13 = (bf16[1792,1,128]{2,0,1:T(8,128)(2,1)S(1)}, bf16[1792,1,128]{2,0,1:T(8,128)(2,1)}, u32[]{:S(2)}) copy-start(bf16[1792,1,128]{2,0,1:T(8,128)(2,1)} %copy-done.12) | copy-start | bytes 1376260 | tf_op jit(solution)/shard_map/while
  154.0 4.4 %copy-start.15 = (bf16[3,256,1,4,128]{4,3,1,0,2:T(4,128)(2,1)S(1)}, bf16[3,256,1,4,128]{4,3,1,0,2:T(4,128)(2,1)}, u32[]{:S(2)}) copy-start(bf16[3,256,1,4,128]{4,3,1,0,2:T(4,128)(2,1)} %copy-done.14) | copy-start | bytes 2359300 | tf_op jit(solution)/shard_map/while
  154.1 4.4 %copy-start.17 = (bf16[3,256,1,4,128]{4,3,1,0,2:T(4,128)(2,1)S(1)}, bf16[3,256,1,4,128]{4,3,1,0,2:T(4,128)(2,1)}, u32[]{:S(2)}) copy-start(bf16[3,256,1,4,128]{4,3,1,0,2:T(4,128)(2,1)} %copy-done.16) | copy-start | bytes 2359300 | tf_op jit(solution)/shard_map/while
  154.1 4.4 %copy-start.24 = (bf16[1792,1,128]{0,2,1:T(8,128)(2,1)S(1)}, bf16[1792,1,128]{0,2,1:T(8,128)(2,1)}, u32[]{:S(2)}) copy-start(bf16[1792,1,128]{0,2,1:T(8,128)(2,1)} %copy-done.23) | copy-start | bytes 1376260 | tf_op jit(solution)/shard_map/while
  158.5 13.9 %copy-start.14 = (bf16[3,256,1,4,128]{4,3,1,0,2:T(4,128)(2,1)}, bf16[3,256,1,4,128]{4,3,1,0,2:T(4,128)(2,1)S(1)}, u32[]{:S(2)}) copy-start(bf16[3,256,1,4,128]{4,3,1,0,2:T(4,128)(2,1)S(1)} %get-tuple-element.543) | copy-start | bytes 2359300 | tf_op jit(solution)/shard_map/while
  158.5 16.3 %copy-start.12 = (bf16[1792,1,128]{2,0,1:T(8,128)(2,1)}, bf16[1792,1,128]{2,0,1:T(8,128)(2,1)S(1)}, u32[]{:S(2)}) copy-start(bf16[1792,1,128]{2,0,1:T(8,128)(2,1)S(1)} %get-tuple-element.547) | copy-start | bytes 1376260 | tf_op jit(solution)/shard_map/while
  158.5 16.3 %copy-start.16 = (bf16[3,256,1,4,128]{4,3,1,0,2:T(4,128)(2,1)}, bf16[3,256,1,4,128]{4,3,1,0,2:T(4,128)(2,1)S(1)}, u32[]{:S(2)}) copy-start(bf16[3,256,1,4,128]{4,3,1,0,2:T(4,128)(2,1)S(1)} %get-tuple-element.548) | copy-start | bytes 2359300 | tf_op jit(solution)/shard_map/while
  158.5 18.3 %copy-start.23 = (bf16[1792,1,128]{0,2,1:T(8,128)(2,1)}, bf16[1792,1,128]{0,2,1:T(8,128)(2,1)S(1)}, u32[]{:S(2)}) copy-start(bf16[1792,1,128]{0,2,1:T(8,128)(2,1)S(1)} %get-tuple-element.549) | copy-start | bytes 1376260 | tf_op jit(solution)/shard_map/while
  172.4 4.4 %copy-start.9 = (bf16[1,256,1,4,128]{4,3,1,0,2:T(4,128)(2,1)}, bf16[1,256,1,4,128]{4,3,1,0,2:T(4,128)(2,1)S(1)}, u32[]{:S(2)}) copy-start(bf16[1,256,1,4,128]{4,3,1,0,2:T(4,128)(2,1)S(1)} %constant_dynamic-slice_fusion.7) | copy-start | bytes 786436 | tf_op jit(solution)/shard_map/while
  172.6 4.3 %copy-start.5 = (bf16[1,256,1,4,128]{4,3,1,0,2:T(4,128)(2,1)}, bf16[1,256,1,4,128]{4,3,1,0,2:T(4,128)(2,1)S(1)}, u32[]{:S(2)}) copy-start(bf16[1,256,1,4,128]{4,3,1,0,2:T(4,128)(2,1)S(1)} %constant_dynamic-slice_fusion.9) | copy-start | bytes 786436 | tf_op jit(solution)/shard_map/while
  174.8 5.1 %copy-start.2 = (f32[256,4,1792]{2,0,1:T(8,128)}, f32[256,4,1792]{2,0,1:T(8,128)S(1)}, u32[]{:S(2)}) copy-start(f32[256,4,1792]{2,0,1:T(8,128)S(1)} %get-tuple-element.502) | copy-start | bytes 22020100 | tf_op jit(solution)/shard_map/while
  179.9 9.1 %slice-start = ((s8[7340032]{0:T(1024)(128)(4,1)}), s8[3145728]{0:T(1024)(128)(4,1)S(1)}, s32[]{:S(2)}) async-start(s8[7340032]{0:T(1024)(128)(4,1)} %bitcast.369), calls=%async_computation.11 | async-start | bytes 6291456 | tf_op jit(solution)/shard_map/while
  181.9 7.1 %slice-start.1 = ((s8[7340032]{0:T(1024)(128)(4,1)}), s8[4194304]{0:T(1024)(128)(4,1)S(1)}, s32[]{:S(2)}) async-start(s8[7340032]{0:T(1024)(128)(4,1)} %bitcast.369), calls=%async_computation.12 | async-start | bytes 8388608 | tf_op jit(solution)/shard_map/while
  181.9 7.1 %copy-start.4 = (pred[256,1792]{1,0:T(8,128)(4,1)S(1)}, pred[256,1792]{1,0:T(8,128)(4,1)}, u32[]{:S(2)}) copy-start(pred[256,1792]{1,0:T(8,128)(4,1)} %copy-done.3) | copy-start | bytes 1376260 | tf_op jit(solution)/shard_map/while
  181.9 7.1 %copy-start.10 = (bf16[1,256,1,4,128]{4,3,1,0,2:T(4,128)(2,1)S(1)}, bf16[1,256,1,4,128]{4,3,1,0,2:T(4,128)(2,1)}, u32[]{:S(2)}) copy-start(bf16[1,256,1,4,128]{4,3,1,0,2:T(4,128)(2,1)} %copy-done.9) | copy-start | bytes 786436 | tf_op jit(solution)/shard_map/while
  189.0 6.2 %copy-start.6 = (bf16[1,256,1,4,128]{4,3,1,0,2:T(4,128)(2,1)S(1)}, bf16[1,256,1,4,128]{4,3,1,0,2:T(4,128)(2,1)}, u32[]{:S(2)}) copy-start(bf16[1,256,1,4,128]{4,3,1,0,2:T(4,128)(2,1)} %copy-done.5) | copy-start | bytes 786436 | tf_op jit(solution)/shard_map/while
  192.9 4.4 %copy-start.13 = (bf16[1792,1,128]{2,0,1:T(8,128)(2,1)S(1)}, bf16[1792,1,128]{2,0,1:T(8,128)(2,1)}, u32[]{:S(2)}) copy-start(bf16[1792,1,128]{2,0,1:T(8,128)(2,1)} %copy-done.12) | copy-start | bytes 1376260 | tf_op jit(solution)/shard_map/while
  192.9 4.4 %copy-start.15 = (bf16[3,256,1,4,128]{4,3,1,0,2:T(4,128)(2,1)S(1)}, bf16[3,256,1,4,128]{4,3,1,0,2:T(4,128)(2,1)}, u32[]{:S(2)}) copy-start(bf16[3,256,1,4,128]{4,3,1,0,2:T(4,128)(2,1)} %copy-done.14) | copy-start | bytes 2359300 | tf_op jit(solution)/shard_map/while
  192.9 4.4 %copy-start.17 = (bf16[3,256,1,4,128]{4,3,1,0,2:T(4,128)(2,1)S(1)}, bf16[3,256,1,4,128]{4,3,1,0,2:T(4,128)(2,1)}, u32[]{:S(2)}) copy-start(bf16[3,256,1,4,128]{4,3,1,0,2:T(4,128)(2,1)} %copy-done.16) | copy-start | bytes 2359300 | tf_op jit(solution)/shard_map/while
  192.9 4.4 %copy-start.24 = (bf16[1792,1,128]{0,2,1:T(8,128)(2,1)S(1)}, bf16[1792,1,128]{0,2,1:T(8,128)(2,1)}, u32[]{:S(2)}) copy-start(bf16[1792,1,128]{0,2,1:T(8,128)(2,1)} %copy-done.23) | copy-start | bytes 1376260 | tf_op jit(solution)/shard_map/while
  199.0 8.9 %copy-start.18 = (f32[1792,1,128]{2,0,1:T(8,128)}, f32[1792,1,128]{2,0,1:T(8,128)S(1)}, u32[]{:S(2)}) copy-start(f32[1792,1,128]{2,0,1:T(8,128)S(1)} %copy.160) | copy-start | bytes 2752516
  203.5 4.4 %copy-start.22 = (bf16[3,256,1,4,128]{4,3,1,0,2:T(4,128)(2,1)S(1)}, bf16[3,256,1,4,128]{4,3,1,0,2:T(4,128)(2,1)}, u32[]{:S(2)}) copy-start(bf16[3,256,1,4,128]{4,3,1,0,2:T(4,128)(2,1)} %get-tuple-element.122) | copy-start | bytes 2359300
  215.7 18.4 %all-to-all-start.5 = ((bf16[8,2,24576]{2,1,0:T(2,128)(2,1)}), bf16[8,2,24576]{2,1,0:T(2,128)(2,1)}, u32[]{:S(2)}, u32[]{:S(2)}) async-start(bf16[8,2,24576]{2,1,0:T(2,128)(2,1)} %reshape.675), calls=%async_computation.5 | async-start | bytes 1572864 | tf_op jit(solution)/shard_map/all_to_all | solution.py:147
  234.1 53.0 %all-to-all-start.4 = ((bf16[8,2,24576]{2,1,0:T(2,128)(2,1)}), bf16[8,2,24576]{2,1,0:T(2,128)(2,1)S(1)}, u32[]{:S(2)}, u32[]{:S(2)}) async-start(bf16[8,2,24576]{2,1,0:T(2,128)(2,1)} %reshape.673), calls=%async_computation.4 | async-start | bytes 1572864 | tf_op jit(solution)/shard_map/all_to_all | solution.py:144
  287.1 12.4 %all-to-all-start.7 = ((bf16[8,2,6144]{2,1,0:T(2,128)(2,1)}), bf16[8,2,6144]{2,1,0:T(2,128)(2,1)S(1)}, u32[]{:S(2)}, u32[]{:S(2)}) async-start(bf16[8,2,6144]{2,1,0:T(2,128)(2,1)} %reshape.679), calls=%async_computation.7 | async-start | bytes 393216 | tf_op jit(solution)/shard_map/all_to_all | solution.py:157
  300.1 14.5 %all-to-all-start.6 = ((bf16[8,2,6144]{2,1,0:T(2,128)(2,1)}), bf16[8,2,6144]{2,1,0:T(2,128)(2,1)}, u32[]{:S(2)}, u32[]{:S(2)}) async-start(bf16[8,2,6144]{2,1,0:T(2,128)(2,1)} %reshape.677), calls=%async_computation.6 | async-start | bytes 393216 | tf_op jit(solution)/shard_map/all_to_all | solution.py:150
  (17 other events, 44.7 us)
Sparse Core Ops, SparseCore 0:
  31.5 45.0 all-gather.2
  208.0 76.4 reduce-scatter.3
where the time goes:
time: 326 us; the launch traced here: 324 us
  local copies, waits for them, and re-layouts  97.6 us (30%)
  waiting for transfers between devices  85.1 us (26%)
  matrix products  58.3 us (18%)
  starting transfers between devices  40.5 us (12%)
  other arithmetic  26.7 us (8%)
  between operations  14.4 us (4%)
    unnamed x3, waiting for transfers between devices  45 us
    gather x3, local copies, waits for them, and re-layouts, attend(): ends[key_pos][None, :]  32.7 us
    dot_general x3, matrix products, attend(): jnp.einsum('kgqn,qkgd->nkd', probs_b, g_blk, preferred_element_type=jnp.f...  20.9 us
    unnamed x39, local copies, waits for them, and re-layouts  18.5 us
    dot_general x3, matrix products, attend(): jnp.einsum('qkgd,nkd->kgqn', g_blk, all_values, preferred_element_type=jn...  11.6 us
    all_to_all x1, waiting for transfers between devices, local(): lax.all_to_all(grad_out.reshape(rows, n_head, q_width), 'head', split_axi...  9.83 us
    all_gather x1, waiting for transfers between devices, local(): arrived = lax.all_gather(first, 'ctx', axis=0, tiled=True)  9.56 us
    dynamic_update_slice x6, local copies, waits for them, and re-layouts, local(): lax.scan(attend, start, inputs)  9.37 us
  transfers between devices with their start and end apart: 10, of which 8 were waited for; matrix products, arithmetic and copies ran while one was open for 15% of the time, Pallas kernels for 0%

commit v1 on v0

v1 whole, which is shorter than its diff:
```python
import functools

import jax
import jax.numpy as jnp
from jax import lax
from jax.experimental import pallas as pl
from jax.experimental.pallas import tpu as pltpu
from jax.sharding import PartitionSpec as P

HQ = 32
KVH = 8
HD = 128
BLK = 256
DMAX = 4
GROUP = HQ // KVH
SCALE = HD**-0.5
SCALE2 = SCALE * 1.4426950408889634
F32 = jnp.float32
BF16 = jnp.bfloat16


def dot(a, b, ca, cb):
    return lax.dot_general(a, b, (((ca,), (cb,)), ((), ())), preferred_element_type=F32)


def ancestor(here, blocks, parent, steps):
    current = here[0] * blocks
    for _ in range(steps):
        current = jnp.where(current >= 0, parent[jnp.maximum(current, 0)], -1)
    return current


def source(here, blocks, parent, steps):
    return jnp.maximum(ancestor(here, blocks, parent, steps), 0) // blocks


def attention_kernel(
    nb, here, parent, q_ref, g_ref, kv_ref, r0, r1, r2, r3, end_ref,
    o_ref, dq_ref, dkv_ref, terms_ref, ks, vs, dks, dvs, bias,
):
    h = pl.program_id(0)
    nr = DMAX * BLK
    found = [ancestor(here, nb, parent, j + 1) for j in range(DMAX)]

    @pl.when(h == 0)
    def _():
        for j, r in enumerate((r0, r1, r2, r3)):
            ks[j * BLK : (j + 1) * BLK] = r[0, :, :HD]
            vs[j * BLK : (j + 1) * BLK] = r[0, :, HD:]
        ks[nr:] = kv_ref[:, :HD]
        vs[nr:] = kv_ref[:, HD:]
        dks[...] = jnp.zeros_like(dks)
        dvs[...] = jnp.zeros_like(dvs)
        i = lax.broadcasted_iota(jnp.int32, (BLK, BLK), 0)
        p = lax.broadcasted_iota(jnp.int32, (BLK, BLK), 1)
        for b in range(nb):
            ok = (p <= i) & (i <= end_ref[b : b + 1, :])
            bias[b] = jnp.where(ok, 0.0, -1e30)

    for b in range(nb):
        rows = pl.ds(b * BLK, BLK)
        q = q_ref[rows, :]
        g = g_ref[rows, :]
        nk = nr + (b + 1) * BLK
        scores = dot(q, ks[:nk, :], 1, 1)
        parts = [scores[:, j * BLK : (j + 1) * BLK] for j in range(DMAX + b + 1)]
        parts[-1] = parts[-1] + bias[b]
        peak = None
        for j, x in enumerate(parts):
            t = jnp.maximum(x[:, :HD], x[:, HD:])
            if j < DMAX:
                t = jnp.where(found[j] >= 0, t, -3e38)
            peak = t if peak is None else jnp.maximum(peak, t)
        peak = jnp.max(peak, axis=1, keepdims=True)
        weights = []
        total = None
        for j, x in enumerate(parts):
            shift = jnp.where(found[j] >= 0, peak, 1e30) if j < DMAX else peak
            w = jnp.exp2((x - shift) * SCALE2)
            t = w[:, :HD] + w[:, HD:]
            total = t if total is None else total + t
            weights.append(w)
        inv = 1.0 / jnp.sum(total, axis=1, keepdims=True)
        w_b = jnp.concatenate([w.astype(BF16) for w in weights], axis=1)
        out = dot(w_b, vs[:nk, :], 1, 0) * inv
        o_ref[rows, :] = out.astype(BF16)
        g_b = (g.astype(F32) * inv).astype(BF16)
        dot_out = jnp.sum(g_b.astype(F32) * out, axis=1, keepdims=True)
        grad_probs = dot(g_b, vs[:nk, :], 1, 1)
        grad_scores = jnp.concatenate(
            [
                (weights[j] * (grad_probs[:, j * BLK : (j + 1) * BLK] - dot_out)).astype(BF16)
                for j in range(DMAX + b + 1)
            ],
            axis=1,
        )
        dq_ref[rows, :] = (dot(grad_scores, ks[:nk, :], 1, 0) * SCALE).astype(BF16)
        dks[:nk, :] += dot(grad_scores, q, 0, 0)
        dvs[:nk, :] += dot(w_b, g_b, 0, 0)

    @pl.when(h == GROUP - 1)
    def _():
        dkv_ref[:, :HD] = dks[nr:, :] * SCALE
        dkv_ref[:, HD:] = dvs[nr:, :]
        terms_ref[...] = jnp.zeros_like(terms_ref)
        for j in range(DMAX):

            @pl.when(found[j] >= 0)
            def _():
                at = found[j] // nb
                terms_ref[at, :, :HD] = (dks[j * BLK : (j + 1) * BLK, :] * SCALE).astype(BF16)
                terms_ref[at, :, HD:] = dvs[j * BLK : (j + 1) * BLK, :].astype(BF16)


def attention(here, parent, q, g, kv, arrived, ends):
    span = q.shape[0]
    nb = span // BLK
    n_ctx = arrived.shape[0]
    keys = (DMAX + nb) * BLK

    def whole(*shape):
        return pl.BlockSpec(shape, lambda h, here, parent: (0,) * len(shape))

    def above(steps):
        return pl.BlockSpec(
            (1, BLK, 2 * HD), lambda h, here, parent: (source(here, nb, parent, steps), 0, 0)
        )

    head = pl.BlockSpec((span, HD), lambda h, here, parent: (0, h))
    spec = pltpu.PrefetchScalarGridSpec(
        num_scalar_prefetch=2,
        grid=(GROUP,),
        in_specs=[head, head, whole(span, 2 * HD)]
        + [above(j + 1) for j in range(DMAX)]
        + [whole(nb, BLK)],
        out_specs=[head, head, whole(span, 2 * HD), whole(n_ctx, BLK, 2 * HD)],
        scratch_shapes=[
            pltpu.VMEM((keys, HD), BF16),
            pltpu.VMEM((keys, HD), BF16),
            pltpu.VMEM((keys, HD), F32),
            pltpu.VMEM((keys, HD), F32),
            pltpu.VMEM((nb, BLK, BLK), F32),
        ],
    )
    pairs = GROUP * sum(DMAX + b + 1 for b in range(nb)) * BLK * BLK
    return pl.pallas_call(
        functools.partial(attention_kernel, nb),
        grid_spec=spec,
        out_shape=[
            jax.ShapeDtypeStruct(q.shape, BF16),
            jax.ShapeDtypeStruct(q.shape, BF16),
            jax.ShapeDtypeStruct((span, 2 * HD), F32),
            jax.ShapeDtypeStruct((n_ctx, BLK, 2 * HD), BF16),
        ],
        compiler_params=pltpu.CompilerParams(vmem_limit_bytes=56 * 2**20),
        cost_estimate=pl.CostEstimate(
            flops=12 * pairs * HD, bytes_accessed=8 * span * 4 * HD, transcendentals=pairs
        ),
        name="tree_attention",
    )(here, parent, q, g, kv, arrived, arrived, arrived, arrived, ends)


def swap(x):
    return lax.all_to_all(x, "head", split_axis=0, concat_axis=0, tiled=True)


def local(queries, keys, values, grad_out, parent, subtree_end):
    n_head = lax.axis_size("head")
    n_ctx = lax.axis_size("ctx")
    here = lax.axis_index("ctx").astype(jnp.int32).reshape(1)
    rows = queries.shape[0]
    span = rows * n_head
    nb = span // BLK

    def split(x):
        return x.reshape(rows, n_head, -1)

    def by_head(x):
        return swap(x.transpose(1, 0, 2)).reshape(span, -1)

    kv = by_head(jnp.concatenate([split(keys), split(values)], axis=2))
    arrived = lax.all_gather(kv[:BLK], "ctx", axis=0, tiled=False)
    q = by_head(split(queries))
    g = by_head(split(grad_out))
    out, dq, dkv, terms = attention(here, parent, q, g, kv, arrived, subtree_end.reshape(nb, BLK))

    def by_token(x):
        return swap(x.reshape(n_head, rows, -1)).transpose(1, 0, 2)

    received = lax.all_to_all(terms, "ctx", split_axis=0, concat_axis=0, tiled=True)
    summed = jnp.sum(received.astype(F32), axis=0)
    dkv = jnp.concatenate([dkv[:BLK] + summed, dkv[BLK:]], axis=0).astype(BF16)
    attn_out = by_token(out).reshape(rows, -1)
    grad_q = by_token(dq).reshape(rows, -1)
    grads = by_token(dkv)
    return attn_out, grad_q, grads[:, :, :HD].reshape(rows, -1), grads[:, :, HD:].reshape(rows, -1)


def solution(mesh):
    placed = P(("ctx", "head"), None)
    return jax.shard_map(
        local,
        mesh=mesh,
        in_specs=(placed, placed, placed, placed, P(), P("ctx")),
        out_specs=(placed, placed, placed, placed),
        check_vma=False,
    )
```

time: 326 us -> 184 us (0.56)
  local copies, waits for them, and re-layouts: 97.6 us -> 10.7 us
  blocking collectives: 0 us -> 62.6 us
  matrix products: 58.3 us -> 0 us
  waiting for transfers between devices: 85.1 us -> 48.1 us
  Pallas kernels: 0 us -> 24.8 us
  other arithmetic: 26.7 us -> 2.11 us
  starting transfers between devices: 40.5 us -> 20.6 us
    all_to_all x0 -> x3, blocking collectives: none -> 62.6 us  [the longest x2 32 us: swap(): return lax.all_to_all(x, 'head', split_axis=0, concat_axis=0, tiled=True)]
    dot_general x19 -> x0, matrix products: 58.3 us -> none  [the longest x3 20.9 us: attend(): jnp.einsum('kgqn,qkgd->nkd', probs_b, g_blk, preferred_element_type=jnp.f...]
    unnamed x3 -> x1, waiting for transfers between devices: 45 us -> 0.02 us
    gather x10 -> x0, local copies, waits for them, and re-layouts: 40.7 us -> none  [the longest x3 32.7 us: attend(): ends[key_pos][None, :]]
    pallas_call x0 -> x1, Pallas kernels: none -> 24.8 us  [attention(): pl.pallas_call(functools.partial(attention_kernel, nb), grid_spec=spec, o...]
    all_to_all x8 -> x4, starting transfers between devices: 40.4 us -> 20.5 us  [swap(): return lax.all_to_all(x, 'head', split_axis=0, concat_axis=0, tiled=True)]
    unnamed x39 -> x15, local copies, waits for them, and re-layouts: 18.5 us -> 0.96 us
    reshape x6 -> x0, other arithmetic: 14.3 us -> none  [the longest x1 5.44 us: local(): outputs.reshape(span, 1, q_width)]
  transfers between devices with their start and end apart: 10 -> 5, of which waited for: 8 -> 5; matrix products, arithmetic and copies ran while one was open for 15% -> 5% of each run, Pallas kernels for 0% -> 0%
where the time goes in v1:
time: 184 us; the launch traced here: 183 us
  blocking collectives  62.6 us (34%)
  waiting for transfers between devices  48.1 us (26%)
  Pallas kernels  24.8 us (13%)
  starting transfers between devices  20.6 us (11%)
  between operations  14.1 us (8%)
  local copies, waits for them, and re-layouts  10.7 us (6%)
  other arithmetic  2.11 us (1%)
    all_to_all x4, waiting for transfers between devices, swap(): return lax.all_to_all(x, 'head', split_axis=0, concat_axis=0, tiled=True)  37.4 us
    all_to_all x2, blocking collectives, swap(): return lax.all_to_all(x, 'head', split_axis=0, concat_axis=0, tiled=True)  32 us
    all_to_all x1, blocking collectives, local(): lax.all_to_all(terms, 'ctx', split_axis=0, concat_axis=0, tiled=True)  30.6 us
    pallas_call x1, Pallas kernels, attention(): pl.pallas_call(functools.partial(attention_kernel, nb), grid_spec=spec, o...  24.8 us
    all_to_all x4, starting transfers between devices, swap(): return lax.all_to_all(x, 'head', split_axis=0, concat_axis=0, tiled=True)  20.5 us
    all_gather x1, waiting for transfers between devices, local(): arrived = lax.all_gather(kv[:BLK], 'ctx', axis=0, tiled=False)  10.8 us
  transfers between devices with their start and end apart: 5, of which 5 were waited for; matrix products, arithmetic and copies ran while one was open for 5% of the time, Pallas kernels for 0%

profile of v1, /device:TPU:1, one launch (start us, length us, event | category | flops | bytes accessed | tf_op | source)
XLA Modules:
  0.0 183.1 jit_solution(6608510179732678495)
XLA Ops:
  7.2 0.0 copy-start
  7.2 0.0 copy-start.1
  7.2 0.0 all-gather.3.cloned.1.call-start
  7.2 0.9 copy-done
  8.1 1.0 copy_bitcast_fusion.2
  9.2 0.0 copy-start.2
  9.2 13.8 %all_to_all.35 = bf16[8,96,256]{2,1,0:T(8,128)(2,1)S(1)} all-to-all(bf16[8,96,256]{2,1,0:T(8,128)(2,1)S(1)} %maximum_bitcast_fusion), channel_id=1, replica_groups=mesh['ctx'=16,'head'=8] {'head'}, dimensions={0} | all-to-all | bytes 786432 | tf_op jit(solution)/shard_map/all_to_all | solution.py:164
  23.0 0.0 copy-start.5
  23.0 0.7 slice.21
  23.7 0.0 all-gather.3.cloned.1.call-update
  23.7 0.0 copy-done.1
  23.7 1.0 copy.33
  24.7 0.0 copy-start.6
  24.7 4.4 %all-to-all-start = ((bf16[8,96,512]{2,1,0:T(8,128)(2,1)}), bf16[8,96,512]{2,1,0:T(8,128)(2,1)S(1)}, u32[]{:S(2)}, u32[]{:S(2)}) async-start(bf16[8,96,512]{2,1,0:T(8,128)(2,1)} %bitcast.48), calls=%async_computation | async-start | bytes 1572864 | tf_op jit(solution)/shard_map/all_to_all | solution.py:164
  29.1 0.0 copy-done.2
  29.1 1.0 copy.32
  30.1 0.0 copy-done.5
  30.1 11.3 %all-to-all-done = bf16[8,96,512]{2,1,0:T(8,128)(2,1)S(1)} async-done(((bf16[8,96,512]{2,1,0:T(8,128)(2,1)}), bf16[8,96,512]{2,1,0:T(8,128)(2,1)S(1)}, u32[]{:S(2)}, u32[]{:S(2)}) %all-to-all-start) | async-done | bytes 786464 | tf_op jit(solution)/shard_map/all_to_all | solution.py:164
  41.4 0.0 copy-start.3
  41.4 4.3 %all-to-all-start.1 = ((bf16[8,96,512]{2,1,0:T(8,128)(2,1)}), bf16[8,96,512]{2,1,0:T(8,128)(2,1)S(1)}, u32[]{:S(2)}, u32[]{:S(2)}) async-start(bf16[8,96,512]{2,1,0:T(8,128)(2,1)} %bitcast.46), calls=%async_computation.1 | async-start | bytes 1572864 | tf_op jit(solution)/shard_map/all_to_all | solution.py:164
  45.8 0.0 copy-done.6
  45.8 0.6 reshape.64.end_ref
  46.4 11.7 %all-to-all-done.1 = bf16[8,96,512]{2,1,0:T(8,128)(2,1)S(1)} async-done(((bf16[8,96,512]{2,1,0:T(8,128)(2,1)}), bf16[8,96,512]{2,1,0:T(8,128)(2,1)S(1)}, u32[]{:S(2)}, u32[]{:S(2)}) %all-to-all-start.1) | async-done | bytes 786464 | tf_op jit(solution)/shard_map/all_to_all | solution.py:164
  58.1 0.0 copy-start.4
  58.1 10.8 %all-gather.3.cloned.1.call-done = bf16[4096,256]{1,0:T(8,128)(2,1)} async-done(((bf16[256,256]{1,0:T(8,128)(2,1)}), bf16[4096,256]{1,0:T(8,128)(2,1)}) %all-gather.3.cloned.1.call-update) | async-done | bytes 2097168 | tf_op jit(solution)/shard_map/all_gather | solution.py:182
  68.8 0.0 copy-done.3
  68.8 0.0 copy-done.4
  68.8 24.8 %tree_attention.1 = (bf16[768,512]{1,0:T(8,128)(2,1)}, bf16[768,512]{1,0:T(8,128)(2,1)}, f32[768,256]{1,0:T(8,128)}, bf16[16,256,256]{2,1,0:T(8,128)(2,1)}) custom-call(s32[1]{0:T(128)} %bitcast.here, s32[48]{0:T(128)} %parent.1, bf16[768,512]{1,0:T(8,128)(2,1)} %bitcast.55, bf16[768,512]{1,0:T(8,128)(2,1)} %bitcast.56, bf16[768,256]{1,0:T(8,128)(2,1)} %bitcast.62, ...), custom_call_target="tpu_custom_call" | custom-call | flops 7247757312 | bytes 3145728 | tf_op jit(solution)/shard_map/tree_attention/pallas_call | solution.py:146
  93.6 18.2 %all_to_all.36 = bf16[8,96,512]{2,1,0:T(8,128)(2,1)S(1)} all-to-all(bf16[8,96,512]{2,1,0:T(8,128)(2,1)} %bitcast.60), channel_id=1, replica_groups=mesh['ctx'=16,'head'=8] {'head'}, dimensions={0} | all-to-all | bytes 1572864 | tf_op jit(solution)/shard_map/all_to_all | solution.py:164
  111.8 30.6 %all_to_all.37 = bf16[16,256,256]{2,1,0:T(8,128)(2,1)S(1)} all-to-all(bf16[16,256,256]{2,1,0:T(8,128)(2,1)} %get-tuple-element.11), channel_id=1, replica_groups=mesh['ctx'=16,'head'=8] {'ctx'}, dimensions={0} | all-to-all | bytes 4194304 | tf_op jit(solution)/shard_map/all_to_all | solution.py:190
  142.5 7.5 %all-to-all-start.3 = ((bf16[8,96,512]{2,1,0:T(8,128)(2,1)}), bf16[8,96,512]{2,1,0:T(8,128)(2,1)}, u32[]{:S(2)}, u32[]{:S(2)}) async-start(bf16[8,96,512]{2,1,0:T(8,128)(2,1)} %bitcast.57), calls=%async_computation.3 | async-start | bytes 1572864 | tf_op jit(solution)/shard_map/all_to_all | solution.py:164
  150.0 1.1 slice.29
  151.1 0.3 convert_reduce_fusion
  151.3 1.0 add_convert_fusion
  152.3 0.8 pad_maximum_fusion
  153.1 9.3 %all-to-all-done.3 = bf16[8,96,512]{2,1,0:T(8,128)(2,1)} async-done(((bf16[8,96,512]{2,1,0:T(8,128)(2,1)}), bf16[8,96,512]{2,1,0:T(8,128)(2,1)}, u32[]{:S(2)}, u32[]{:S(2)}) %all-to-all-start.3) | async-done | bytes 786464 | tf_op jit(solution)/shard_map/all_to_all | solution.py:164
  162.4 4.2 %all-to-all-start.6 = ((bf16[8,96,256]{2,1,0:T(8,128)(2,1)}), bf16[8,96,256]{2,1,0:T(8,128)(2,1)S(1)}, u32[]{:S(2)}, u32[]{:S(2)}) async-start(bf16[8,96,256]{2,1,0:T(8,128)(2,1)} %bitcast.12), calls=%async_computation.6 | async-start | bytes 786432 | tf_op jit(solution)/shard_map/all_to_all | solution.py:164
  166.6 1.0 copy.23
  167.6 2.1 %copy.22 = bf16[8,12,8,512]{3,2,0,1:T(8,128)(2,1)} copy(bf16[8,12,8,512]{3,2,1,0:T(8,128)(2,1)} %bitcast.22) | data formatting | bytes 1572864 | tf_op jit(solution)/shard_map/reshape | solution.py:193
  169.7 5.0 %all-to-all-done.6 = bf16[8,96,256]{2,1,0:T(8,128)(2,1)S(1)} async-done(((bf16[8,96,256]{2,1,0:T(8,128)(2,1)}), bf16[8,96,256]{2,1,0:T(8,128)(2,1)S(1)}, u32[]{:S(2)}, u32[]{:S(2)}) %all-to-all-start.6) | async-done | bytes 393248 | tf_op jit(solution)/shard_map/all_to_all | solution.py:164
  174.7 0.1 slice_bitcast_fusion
  174.8 0.7 copy.34
  175.5 0.7 copy.35
  (1 shorter events, 0.0 us)
Async XLA Ops:
  7.2 0.9 copy-start
  7.2 16.5 %copy-start.1 = (bf16[96,4096]{1,0:T(8,128)(2,1)S(1)}, bf16[96,4096]{1,0:T(8,128)(2,1)}, u32[]{:S(2)}) copy-start(bf16[96,4096]{1,0:T(8,128)(2,1)} %param.6) | copy-start | bytes 2359300
  7.2 61.6 %all-gather.3.cloned.1.call-start = ((), (), s32[]{:S(2)}) async-start(), calls=%async_computation.7 | async-start | bytes 2228224 | tf_op jit(solution)/shard_map/all_gather | solution.py:182
  9.2 20.0 %copy-start.2 = (bf16[96,4096]{1,0:T(8,128)(2,1)S(1)}, bf16[96,4096]{1,0:T(8,128)(2,1)}, u32[]{:S(2)}) copy-start(bf16[96,4096]{1,0:T(8,128)(2,1)} %param.9) | copy-start | bytes 2359300
  23.0 7.1 %copy-start.5 = (bf16[8,96,256]{2,1,0:T(8,128)(2,1)}, bf16[8,96,256]{2,1,0:T(8,128)(2,1)S(1)}, u32[]{:S(2)}) copy-start(bf16[8,96,256]{2,1,0:T(8,128)(2,1)S(1)} %all_to_all.35) | copy-start | bytes 1179652
  24.7 21.1 %copy-start.6 = (s32[768]{0:T(1024)S(1)}, s32[768]{0:T(1024)}, u32[]{:S(2)}) copy-start(s32[768]{0:T(1024)} %param.11) | copy-start | bytes 9220
  24.7 16.8 %all-to-all-start = ((bf16[8,96,512]{2,1,0:T(8,128)(2,1)}), bf16[8,96,512]{2,1,0:T(8,128)(2,1)S(1)}, u32[]{:S(2)}, u32[]{:S(2)}) async-start(bf16[8,96,512]{2,1,0:T(8,128)(2,1)} %bitcast.48), calls=%async_computation | async-start | bytes 1572864 | tf_op jit(solution)/shard_map/all_to_all | solution.py:164
  41.4 27.4 %copy-start.3 = (bf16[8,96,512]{2,1,0:T(8,128)(2,1)}, bf16[8,96,512]{2,1,0:T(8,128)(2,1)S(1)}, u32[]{:S(2)}) copy-start(bf16[8,96,512]{2,1,0:T(8,128)(2,1)S(1)} %all-to-all-done) | copy-start | bytes 2359300
  41.4 16.6 %all-to-all-start.1 = ((bf16[8,96,512]{2,1,0:T(8,128)(2,1)}), bf16[8,96,512]{2,1,0:T(8,128)(2,1)S(1)}, u32[]{:S(2)}, u32[]{:S(2)}) async-start(bf16[8,96,512]{2,1,0:T(8,128)(2,1)} %bitcast.46), calls=%async_computation.1 | async-start | bytes 1572864 | tf_op jit(solution)/shard_map/all_to_all | solution.py:164
  58.1 10.8 %copy-start.4 = (bf16[8,96,512]{2,1,0:T(8,128)(2,1)}, bf16[8,96,512]{2,1,0:T(8,128)(2,1)S(1)}, u32[]{:S(2)}) copy-start(bf16[8,96,512]{2,1,0:T(8,128)(2,1)S(1)} %all-to-all-done.1) | copy-start | bytes 2359300
  142.5 19.9 %all-to-all-start.3 = ((bf16[8,96,512]{2,1,0:T(8,128)(2,1)}), bf16[8,96,512]{2,1,0:T(8,128)(2,1)}, u32[]{:S(2)}, u32[]{:S(2)}) async-start(bf16[8,96,512]{2,1,0:T(8,128)(2,1)} %bitcast.57), calls=%async_computation.3 | async-start | bytes 1572864 | tf_op jit(solution)/shard_map/all_to_all | solution.py:164
  162.4 12.3 %all-to-all-start.6 = ((bf16[8,96,256]{2,1,0:T(8,128)(2,1)}), bf16[8,96,256]{2,1,0:T(8,128)(2,1)S(1)}, u32[]{:S(2)}, u32[]{:S(2)}) async-start(bf16[8,96,256]{2,1,0:T(8,128)(2,1)} %bitcast.12), calls=%async_computation.6 | async-start | bytes 786432 | tf_op jit(solution)/shard_map/all_to_all | solution.py:164
Sparse Core Ops, SparseCore 0:
  23.8 44.9 all-gather.2

commit v2 on v1

v2 whole, which is shorter than its diff:
```python
import functools

import jax
import jax.numpy as jnp
from jax import lax
from jax.experimental import pallas as pl
from jax.experimental.pallas import tpu as pltpu
from jax.sharding import PartitionSpec as P

HQ = 32
KVH = 8
HD = 128
BLK = 256
DMAX = 4
GROUP = HQ // KVH
SIDE = 4
SCALE = HD**-0.5
SCALE2 = SCALE * 1.4426950408889634
F32 = jnp.float32
BF16 = jnp.bfloat16


def dot(a, b, ca, cb):
    return lax.dot_general(a, b, (((ca,), (cb,)), ((), ())), preferred_element_type=F32)


def ring_pairs(side, cores, along, by):
    pairs = []
    for y in range(side):
        for z in range(side):
            for h in range(cores):
                if (along + h) % 2:
                    to = y * side + (z + by) % side
                else:
                    to = (y + by) % side * side + z
                pairs.append(((y * side + z) * cores + h, to * cores + h))
    return pairs


def shifted(x, along, by):
    pairs = ring_pairs(SIDE, lax.axis_size("head"), along, by)
    return lax.ppermute(x, ("ctx", "head"), pairs)


def offsets(here, device):
    dy = (here[0] // SIDE - device // SIDE) % SIDE
    dz = (here[0] % SIDE - device % SIDE) % SIDE
    odd = here[1] % 2 == 1
    return jnp.where(odd, dz, dy), jnp.where(odd, dy, dz)


def attention_kernel(
    nb, here, parent, q_ref, g_ref, kv_ref, a0, a1, a2, a3, end_ref,
    out_ref, dkv_ref, terms_ref, ks, vs, dks, dvs, bias,
):
    h = pl.program_id(0)
    nr = DMAX * BLK
    found = []
    current = here[0] * nb
    for _ in range(DMAX):
        current = jnp.where(current >= 0, parent[jnp.maximum(current, 0)], -1)
        found.append(current)

    @pl.when(h == 0)
    def _():
        for j in range(DMAX):
            second, first = offsets(here, jnp.maximum(found[j], 0) // nb)
            for s, r in enumerate((a0, a1, a2, a3)):

                @pl.when(second == s)
                def _():
                    ks[j * BLK : (j + 1) * BLK] = r[first, :, :HD]
                    vs[j * BLK : (j + 1) * BLK] = r[first, :, HD:]

        ks[nr:] = kv_ref[:, :HD]
        vs[nr:] = kv_ref[:, HD:]
        dks[...] = jnp.zeros_like(dks)
        dvs[...] = jnp.zeros_like(dvs)
        i = lax.broadcasted_iota(jnp.int32, (BLK, BLK), 0)
        p = lax.broadcasted_iota(jnp.int32, (BLK, BLK), 1)
        for b in range(nb):
            ok = (p <= i) & (i <= end_ref[b : b + 1, :])
            bias[b] = jnp.where(ok, 0.0, -1e30)

    for b in range(nb):
        rows = pl.ds(b * BLK, BLK)
        q = q_ref[rows, :]
        g = g_ref[rows, :]
        nk = nr + (b + 1) * BLK
        scores = dot(q, ks[:nk, :], 1, 1)
        parts = [scores[:, j * BLK : (j + 1) * BLK] for j in range(DMAX + b + 1)]
        parts[-1] = parts[-1] + bias[b]
        peak = None
        for j, x in enumerate(parts):
            t = jnp.maximum(x[:, :HD], x[:, HD:])
            if j < DMAX:
                t = jnp.where(found[j] >= 0, t, -3e38)
            peak = t if peak is None else jnp.maximum(peak, t)
        peak = jnp.max(peak, axis=1, keepdims=True)
        weights = []
        total = None
        for j, x in enumerate(parts):
            shift = jnp.where(found[j] >= 0, peak, 1e30) if j < DMAX else peak
            w = jnp.exp2((x - shift) * SCALE2)
            t = w[:, :HD] + w[:, HD:]
            total = t if total is None else total + t
            weights.append(w)
        inv = 1.0 / jnp.sum(total, axis=1, keepdims=True)
        w_b = jnp.concatenate([w.astype(BF16) for w in weights], axis=1)
        out = dot(w_b, vs[:nk, :], 1, 0) * inv
        out_ref[rows, pl.ds(pl.multiple_of(h * HD, HD), HD)] = out.astype(BF16)
        g_b = (g.astype(F32) * inv).astype(BF16)
        dot_out = jnp.sum(g_b.astype(F32) * out, axis=1, keepdims=True)
        grad_probs = dot(g_b, vs[:nk, :], 1, 1)
        grad_scores = jnp.concatenate(
            [
                (weights[j] * (grad_probs[:, j * BLK : (j + 1) * BLK] - dot_out)).astype(BF16)
                for j in range(DMAX + b + 1)
            ],
            axis=1,
        )
        dq = (dot(grad_scores, ks[:nk, :], 1, 0) * SCALE).astype(BF16)
        out_ref[rows, pl.ds(pl.multiple_of((GROUP + h) * HD, HD), HD)] = dq
        dks[:nk, :] += dot(grad_scores, q, 0, 0)
        dvs[:nk, :] += dot(w_b, g_b, 0, 0)

    @pl.when(h == GROUP - 1)
    def _():
        dkv_ref[:, :HD] = dks[nr:, :] * SCALE
        dkv_ref[:, HD:] = dvs[nr:, :]
        terms_ref[...] = jnp.zeros_like(terms_ref)
        for j in range(DMAX):

            @pl.when(found[j] >= 0)
            def _():
                second, first = offsets(here, found[j] // nb)
                at = (SIDE - second) % SIDE * SIDE + (SIDE - first) % SIDE
                terms_ref[at, :, :HD] = (dks[j * BLK : (j + 1) * BLK, :] * SCALE).astype(BF16)
                terms_ref[at, :, HD:] = dvs[j * BLK : (j + 1) * BLK, :].astype(BF16)


def attention(here, parent, qg, kv, arrived, ends):
    span = qg.shape[0]
    nb = span // BLK
    keys = (DMAX + nb) * BLK
    n_ctx = SIDE * SIDE

    def whole(*shape):
        return pl.BlockSpec(shape, lambda h, here, parent: (0,) * len(shape))

    spec = pltpu.PrefetchScalarGridSpec(
        num_scalar_prefetch=2,
        grid=(GROUP,),
        in_specs=[
            pl.BlockSpec((span, HD), lambda h, here, parent: (0, h)),
            pl.BlockSpec((span, HD), lambda h, here, parent: (0, GROUP + h)),
            whole(span, 2 * HD),
        ]
        + [whole(SIDE, BLK, 2 * HD)] * SIDE
        + [whole(nb, BLK)],
        out_specs=[
            whole(span, 2 * GROUP * HD),
            whole(span, 2 * HD),
            whole(n_ctx, BLK, 2 * HD),
        ],
        scratch_shapes=[
            pltpu.VMEM((keys, HD), BF16),
            pltpu.VMEM((keys, HD), BF16),
            pltpu.VMEM((keys, HD), F32),
            pltpu.VMEM((keys, HD), F32),
            pltpu.VMEM((nb, BLK, BLK), F32),
        ],
    )
    pairs = GROUP * sum(DMAX + b + 1 for b in range(nb)) * BLK * BLK
    return pl.pallas_call(
        functools.partial(attention_kernel, nb),
        grid_spec=spec,
        out_shape=[
            jax.ShapeDtypeStruct(qg.shape, BF16),
            jax.ShapeDtypeStruct((span, 2 * HD), F32),
            jax.ShapeDtypeStruct((n_ctx, BLK, 2 * HD), BF16),
        ],
        compiler_params=pltpu.CompilerParams(vmem_limit_bytes=56 * 2**20),
        cost_estimate=pl.CostEstimate(
            flops=12 * pairs * HD, bytes_accessed=8 * span * 4 * HD, transcendentals=pairs
        ),
        name="tree_attention",
    )(here, parent, qg, qg, kv, *arrived, ends)


def swap(x):
    return lax.all_to_all(x, "head", split_axis=0, concat_axis=0, tiled=True)


def local(queries, keys, values, grad_out, parent, subtree_end):
    n_head = lax.axis_size("head")
    here = jnp.stack([lax.axis_index("ctx"), lax.axis_index("head")]).astype(jnp.int32)
    rows = queries.shape[0]
    span = rows * n_head
    nb = span // BLK

    def by_head(x, y):
        both = [a.reshape(rows, n_head, -1) for a in (x, y)]
        return swap(jnp.concatenate(both, axis=2).transpose(1, 0, 2)).reshape(span, -1)

    kv = by_head(keys, values)
    first = kv[:BLK]
    line = jnp.stack([first] + [shifted(first, 1, s) for s in range(1, SIDE)])
    arrived = [line] + [shifted(line, 0, s) for s in range(1, SIDE)]
    qg = by_head(queries, grad_out)
    out, dkv, terms = attention(here, parent, qg, kv, arrived, subtree_end.reshape(nb, BLK))

    def send_back(x):
        return swap(x.reshape(n_head, rows, -1))

    def by_token(x):
        return [a.reshape(rows, -1) for a in jnp.split(x.transpose(1, 0, 2), 2, axis=2)]

    out = send_back(out)

    terms = terms.reshape(SIDE, SIDE, BLK, 2 * HD)
    part = terms[0].astype(F32)
    for s in range(1, SIDE):
        part = part + shifted(terms[s], 0, s).astype(F32)
    part_b = part.astype(BF16)
    summed = part[0]
    for s in range(1, SIDE):
        summed = summed + shifted(part_b[s], 1, s).astype(F32)
    dkv = jnp.concatenate([dkv[:BLK] + summed, dkv[BLK:]], axis=0).astype(BF16)
    out, dkv = lax.optimization_barrier((out, dkv))
    attn_out, grad_q = by_token(out)
    grad_k, grad_v = by_token(send_back(dkv))
    return attn_out, grad_q, grad_k, grad_v


def solution(mesh):
    placed = P(("ctx", "head"), None)
    return jax.shard_map(
        local,
        mesh=mesh,
        in_specs=(placed, placed, placed, placed, P(), P("ctx")),
        out_specs=(placed, placed, placed, placed),
        check_vma=False,
    )
```

time: 184 us -> 125 us (0.68)
  blocking collectives: 62.6 us -> 0 us
  starting transfers between devices: 20.6 us -> 39.1 us
  between operations: 14.1 us -> 0.76 us
  waiting for transfers between devices: 48.1 us -> 43.1 us
  other arithmetic: 2.11 us -> 5.07 us
    all_to_all x3 -> x0, blocking collectives: 62.6 us -> none  [the longest x2 32 us: swap(): return lax.all_to_all(x, 'head', split_axis=0, concat_axis=0, tiled=True)]
    ppermute x0 -> x12, waiting for transfers between devices: none -> 25.1 us  [shifted(): return lax.ppermute(x, ('ctx', 'head'), pairs)]
    all_to_all x4, waiting for transfers between devices: 37.4 us -> 18 us  [swap(): return lax.all_to_all(x, 'head', split_axis=0, concat_axis=0, tiled=True)]
    ppermute x0 -> x12, starting transfers between devices: none -> 16.9 us  [shifted(): return lax.ppermute(x, ('ctx', 'head'), pairs)]
    all_gather x1 -> x0, waiting for transfers between devices: 10.8 us -> none  [local(): arrived = lax.all_gather(kv[:BLK], 'ctx', axis=0, tiled=False)]
    reshape x7 -> x6, local copies, waits for them, and re-layouts: 7.4 us -> 4.5 us  [the longest x4 3.34 us: by_token(): a.reshape(rows, -1)]
    transpose x1 -> x2, other arithmetic: 0.05 us -> 2.19 us  [by_head(): jnp.concatenate(both, axis=2).transpose(1, 0, 2)]
  transfers between devices with their start and end apart: 5 -> 16, of which waited for: 5 -> 9; matrix products, arithmetic and copies ran while one was open for 5% -> 6% of each run, Pallas kernels for 0% -> 0%
where the time goes in v2:
time: 125 us; the launch traced here: 124 us
  waiting for transfers between devices  43.1 us (34%)
  starting transfers between devices  39.1 us (31%)
  Pallas kernels  25.3 us (20%)
  local copies, waits for them, and re-layouts  10.9 us (9%)
  other arithmetic  5.07 us (4%)
    pallas_call x1, Pallas kernels, attention(): pl.pallas_call(functools.partial(attention_kernel, nb), grid_spec=spec, o...  25.3 us
    ppermute x12, waiting for transfers between devices, shifted(): return lax.ppermute(x, ('ctx', 'head'), pairs)  25.1 us
    all_to_all x4, starting transfers between devices, swap(): return lax.all_to_all(x, 'head', split_axis=0, concat_axis=0, tiled=True)  22.3 us
    all_to_all x4, waiting for transfers between devices, swap(): return lax.all_to_all(x, 'head', split_axis=0, concat_axis=0, tiled=True)  18 us
    ppermute x12, starting transfers between devices, shifted(): return lax.ppermute(x, ('ctx', 'head'), pairs)  16.9 us
    reshape x4, local copies, waits for them, and re-layouts, by_token(): a.reshape(rows, -1)  3.34 us
    slice x1, local copies, waits for them, and re-layouts, local(): part = part + shifted(terms[s], 0, s).astype(F32)  2.54 us
  transfers between devices with their start and end apart: 16, of which 9 were waited for; matrix products, arithmetic and copies ran while one was open for 6% of the time, Pallas kernels for 0%

profile of v2, /device:TPU:1, one launch (start us, length us, event | category | flops | bytes accessed | tf_op | source)
XLA Modules:
  0.0 124.3 jit_solution(2648813220298852269)
XLA Ops:
  0.6 0.0 copy-start
  0.6 0.0 copy-start.2
  0.7 0.0 copy-start.3
  0.7 0.9 copy-done
  1.6 1.0 copy_bitcast_fusion.4
  2.6 0.8 maximum_bitcast_fusion.1
  3.4 5.8 %all-to-all-start.1 = ((bf16[8,96,256]{2,1,0:T(8,128)(2,1)}), bf16[8,96,256]{2,1,0:T(8,128)(2,1)}, u32[]{:S(2)}, u32[]{:S(2)}) async-start(bf16[8,96,256]{2,1,0:T(8,128)(2,1)} %maximum_bitcast_fusion.1), calls=%async_computation.1 | async-start | bytes 786432 | tf_op jit(solution)/shard_map/all_to_all | solution.py:192
  9.2 0.0 copy-done.2
  9.2 0.0 copy-done.3
  9.2 0.2 copy_bitcast_fusion
  9.3 1.4 %maximum_bitcast_fusion = bf16[8,96,1024]{2,1,0:T(8,128)(2,1)} fusion(bf16[96,8,512]{2,0,1:T(8,128)(2,1)S(1)} %get-tuple-element.28, bf16[96,8,512]{2,0,1:T(8,128)(2,1)S(1)} %get-tuple-element.29), kind=kLoop, calls=%fused_computation | loop fusion | flops 3145728 | bytes 3145728 | tf_op jit(solution)/shard_map/transpose | solution.py:204
  10.7 6.6 %all-to-all-done.1 = bf16[8,96,256]{2,1,0:T(8,128)(2,1)} async-done(((bf16[8,96,256]{2,1,0:T(8,128)(2,1)}), bf16[8,96,256]{2,1,0:T(8,128)(2,1)}, u32[]{:S(2)}, u32[]{:S(2)}) %all-to-all-start.1) | async-done | bytes 393248 | tf_op jit(solution)/shard_map/all_to_all | solution.py:192
  17.3 4.4 %all-to-all-start = ((bf16[8,96,1024]{2,1,0:T(8,128)(2,1)}), bf16[8,96,1024]{2,1,0:T(8,128)(2,1)S(1)}, u32[]{:S(2)}, u32[]{:S(2)}) async-start(bf16[8,96,1024]{2,1,0:T(8,128)(2,1)} %maximum_bitcast_fusion), calls=%async_computation | async-start | bytes 3145728 | tf_op jit(solution)/shard_map/all_to_all | solution.py:192
  21.7 0.9 slice_bitcast_fusion.8
  22.6 3.0 %collective-permute-start.1 = (bf16[256,256]{1,0:T(8,128)(2,1)S(1)}, bf16[256,256]{1,0:T(8,128)(2,1)S(1)}, u32[]{:S(2)}, u32[]{:S(2)}) collective-permute-start(bf16[256,256]{1,0:T(8,128)(2,1)S(1)} %get-tuple-element.27), channel_id=1, source_target_pairs={{0,16},{1,65},{2,18},{3,67},{4,20},{5,69},{6,22},{7,71},{8,24},{9,... | collective-permute-start | bytes 393224 | tf_op jit(solution)/shard_map/ppermute | solution.py:42
  25.6 0.4 collective-permute-start
  26.0 2.3 %collective-permute-start.2 = (bf16[256,256]{1,0:T(8,128)(2,1)S(1)}, bf16[256,256]{1,0:T(8,128)(2,1)S(1)}, u32[]{:S(2)}, u32[]{:S(2)}) collective-permute-start(bf16[256,256]{1,0:T(8,128)(2,1)S(1)} %get-tuple-element.27), channel_id=1, source_target_pairs={{0,24},{1,97},{2,26},{3,99},{4,28},{5,101},{6,30},{7,103},{8,0},{9... | collective-permute-start | bytes 393224 | tf_op jit(solution)/shard_map/ppermute | solution.py:42
  28.3 0.0 collective-permute-done.1
  28.3 2.3 %collective-permute-done = bf16[256,256]{1,0:T(8,128)(2,1)S(1)} collective-permute-done((bf16[256,256]{1,0:T(8,128)(2,1)S(1)}, bf16[256,256]{1,0:T(8,128)(2,1)S(1)}, u32[]{:S(2)}, u32[]{:S(2)}) %collective-permute-start) | collective-permute-done | bytes 131104 | tf_op jit(solution)/shard_map/ppermute | solution.py:42
  30.6 0.0 collective-permute-done.2
  30.6 0.1 pad_maximum_fusion.a0
  30.7 0.0 copy-start.4
  30.7 4.1 %collective-permute-start.5 = (bf16[4,256,256]{2,1,0:T(8,128)(2,1)S(1)}, bf16[4,256,256]{2,1,0:T(8,128)(2,1)S(1)}, u32[]{:S(2)}, u32[]{:S(2)}) collective-permute-start(bf16[4,256,256]{2,1,0:T(8,128)(2,1)S(1)} %pad_maximum_fusion.a0), channel_id=1, source_target_pairs={{0,96},{1,25},{2,98},{3,27},{4,100},{5,29},{6,102},{7,31},{8,104},... | collective-permute-start | bytes 1572872 | tf_op jit(solution)/shard_map/ppermute | solution.py:42
  34.9 0.0 collective-permute-start.4
  34.9 0.7 collective-permute-start.3
  35.5 0.0 copy-done.6
  35.5 0.6 reshape.62.end_ref
  36.1 0.6 pad_add_fusion.here
  36.7 9.9 %collective-permute-done.5.a3 = bf16[4,256,256]{2,1,0:T(8,128)(2,1)S(1)} collective-permute-done((bf16[4,256,256]{2,1,0:T(8,128)(2,1)S(1)}, bf16[4,256,256]{2,1,0:T(8,128)(2,1)S(1)}, u32[]{:S(2)}, u32[]{:S(2)}) %collective-permute-start.5) | collective-permute-done | bytes 524320 | tf_op jit(solution)/shard_map/ppermute | solution.py:42
  46.6 0.0 collective-permute-done.4.a2
  46.6 3.5 %collective-permute-done.3.a1 = bf16[4,256,256]{2,1,0:T(8,128)(2,1)} collective-permute-done((bf16[4,256,256]{2,1,0:T(8,128)(2,1)S(1)}, bf16[4,256,256]{2,1,0:T(8,128)(2,1)}, u32[]{:S(2)}, u32[]{:S(2)}) %collective-permute-start.3) | collective-permute-done | bytes 524320 | tf_op jit(solution)/shard_map/ppermute | solution.py:42
  50.1 0.0 all-to-all-done
  50.1 0.0 copy-done.4
  50.1 0.0 copy-done.7
  50.1 0.0 copy-done.8
  50.1 1.2 copy-done.1
  51.3 25.3 %tree_attention.1 = (bf16[768,1024]{1,0:T(8,128)(2,1)}, f32[768,256]{1,0:T(8,128)}, bf16[16,256,256]{2,1,0:T(8,128)(2,1)}) custom-call(s32[2]{0:T(128)} %pad_add_fusion.here, s32[48]{0:T(128)} %parent.1, bf16[768,1024]{1,0:T(8,128)(2,1)} %bitcast.68, bf16[768,1024]{1,0:T(8,128)(2,1)} %bitcast.69, bf16[768,256]{1,0:T(8,128)(2,1)} %bitcast.5.kv_ref, ...), custom_call_target="tpu_custom_call" | custom-call | flops 7247757312 | bytes 3145728 | tf_op jit(solution)/shard_map/tree_attention/pallas_call | solution.py:175
  76.6 2.5 %fusion.6 = (bf16[4,256,256]{2,1,0:T(8,128)(2,1)}, bf16[4,256,256]{2,1,0:T(8,128)(2,1)}, bf16[4,256,256]{2,1,0:T(8,128)(2,1)}) fusion(bf16[16,256,256]{2,1,0:T(8,128)(2,1)} %get-tuple-element.11), kind=kLoop, calls=%fused_computation.28 | loop fusion | bytes 3145728 | tf_op jit(solution)/shard_map/slice | solution.py:224
  79.2 0.0 collective-permute-start.6
  79.2 2.7 %collective-permute-start.8 = (bf16[4,256,256]{2,1,0:T(8,128)(2,1)}, bf16[4,256,256]{2,1,0:T(8,128)(2,1)S(1)}, u32[]{:S(2)}, u32[]{:S(2)}) collective-permute-start(bf16[4,256,256]{2,1,0:T(8,128)(2,1)} %get-tuple-element.17), channel_id=1, source_target_pairs={{0,96},{1,25},{2,98},{3,27},{4,100},{5,29},{6,102},{7,31},{8,104},... | collective-permute-start | bytes 1572872 | tf_op jit(solution)/shard_map/ppermute | solution.py:42
  81.8 0.0 collective-permute-start.7
  81.8 7.6 %all-to-all-start.2 = ((bf16[8,96,1024]{2,1,0:T(8,128)(2,1)}), bf16[8,96,1024]{2,1,0:T(8,128)(2,1)S(1)}, u32[]{:S(2)}, u32[]{:S(2)}) async-start(bf16[8,96,1024]{2,1,0:T(8,128)(2,1)} %bitcast.10), calls=%async_computation.2 | async-start | bytes 3145728 | tf_op jit(solution)/shard_map/all_to_all | solution.py:192
  89.4 5.1 %collective-permute-done.6 = bf16[4,256,256]{2,1,0:T(8,128)(2,1)S(1)} collective-permute-done((bf16[4,256,256]{2,1,0:T(8,128)(2,1)}, bf16[4,256,256]{2,1,0:T(8,128)(2,1)S(1)}, u32[]{:S(2)}, u32[]{:S(2)}) %collective-permute-start.6) | collective-permute-done | bytes 524320 | tf_op jit(solution)/shard_map/ppermute | solution.py:42
  94.5 0.0 collective-permute-done.8
  94.5 0.0 collective-permute-done.7
  94.5 1.3 %fusion.5 = (bf16[4,256,256]{2,1,0:T(8,128)(2,1)S(1)}, f32[4,256,256]{2,1,0:T(8,128)S(1)}) fusion(bf16[4,256,256]{2,1,0:T(8,128)(2,1)S(1)} %collective-permute-done.8, bf16[4,256,256]{2,1,0:T(8,128)(2,1)S(1)} %collective-permute-done.7, bf16[4,256,256]{2,1,0:T(8,128)(2,1)S(1)} %collective-permute-done.6, bf16[16,256,256]{2,1,0:T(8,128)(2,1)} %get-tuple-element.11), kind=kLoop, calls=%fused_computation.27 | loop fusion | flops 2097152 | bytes 3670016 | tf_op jit(solution)/shard_map/convert_element_type | solution.py:225
  95.9 0.2 collective-permute-start.9
  96.1 2.5 %collective-permute-start.11 = (bf16[256,256]{1,0:T(8,128)(2,1)S(1)}, bf16[256,256]{1,0:T(8,128)(2,1)S(1)}, u32[]{:S(2)}, u32[]{:S(2)}) collective-permute-start(bf16[256,256]{1,0:T(8,128)(2,1)S(1)} %get-tuple-element.22), channel_id=1, source_target_pairs={{0,24},{1,97},{2,26},{3,99},{4,28},{5,101},{6,30},{7,103},{8,0},{9... | collective-permute-start | bytes 393224 | tf_op jit(solution)/shard_map/ppermute | solution.py:42
  98.7 1.0 collective-permute-start.10
  99.6 0.0 copy-done.5
  99.7 1.6 %collective-permute-done.9 = bf16[256,256]{1,0:T(8,128)(2,1)S(1)} collective-permute-done((bf16[256,256]{1,0:T(8,128)(2,1)S(1)}, bf16[256,256]{1,0:T(8,128)(2,1)S(1)}, u32[]{:S(2)}, u32[]{:S(2)}) %collective-permute-start.9) | collective-permute-done | bytes 131104 | tf_op jit(solution)/shard_map/ppermute | solution.py:42
  101.3 0.0 collective-permute-done.11
  101.3 2.7 %collective-permute-done.10 = bf16[256,256]{1,0:T(8,128)(2,1)S(1)} collective-permute-done((bf16[256,256]{1,0:T(8,128)(2,1)S(1)}, bf16[256,256]{1,0:T(8,128)(2,1)S(1)}, u32[]{:S(2)}, u32[]{:S(2)}) %collective-permute-start.10) | collective-permute-done | bytes 131104 | tf_op jit(solution)/shard_map/ppermute | solution.py:42
  104.0 0.1 fusion.4
  104.1 0.8 pad_maximum_fusion.1
  104.8 5.3 %all-to-all-done.2 = bf16[8,96,1024]{2,1,0:T(8,128)(2,1)S(1)} async-done(((bf16[8,96,1024]{2,1,0:T(8,128)(2,1)}), bf16[8,96,1024]{2,1,0:T(8,128)(2,1)S(1)}, u32[]{:S(2)}, u32[]{:S(2)}) %all-to-all-start.2) | async-done | bytes 1572896 | tf_op jit(solution)/shard_map/all_to_all | solution.py:192
  110.1 4.5 %all-to-all-start.3 = ((bf16[8,96,256]{2,1,0:T(8,128)(2,1)}), bf16[8,96,256]{2,1,0:T(8,128)(2,1)S(1)}, u32[]{:S(2)}, u32[]{:S(2)}) async-start(bf16[8,96,256]{2,1,0:T(8,128)(2,1)} %bitcast.16), calls=%async_computation.3 | async-start | bytes 786432 | tf_op jit(solution)/shard_map/all_to_all | solution.py:192
  114.7 0.1 slice_bitcast_fusion
  114.8 0.9 copy.23
  115.8 0.9 copy.22
  116.7 6.0 %all-to-all-done.3 = bf16[8,96,256]{2,1,0:T(8,128)(2,1)S(1)} async-done(((bf16[8,96,256]{2,1,0:T(8,128)(2,1)}), bf16[8,96,256]{2,1,0:T(8,128)(2,1)S(1)}, u32[]{:S(2)}, u32[]{:S(2)}) %all-to-all-start.3) | async-done | bytes 393248 | tf_op jit(solution)/shard_map/all_to_all | solution.py:192
  122.7 0.1 slice_bitcast_fusion.3
  122.8 0.7 copy.32
  123.5 0.7 copy.33
  (7 shorter events, 0.1 us)
Async XLA Ops:
  0.6 0.9 copy-start
  0.6 8.5 %copy-start.2 = (bf16[96,4096]{1,0:T(8,128)(2,1)S(1)}, bf16[96,4096]{1,0:T(8,128)(2,1)}, u32[]{:S(2)}) copy-start(bf16[96,4096]{1,0:T(8,128)(2,1)} %param.9) | copy-start | bytes 2359300
  0.7 8.5 %copy-start.3 = (bf16[96,4096]{1,0:T(8,128)(2,1)S(1)}, bf16[96,4096]{1,0:T(8,128)(2,1)}, u32[]{:S(2)}) copy-start(bf16[96,4096]{1,0:T(8,128)(2,1)} %param.6) | copy-start | bytes 2359300
  3.4 14.0 %all-to-all-start.1 = ((bf16[8,96,256]{2,1,0:T(8,128)(2,1)}), bf16[8,96,256]{2,1,0:T(8,128)(2,1)}, u32[]{:S(2)}, u32[]{:S(2)}) async-start(bf16[8,96,256]{2,1,0:T(8,128)(2,1)} %maximum_bitcast_fusion.1), calls=%async_computation.1 | async-start | bytes 786432 | tf_op jit(solution)/shard_map/all_to_all | solution.py:192
  10.7 24.8 %copy-start.6 = (s32[768]{0:T(1024)S(1)}, s32[768]{0:T(1024)}, u32[]{:S(2)}) copy-start(s32[768]{0:T(1024)} %param.11) | copy-start | bytes 9220
  17.3 32.8 %all-to-all-start = ((bf16[8,96,1024]{2,1,0:T(8,128)(2,1)}), bf16[8,96,1024]{2,1,0:T(8,128)(2,1)S(1)}, u32[]{:S(2)}, u32[]{:S(2)}) async-start(bf16[8,96,1024]{2,1,0:T(8,128)(2,1)} %maximum_bitcast_fusion), calls=%async_computation | async-start | bytes 3145728 | tf_op jit(solution)/shard_map/all_to_all | solution.py:192
  22.6 5.7 %collective-permute-start.1 = (bf16[256,256]{1,0:T(8,128)(2,1)S(1)}, bf16[256,256]{1,0:T(8,128)(2,1)S(1)}, u32[]{:S(2)}, u32[]{:S(2)}) collective-permute-start(bf16[256,256]{1,0:T(8,128)(2,1)S(1)} %get-tuple-element.27), channel_id=1, source_target_pairs={{0,16},{1,65},{2,18},{3,67},{4,20},{5,69},{6,22},{7,71},{8,24},{9,... | collective-permute-start | bytes 393224 | tf_op jit(solution)/shard_map/ppermute | solution.py:42
  25.6 5.0 %collective-permute-start = (bf16[256,256]{1,0:T(8,128)(2,1)S(1)}, bf16[256,256]{1,0:T(8,128)(2,1)S(1)}, u32[]{:S(2)}, u32[]{:S(2)}) collective-permute-start(bf16[256,256]{1,0:T(8,128)(2,1)S(1)} %get-tuple-element.27), channel_id=1, source_target_pairs={{0,8},{1,33},{2,10},{3,35},{4,12},{5,37},{6,14},{7,39},{8,16},{9,4... | collective-permute-start | bytes 393224 | tf_op jit(solution)/shard_map/ppermute | solution.py:42
  26.0 4.6 %collective-permute-start.2 = (bf16[256,256]{1,0:T(8,128)(2,1)S(1)}, bf16[256,256]{1,0:T(8,128)(2,1)S(1)}, u32[]{:S(2)}, u32[]{:S(2)}) collective-permute-start(bf16[256,256]{1,0:T(8,128)(2,1)S(1)} %get-tuple-element.27), channel_id=1, source_target_pairs={{0,24},{1,97},{2,26},{3,99},{4,28},{5,101},{6,30},{7,103},{8,0},{9... | collective-permute-start | bytes 393224 | tf_op jit(solution)/shard_map/ppermute | solution.py:42
  30.7 19.4 %copy-start.4 = (bf16[4,256,256]{2,1,0:T(8,128)(2,1)}, bf16[4,256,256]{2,1,0:T(8,128)(2,1)S(1)}, u32[]{:S(2)}) copy-start(bf16[4,256,256]{2,1,0:T(8,128)(2,1)S(1)} %pad_maximum_fusion.a0) | copy-start | bytes 1572868
  30.7 15.9 %collective-permute-start.5 = (bf16[4,256,256]{2,1,0:T(8,128)(2,1)S(1)}, bf16[4,256,256]{2,1,0:T(8,128)(2,1)S(1)}, u32[]{:S(2)}, u32[]{:S(2)}) collective-permute-start(bf16[4,256,256]{2,1,0:T(8,128)(2,1)S(1)} %pad_maximum_fusion.a0), channel_id=1, source_target_pairs={{0,96},{1,25},{2,98},{3,27},{4,100},{5,29},{6,102},{7,31},{8,104},... | collective-permute-start | bytes 1572872 | tf_op jit(solution)/shard_map/ppermute | solution.py:42
  34.9 11.7 %collective-permute-start.4 = (bf16[4,256,256]{2,1,0:T(8,128)(2,1)S(1)}, bf16[4,256,256]{2,1,0:T(8,128)(2,1)S(1)}, u32[]{:S(2)}, u32[]{:S(2)}) collective-permute-start(bf16[4,256,256]{2,1,0:T(8,128)(2,1)S(1)} %pad_maximum_fusion.a0), channel_id=1, source_target_pairs={{0,64},{1,17},{2,66},{3,19},{4,68},{5,21},{6,70},{7,23},{8,72},{9,... | collective-permute-start | bytes 1572872 | tf_op jit(solution)/shard_map/ppermute | solution.py:42
  34.9 15.3 %collective-permute-start.3 = (bf16[4,256,256]{2,1,0:T(8,128)(2,1)S(1)}, bf16[4,256,256]{2,1,0:T(8,128)(2,1)}, u32[]{:S(2)}, u32[]{:S(2)}) collective-permute-start(bf16[4,256,256]{2,1,0:T(8,128)(2,1)S(1)} %pad_maximum_fusion.a0), channel_id=1, source_target_pairs={{0,32},{1,9},{2,34},{3,11},{4,36},{5,13},{6,38},{7,15},{8,40},{9,1... | collective-permute-start | bytes 1572872 | tf_op jit(solution)/shard_map/ppermute | solution.py:42
  46.6 3.5 %copy-start.7 = (bf16[4,256,256]{2,1,0:T(8,128)(2,1)}, bf16[4,256,256]{2,1,0:T(8,128)(2,1)S(1)}, u32[]{:S(2)}) copy-start(bf16[4,256,256]{2,1,0:T(8,128)(2,1)S(1)} %collective-permute-done.5.a3) | copy-start | bytes 1572868
  46.6 3.5 %copy-start.8 = (bf16[4,256,256]{2,1,0:T(8,128)(2,1)}, bf16[4,256,256]{2,1,0:T(8,128)(2,1)S(1)}, u32[]{:S(2)}) copy-start(bf16[4,256,256]{2,1,0:T(8,128)(2,1)S(1)} %collective-permute-done.4.a2) | copy-start | bytes 1572868
  50.1 1.2 copy-start.1
  79.2 15.4 %collective-permute-start.6 = (bf16[4,256,256]{2,1,0:T(8,128)(2,1)}, bf16[4,256,256]{2,1,0:T(8,128)(2,1)S(1)}, u32[]{:S(2)}, u32[]{:S(2)}) collective-permute-start(bf16[4,256,256]{2,1,0:T(8,128)(2,1)} %get-tuple-element.16), channel_id=1, source_target_pairs={{0,32},{1,9},{2,34},{3,11},{4,36},{5,13},{6,38},{7,15},{8,40},{9,1... | collective-permute-start | bytes 1572872 | tf_op jit(solution)/shard_map/ppermute | solution.py:42
  79.2 15.4 %collective-permute-start.8 = (bf16[4,256,256]{2,1,0:T(8,128)(2,1)}, bf16[4,256,256]{2,1,0:T(8,128)(2,1)S(1)}, u32[]{:S(2)}, u32[]{:S(2)}) collective-permute-start(bf16[4,256,256]{2,1,0:T(8,128)(2,1)} %get-tuple-element.17), channel_id=1, source_target_pairs={{0,96},{1,25},{2,98},{3,27},{4,100},{5,29},{6,102},{7,31},{8,104},... | collective-permute-start | bytes 1572872 | tf_op jit(solution)/shard_map/ppermute | solution.py:42
  81.8 12.7 %collective-permute-start.7 = (bf16[4,256,256]{2,1,0:T(8,128)(2,1)}, bf16[4,256,256]{2,1,0:T(8,128)(2,1)S(1)}, u32[]{:S(2)}, u32[]{:S(2)}) collective-permute-start(bf16[4,256,256]{2,1,0:T(8,128)(2,1)} %get-tuple-element.18), channel_id=1, source_target_pairs={{0,64},{1,17},{2,66},{3,19},{4,68},{5,21},{6,70},{7,23},{8,72},{9,... | collective-permute-start | bytes 1572872 | tf_op jit(solution)/shard_map/ppermute | solution.py:42
  81.8 28.3 %all-to-all-start.2 = ((bf16[8,96,1024]{2,1,0:T(8,128)(2,1)}), bf16[8,96,1024]{2,1,0:T(8,128)(2,1)S(1)}, u32[]{:S(2)}, u32[]{:S(2)}) async-start(bf16[8,96,1024]{2,1,0:T(8,128)(2,1)} %bitcast.10), calls=%async_computation.2 | async-start | bytes 3145728 | tf_op jit(solution)/shard_map/all_to_all | solution.py:192
  89.4 10.2 %copy-start.5 = (f32[768,256]{1,0:T(8,128)S(1)}, f32[768,256]{1,0:T(8,128)}, u32[]{:S(2)}) copy-start(f32[768,256]{1,0:T(8,128)} %get-tuple-element.10) | copy-start | bytes 2359300
  95.9 5.4 %collective-permute-start.9 = (bf16[256,256]{1,0:T(8,128)(2,1)S(1)}, bf16[256,256]{1,0:T(8,128)(2,1)S(1)}, u32[]{:S(2)}, u32[]{:S(2)}) collective-permute-start(bf16[256,256]{1,0:T(8,128)(2,1)S(1)} %get-tuple-element.21), channel_id=1, source_target_pairs={{0,8},{1,33},{2,10},{3,35},{4,12},{5,37},{6,14},{7,39},{8,16},{9,4... | collective-permute-start | bytes 393224 | tf_op jit(solution)/shard_map/ppermute | solution.py:42
  96.1 5.2 %collective-permute-start.11 = (bf16[256,256]{1,0:T(8,128)(2,1)S(1)}, bf16[256,256]{1,0:T(8,128)(2,1)S(1)}, u32[]{:S(2)}, u32[]{:S(2)}) collective-permute-start(bf16[256,256]{1,0:T(8,128)(2,1)S(1)} %get-tuple-element.22), channel_id=1, source_target_pairs={{0,24},{1,97},{2,26},{3,99},{4,28},{5,101},{6,30},{7,103},{8,0},{9... | collective-permute-start | bytes 393224 | tf_op jit(solution)/shard_map/ppermute | solution.py:42
  98.7 5.3 %collective-permute-start.10 = (bf16[256,256]{1,0:T(8,128)(2,1)S(1)}, bf16[256,256]{1,0:T(8,128)(2,1)S(1)}, u32[]{:S(2)}, u32[]{:S(2)}) collective-permute-start(bf16[256,256]{1,0:T(8,128)(2,1)S(1)} %get-tuple-element.23), channel_id=1, source_target_pairs={{0,16},{1,65},{2,18},{3,67},{4,20},{5,69},{6,22},{7,71},{8,24},{9,... | collective-permute-start | bytes 393224 | tf_op jit(solution)/shard_map/ppermute | solution.py:42
  110.1 12.6 %all-to-all-start.3 = ((bf16[8,96,256]{2,1,0:T(8,128)(2,1)}), bf16[8,96,256]{2,1,0:T(8,128)(2,1)S(1)}, u32[]{:S(2)}, u32[]{:S(2)}) async-start(bf16[8,96,256]{2,1,0:T(8,128)(2,1)} %bitcast.16), calls=%async_computation.3 | async-start | bytes 786432 | tf_op jit(solution)/shard_map/all_to_all | solution.py:192

commit v3 on v2

--- a/solution.py
+++ b/solution.py
@@ -51,10 +51,11 @@
 
 def attention_kernel(
     nb, here, parent, q_ref, g_ref, kv_ref, a0, a1, a2, a3, end_ref,
-    out_ref, dkv_ref, terms_ref, ks, vs, dks, dvs, bias,
+    out_ref, dkv_ref, t0, t1, t2, t3, ks, vs, dks, dvs, bias,
 ):
     h = pl.program_id(0)
     nr = DMAX * BLK
+    term_refs = (t0, t1, t2, t3)
     found = []
     current = here[0] * nb
     for _ in range(DMAX):
@@ -82,13 +83,18 @@
             ok = (p <= i) & (i <= end_ref[b : b + 1, :])
             bias[b] = jnp.where(ok, 0.0, -1e30)
 
-    for b in range(nb):
-        rows = pl.ds(b * BLK, BLK)
-        q = q_ref[rows, :]
-        g = g_ref[rows, :]
-        nk = nr + (b + 1) * BLK
-        scores = dot(q, ks[:nk, :], 1, 1)
-        parts = [scores[:, j * BLK : (j + 1) * BLK] for j in range(DMAX + b + 1)]
+    def width(b):
+        return nr + (b + 1) * BLK
+
+    def block(ref, b):
+        return ref[b * BLK : (b + 1) * BLK, :]
+
+    def chunk(x, j):
+        return x[:, j * BLK : (j + 1) * BLK]
+
+    def scores(b):
+        s = dot(block(q_ref, b), ks[: width(b), :], 1, 1)
+        parts = [chunk(s, j) for j in range(DMAX + b + 1)]
         parts[-1] = parts[-1] + bias[b]
         peak = None
         for j, x in enumerate(parts):
@@ -96,6 +102,9 @@
             if j < DMAX:
                 t = jnp.where(found[j] >= 0, t, -3e38)
             peak = t if peak is None else jnp.maximum(peak, t)
+        return parts, peak
+
+    def softmax(b, parts, peak):
         peak = jnp.max(peak, axis=1, keepdims=True)
         weights = []
         total = None
@@ -105,45 +114,73 @@
             t = w[:, :HD] + w[:, HD:]
             total = t if total is None else total + t
             weights.append(w)
+        return weights, total, jnp.concatenate([w.astype(BF16) for w in weights], axis=1)
+
+    def attend(b, w_b, total):
         inv = 1.0 / jnp.sum(total, axis=1, keepdims=True)
-        w_b = jnp.concatenate([w.astype(BF16) for w in weights], axis=1)
-        out = dot(w_b, vs[:nk, :], 1, 0) * inv
-        out_ref[rows, pl.ds(pl.multiple_of(h * HD, HD), HD)] = out.astype(BF16)
-        g_b = (g.astype(F32) * inv).astype(BF16)
-        dot_out = jnp.sum(g_b.astype(F32) * out, axis=1, keepdims=True)
-        grad_probs = dot(g_b, vs[:nk, :], 1, 1)
-        grad_scores = jnp.concatenate(
-            [
-                (weights[j] * (grad_probs[:, j * BLK : (j + 1) * BLK] - dot_out)).astype(BF16)
-                for j in range(DMAX + b + 1)
-            ],
-            axis=1,
-        )
-        dq = (dot(grad_scores, ks[:nk, :], 1, 0) * SCALE).astype(BF16)
-        out_ref[rows, pl.ds(pl.multiple_of((GROUP + h) * HD, HD), HD)] = dq
-        dks[:nk, :] += dot(grad_scores, q, 0, 0)
-        dvs[:nk, :] += dot(w_b, g_b, 0, 0)
+        out = dot(w_b, vs[: width(b), :], 1, 0) * inv
+        at = pl.ds(pl.multiple_of(h * HD, HD), HD)
+        out_ref[b * BLK : (b + 1) * BLK, at] = out.astype(BF16)
+        g_b = (block(g_ref, b).astype(F32) * inv).astype(BF16)
+        return g_b, jnp.sum(g_b.astype(F32) * out, axis=1, keepdims=True)
+
+    def grad_probs(b, g_b):
+        return dot(g_b, vs[: width(b), :], 1, 1)
+
+    def grad_scores(b, weights, grad_p, dot_out):
+        each = [
+            (weights[j] * (chunk(grad_p, j) - dot_out)).astype(BF16) for j in range(DMAX + b + 1)
+        ]
+        return jnp.concatenate(each, axis=1)
+
+    def grads(b, grad_s, w_b, g_b):
+        at = pl.ds(pl.multiple_of((GROUP + h) * HD, HD), HD)
+        dq = dot(grad_s, ks[: width(b), :], 1, 0) * SCALE
+        out_ref[b * BLK : (b + 1) * BLK, at] = dq.astype(BF16)
+        dks[:, : width(b)] += dot(block(q_ref, b).T, grad_s, 1, 0)
+        dvs[:, : width(b)] += dot(g_b.T, w_b, 1, 0)
+
+    s, w, o, d, t = {}, {}, {}, {}, {}
+    for step in range(nb + 3):
+        b = step
+        if b == 0:
+            s[b] = scores(b)
+        if b < nb:
+            w[b] = softmax(b, *s.pop(b))
+        if b + 1 < nb:
+            s[b + 1] = scores(b + 1)
+        if 0 <= b - 1 < nb:
+            t[b - 1] = grad_scores(b - 1, w[b - 1][0], d.pop(b - 1), o[b - 1][1])
+        if b < nb:
+            o[b] = attend(b, w[b][2], w[b][1])
+        if 0 <= b - 1 < nb:
+            grads(b - 1, t.pop(b - 1), w[b - 1][2], o[b - 1][0])
+        if b < nb:
+            d[b] = grad_probs(b, o[b][0])
 
     @pl.when(h == GROUP - 1)
     def _():
-        dkv_ref[:, :HD] = dks[nr:, :] * SCALE
-        dkv_ref[:, HD:] = dvs[nr:, :]
-        terms_ref[...] = jnp.zeros_like(terms_ref)
+        dk = dks[...].T * SCALE
+        dv = dvs[...].T
+        dkv_ref[:, :HD] = dk[nr:, :]
+        dkv_ref[:, HD:] = dv[nr:, :]
+        for r in term_refs:
+            r[...] = jnp.zeros_like(r)
         for j in range(DMAX):
-
-            @pl.when(found[j] >= 0)
-            def _():
-                second, first = offsets(here, found[j] // nb)
-                at = (SIDE - second) % SIDE * SIDE + (SIDE - first) % SIDE
-                terms_ref[at, :, :HD] = (dks[j * BLK : (j + 1) * BLK, :] * SCALE).astype(BF16)
-                terms_ref[at, :, HD:] = dvs[j * BLK : (j + 1) * BLK, :].astype(BF16)
+            second, first = offsets(here, jnp.maximum(found[j], 0) // nb)
+            for s, r in enumerate(term_refs):
+
+                @pl.when((found[j] >= 0) & ((SIDE - second) % SIDE == s))
+                def _():
+                    at = (SIDE - first) % SIDE
+                    r[at, :, :HD] = dk[j * BLK : (j + 1) * BLK, :].astype(BF16)
+                    r[at, :, HD:] = dv[j * BLK : (j + 1) * BLK, :].astype(BF16)
 
 
 def attention(here, parent, qg, kv, arrived, ends):
     span = qg.shape[0]
     nb = span // BLK
     keys = (DMAX + nb) * BLK
-    n_ctx = SIDE * SIDE
 
     def whole(*shape):
         return pl.BlockSpec(shape, lambda h, here, parent: (0,) * len(shape))
@@ -161,13 +198,13 @@
         out_specs=[
             whole(span, 2 * GROUP * HD),
             whole(span, 2 * HD),
-            whole(n_ctx, BLK, 2 * HD),
-        ],
+        ]
+        + [whole(SIDE, BLK, 2 * HD)] * SIDE,
         scratch_shapes=[
             pltpu.VMEM((keys, HD), BF16),
             pltpu.VMEM((keys, HD), BF16),
-            pltpu.VMEM((keys, HD), F32),
-            pltpu.VMEM((keys, HD), F32),
+            pltpu.VMEM((HD, keys), F32),
+            pltpu.VMEM((HD, keys), F32),
             pltpu.VMEM((nb, BLK, BLK), F32),
         ],
     )
@@ -178,8 +215,8 @@
         out_shape=[
             jax.ShapeDtypeStruct(qg.shape, BF16),
             jax.ShapeDtypeStruct((span, 2 * HD), F32),
-            jax.ShapeDtypeStruct((n_ctx, BLK, 2 * HD), BF16),
-        ],
+        ]
+        + [jax.ShapeDtypeStruct((SIDE, BLK, 2 * HD), BF16)] * SIDE,
         compiler_params=pltpu.CompilerParams(vmem_limit_bytes=56 * 2**20),
         cost_estimate=pl.CostEstimate(
             flops=12 * pairs * HD, bytes_accessed=8 * span * 4 * HD, transcendentals=pairs
@@ -208,7 +245,7 @@
     line = jnp.stack([first] + [shifted(first, 1, s) for s in range(1, SIDE)])
     arrived = [line] + [shifted(line, 0, s) for s in range(1, SIDE)]
     qg = by_head(queries, grad_out)
-    out, dkv, terms = attention(here, parent, qg, kv, arrived, subtree_end.reshape(nb, BLK))
+    out, dkv, *terms = attention(here, parent, qg, kv, arrived, subtree_end.reshape(nb, BLK))
 
     def send_back(x):
         return swap(x.reshape(n_head, rows, -1))
@@ -218,7 +255,6 @@
 
     out = send_back(out)
 
-    terms = terms.reshape(SIDE, SIDE, BLK, 2 * HD)
     part = terms[0].astype(F32)
     for s in range(1, SIDE):
         part = part + shifted(terms[s], 0, s).astype(F32)

time: 125 us -> 119 us (0.952)
  Pallas kernels: 25.3 us -> 21.1 us
  local copies, waits for them, and re-layouts: 10.9 us -> 8.36 us
    pallas_call x1, Pallas kernels: 25.3 us -> 21.1 us  [attention(): pl.pallas_call(functools.partial(attention_kernel, nb), grid_spec=spec, o...]
    slice x1 -> x0, local copies, waits for them, and re-layouts: 2.54 us -> none  [local(): part = part + shifted(terms[s], 0, s).astype(F32)]
  transfers between devices with their start and end apart: 16 -> 16, of which waited for: 9 -> 10; matrix products, arithmetic and copies ran while one was open for 6% -> 7% of each run, Pallas kernels for 0% -> 0%
where the time goes in v3:
time: 119 us
  waiting for transfers between devices  43.1 us (36%)
  starting transfers between devices  40.1 us (34%)
  Pallas kernels  21.1 us (18%)
  local copies, waits for them, and re-layouts  8.36 us (7%)
  other arithmetic  5.13 us (4%)
    ppermute x12, waiting for transfers between devices, shifted(): return lax.ppermute(x, ('ctx', 'head'), pairs)  25.7 us
    all_to_all x4, starting transfers between devices, swap(): return lax.all_to_all(x, 'head', split_axis=0, concat_axis=0, tiled=True)  23.3 us
    pallas_call x1, Pallas kernels, attention(): pl.pallas_call(functools.partial(attention_kernel, nb), grid_spec=spec, o...  21.1 us
    all_to_all x4, waiting for transfers between devices, swap(): return lax.all_to_all(x, 'head', split_axis=0, concat_axis=0, tiled=True)  17.4 us
    ppermute x12, starting transfers between devices, shifted(): return lax.ppermute(x, ('ctx', 'head'), pairs)  16.8 us
    reshape x4, local copies, waits for them, and re-layouts, by_token(): a.reshape(rows, -1)  3.34 us
  transfers between devices with their start and end apart: 16, of which 10 were waited for; matrix products, arithmetic and copies ran while one was open for 7% of the time, Pallas kernels for 0%

profile of v3, /device:TPU:1, one launch (start us, length us, event | category | flops | bytes accessed | tf_op | source)
XLA Modules:
  0.0 118.5 jit_solution(14262642100458821491)
XLA Ops:
  0.6 0.0 copy-start
  0.6 0.0 copy-start.2
  0.7 0.0 copy-start.3
  0.7 0.9 copy-done
  1.6 1.0 copy_bitcast_fusion.4
  2.6 0.8 maximum_bitcast_fusion.1
  3.4 5.8 %all-to-all-start.1 = ((bf16[8,96,256]{2,1,0:T(8,128)(2,1)}), bf16[8,96,256]{2,1,0:T(8,128)(2,1)}, u32[]{:S(2)}, u32[]{:S(2)}) async-start(bf16[8,96,256]{2,1,0:T(8,128)(2,1)} %maximum_bitcast_fusion.1), calls=%async_computation.1 | async-start | bytes 786432 | tf_op jit(solution)/shard_map/all_to_all | solution.py:229
  9.2 0.0 copy-done.2
  9.2 0.0 copy-done.3
  9.2 0.2 copy_bitcast_fusion
  9.3 1.4 %maximum_bitcast_fusion = bf16[8,96,1024]{2,1,0:T(8,128)(2,1)} fusion(bf16[96,8,512]{2,0,1:T(8,128)(2,1)S(1)} %get-tuple-element.31, bf16[96,8,512]{2,0,1:T(8,128)(2,1)S(1)} %get-tuple-element.32), kind=kLoop, calls=%fused_computation | loop fusion | flops 3145728 | bytes 3145728 | tf_op jit(solution)/shard_map/transpose | solution.py:241
  10.7 6.6 %all-to-all-done.1 = bf16[8,96,256]{2,1,0:T(8,128)(2,1)} async-done(((bf16[8,96,256]{2,1,0:T(8,128)(2,1)}), bf16[8,96,256]{2,1,0:T(8,128)(2,1)}, u32[]{:S(2)}, u32[]{:S(2)}) %all-to-all-start.1) | async-done | bytes 393248 | tf_op jit(solution)/shard_map/all_to_all | solution.py:229
  17.3 4.4 %all-to-all-start = ((bf16[8,96,1024]{2,1,0:T(8,128)(2,1)}), bf16[8,96,1024]{2,1,0:T(8,128)(2,1)S(1)}, u32[]{:S(2)}, u32[]{:S(2)}) async-start(bf16[8,96,1024]{2,1,0:T(8,128)(2,1)} %maximum_bitcast_fusion), calls=%async_computation | async-start | bytes 3145728 | tf_op jit(solution)/shard_map/all_to_all | solution.py:229
  21.7 0.9 slice_bitcast_fusion.8
  22.6 3.0 %collective-permute-start.1 = (bf16[256,256]{1,0:T(8,128)(2,1)S(1)}, bf16[256,256]{1,0:T(8,128)(2,1)S(1)}, u32[]{:S(2)}, u32[]{:S(2)}) collective-permute-start(bf16[256,256]{1,0:T(8,128)(2,1)S(1)} %get-tuple-element.30), channel_id=1, source_target_pairs={{0,16},{1,65},{2,18},{3,67},{4,20},{5,69},{6,22},{7,71},{8,24},{9,... | collective-permute-start | bytes 393224 | tf_op jit(solution)/shard_map/ppermute | solution.py:42
  25.6 0.4 collective-permute-start
  26.0 2.3 %collective-permute-start.2 = (bf16[256,256]{1,0:T(8,128)(2,1)S(1)}, bf16[256,256]{1,0:T(8,128)(2,1)S(1)}, u32[]{:S(2)}, u32[]{:S(2)}) collective-permute-start(bf16[256,256]{1,0:T(8,128)(2,1)S(1)} %get-tuple-element.30), channel_id=1, source_target_pairs={{0,24},{1,97},{2,26},{3,99},{4,28},{5,101},{6,30},{7,103},{8,0},{9... | collective-permute-start | bytes 393224 | tf_op jit(solution)/shard_map/ppermute | solution.py:42
  28.3 0.0 collective-permute-done.1
  28.3 2.3 %collective-permute-done = bf16[256,256]{1,0:T(8,128)(2,1)S(1)} collective-permute-done((bf16[256,256]{1,0:T(8,128)(2,1)S(1)}, bf16[256,256]{1,0:T(8,128)(2,1)S(1)}, u32[]{:S(2)}, u32[]{:S(2)}) %collective-permute-start) | collective-permute-done | bytes 131104 | tf_op jit(solution)/shard_map/ppermute | solution.py:42
  30.6 0.0 collective-permute-done.2
  30.6 0.1 pad_maximum_fusion.a0
  30.7 0.0 copy-start.5
  30.7 4.1 %collective-permute-start.5 = (bf16[4,256,256]{2,1,0:T(8,128)(2,1)S(1)}, bf16[4,256,256]{2,1,0:T(8,128)(2,1)S(1)}, u32[]{:S(2)}, u32[]{:S(2)}) collective-permute-start(bf16[4,256,256]{2,1,0:T(8,128)(2,1)S(1)} %pad_maximum_fusion.a0), channel_id=1, source_target_pairs={{0,96},{1,25},{2,98},{3,27},{4,100},{5,29},{6,102},{7,31},{8,104},... | collective-permute-start | bytes 1572872 | tf_op jit(solution)/shard_map/ppermute | solution.py:42
  34.9 0.0 collective-permute-start.4
  34.9 0.7 collective-permute-start.3
  35.5 0.0 copy-done.7
  35.5 0.6 reshape.53.end_ref
  36.1 0.6 pad_add_fusion.here
  36.7 9.9 %collective-permute-done.5.a3 = bf16[4,256,256]{2,1,0:T(8,128)(2,1)S(1)} collective-permute-done((bf16[4,256,256]{2,1,0:T(8,128)(2,1)S(1)}, bf16[4,256,256]{2,1,0:T(8,128)(2,1)S(1)}, u32[]{:S(2)}, u32[]{:S(2)}) %collective-permute-start.5) | collective-permute-done | bytes 524320 | tf_op jit(solution)/shard_map/ppermute | solution.py:42
  46.6 0.0 collective-permute-done.4.a2
  46.6 3.5 %collective-permute-done.3.a1 = bf16[4,256,256]{2,1,0:T(8,128)(2,1)} collective-permute-done((bf16[4,256,256]{2,1,0:T(8,128)(2,1)S(1)}, bf16[4,256,256]{2,1,0:T(8,128)(2,1)}, u32[]{:S(2)}, u32[]{:S(2)}) %collective-permute-start.3) | collective-permute-done | bytes 524320 | tf_op jit(solution)/shard_map/ppermute | solution.py:42
  50.1 0.0 all-to-all-done
  50.1 0.0 copy-done.5
  50.1 0.0 copy-done.8
  50.1 0.0 copy-done.9
  50.1 1.1 copy-done.1
  51.3 21.1 %tree_attention.1 = (bf16[768,1024]{1,0:T(8,128)(2,1)}, f32[768,256]{1,0:T(8,128)}, bf16[4,256,256]{2,1,0:T(8,128)(2,1)}, bf16[4,256,256]{2,1,0:T(8,128)(2,1)}, ...) custom-call(s32[2]{0:T(128)} %pad_add_fusion.here, s32[48]{0:T(128)} %parent.1, bf16[768,1024]{1,0:T(8,128)(2,1)} %bitcast.68, ...), custom_call_target="tpu_custom_call" | custom-call | flops 7247757312 | bytes 3145728 | tf_op jit(solution)/shard_map/tree_attention/pallas_call | solution.py:212
  72.4 0.0 collective-permute-start.6
  72.4 1.9 %collective-permute-start.7 = (bf16[4,256,256]{2,1,0:T(8,128)(2,1)}, bf16[4,256,256]{2,1,0:T(8,128)(2,1)S(1)}, u32[]{:S(2)}, u32[]{:S(2)}) collective-permute-start(bf16[4,256,256]{2,1,0:T(8,128)(2,1)} %get-tuple-element.16), channel_id=1, source_target_pairs={{0,64},{1,17},{2,66},{3,19},{4,68},{5,21},{6,70},{7,23},{8,72},{9,... | collective-permute-start | bytes 1572872 | tf_op jit(solution)/shard_map/ppermute | solution.py:42
  74.3 0.8 collective-permute-start.8
  75.1 7.8 %all-to-all-start.2 = ((bf16[8,96,1024]{2,1,0:T(8,128)(2,1)}), bf16[8,96,1024]{2,1,0:T(8,128)(2,1)S(1)}, u32[]{:S(2)}, u32[]{:S(2)}) async-start(bf16[8,96,1024]{2,1,0:T(8,128)(2,1)} %bitcast.70), calls=%async_computation.2 | async-start | bytes 3145728 | tf_op jit(solution)/shard_map/all_to_all | solution.py:229
  82.9 4.9 %collective-permute-done.6 = bf16[4,256,256]{2,1,0:T(8,128)(2,1)S(1)} collective-permute-done((bf16[4,256,256]{2,1,0:T(8,128)(2,1)}, bf16[4,256,256]{2,1,0:T(8,128)(2,1)S(1)}, u32[]{:S(2)}, u32[]{:S(2)}) %collective-permute-start.6) | collective-permute-done | bytes 524320 | tf_op jit(solution)/shard_map/ppermute | solution.py:42
  87.8 0.0 collective-permute-done.7
  87.8 0.7 collective-permute-done.8
  88.5 0.0 copy-done.4
  88.5 1.4 %fusion.5 = (bf16[4,256,256]{2,1,0:T(8,128)(2,1)S(1)}, f32[4,256,256]{2,1,0:T(8,128)S(1)}) fusion(bf16[4,256,256]{2,1,0:T(8,128)(2,1)} %collective-permute-done.8, bf16[4,256,256]{2,1,0:T(8,128)(2,1)S(1)} %collective-permute-done.7, bf16[4,256,256]{2,1,0:T(8,128)(2,1)S(1)} %collective-permute-done.6, bf16[4,256,256]{2,1,0:T(8,128)(2,1)S(1)} %copy-done.4), kind=kLoop, calls=%fused_computation.27 | loop fusion | flops 2097152 | bytes 3670016 | tf_op jit(solution)/shard_map/convert_element_type | solution.py:261
  90.0 0.1 collective-permute-start.9
  90.1 2.6 %collective-permute-start.11 = (bf16[256,256]{1,0:T(8,128)(2,1)S(1)}, bf16[256,256]{1,0:T(8,128)(2,1)S(1)}, u32[]{:S(2)}, u32[]{:S(2)}) collective-permute-start(bf16[256,256]{1,0:T(8,128)(2,1)S(1)} %get-tuple-element.25), channel_id=1, source_target_pairs={{0,24},{1,97},{2,26},{3,99},{4,28},{5,101},{6,30},{7,103},{8,0},{9... | collective-permute-start | bytes 393224 | tf_op jit(solution)/shard_map/ppermute | solution.py:42
  92.7 0.9 collective-permute-start.10
  93.6 0.0 copy-done.6
  93.7 1.7 %collective-permute-done.9 = bf16[256,256]{1,0:T(8,128)(2,1)S(1)} collective-permute-done((bf16[256,256]{1,0:T(8,128)(2,1)S(1)}, bf16[256,256]{1,0:T(8,128)(2,1)S(1)}, u32[]{:S(2)}, u32[]{:S(2)}) %collective-permute-start.9) | collective-permute-done | bytes 131104 | tf_op jit(solution)/shard_map/ppermute | solution.py:42
  95.4 0.0 collective-permute-done.11
  95.4 2.7 %collective-permute-done.10 = bf16[256,256]{1,0:T(8,128)(2,1)S(1)} collective-permute-done((bf16[256,256]{1,0:T(8,128)(2,1)S(1)}, bf16[256,256]{1,0:T(8,128)(2,1)S(1)}, u32[]{:S(2)}, u32[]{:S(2)}) %collective-permute-start.10) | collective-permute-done | bytes 131104 | tf_op jit(solution)/shard_map/ppermute | solution.py:42
  98.0 0.1 fusion.4
  98.1 0.8 pad_maximum_fusion.1
  98.9 4.7 %all-to-all-done.2 = bf16[8,96,1024]{2,1,0:T(8,128)(2,1)S(1)} async-done(((bf16[8,96,1024]{2,1,0:T(8,128)(2,1)}), bf16[8,96,1024]{2,1,0:T(8,128)(2,1)S(1)}, u32[]{:S(2)}, u32[]{:S(2)}) %all-to-all-start.2) | async-done | bytes 1572896 | tf_op jit(solution)/shard_map/all_to_all | solution.py:229
  103.6 5.3 %all-to-all-start.3 = ((bf16[8,96,256]{2,1,0:T(8,128)(2,1)}), bf16[8,96,256]{2,1,0:T(8,128)(2,1)S(1)}, u32[]{:S(2)}, u32[]{:S(2)}) async-start(bf16[8,96,256]{2,1,0:T(8,128)(2,1)} %bitcast.16), calls=%async_computation.3 | async-start | bytes 786432 | tf_op jit(solution)/shard_map/all_to_all | solution.py:229
  108.9 0.1 slice_bitcast_fusion
  109.1 0.9 copy.23
  110.0 0.9 copy.22
  111.0 6.0 %all-to-all-done.3 = bf16[8,96,256]{2,1,0:T(8,128)(2,1)S(1)} async-done(((bf16[8,96,256]{2,1,0:T(8,128)(2,1)}), bf16[8,96,256]{2,1,0:T(8,128)(2,1)S(1)}, u32[]{:S(2)}, u32[]{:S(2)}) %all-to-all-start.3) | async-done | bytes 393248 | tf_op jit(solution)/shard_map/all_to_all | solution.py:229
  117.0 0.1 slice_bitcast_fusion.3
  117.1 0.7 copy.32
  117.8 0.7 copy.33
  (8 shorter events, 0.1 us)
Async XLA Ops:
  0.6 0.9 copy-start
  0.6 8.5 %copy-start.2 = (bf16[96,4096]{1,0:T(8,128)(2,1)S(1)}, bf16[96,4096]{1,0:T(8,128)(2,1)}, u32[]{:S(2)}) copy-start(bf16[96,4096]{1,0:T(8,128)(2,1)} %param.9) | copy-start | bytes 2359300
  0.7 8.5 %copy-start.3 = (bf16[96,4096]{1,0:T(8,128)(2,1)S(1)}, bf16[96,4096]{1,0:T(8,128)(2,1)}, u32[]{:S(2)}) copy-start(bf16[96,4096]{1,0:T(8,128)(2,1)} %param.6) | copy-start | bytes 2359300
  3.4 14.0 %all-to-all-start.1 = ((bf16[8,96,256]{2,1,0:T(8,128)(2,1)}), bf16[8,96,256]{2,1,0:T(8,128)(2,1)}, u32[]{:S(2)}, u32[]{:S(2)}) async-start(bf16[8,96,256]{2,1,0:T(8,128)(2,1)} %maximum_bitcast_fusion.1), calls=%async_computation.1 | async-start | bytes 786432 | tf_op jit(solution)/shard_map/all_to_all | solution.py:229
  10.7 24.8 %copy-start.7 = (s32[768]{0:T(1024)S(1)}, s32[768]{0:T(1024)}, u32[]{:S(2)}) copy-start(s32[768]{0:T(1024)} %param.11) | copy-start | bytes 9220
  17.3 32.8 %all-to-all-start = ((bf16[8,96,1024]{2,1,0:T(8,128)(2,1)}), bf16[8,96,1024]{2,1,0:T(8,128)(2,1)S(1)}, u32[]{:S(2)}, u32[]{:S(2)}) async-start(bf16[8,96,1024]{2,1,0:T(8,128)(2,1)} %maximum_bitcast_fusion), calls=%async_computation | async-start | bytes 3145728 | tf_op jit(solution)/shard_map/all_to_all | solution.py:229
  22.6 5.7 %collective-permute-start.1 = (bf16[256,256]{1,0:T(8,128)(2,1)S(1)}, bf16[256,256]{1,0:T(8,128)(2,1)S(1)}, u32[]{:S(2)}, u32[]{:S(2)}) collective-permute-start(bf16[256,256]{1,0:T(8,128)(2,1)S(1)} %get-tuple-element.30), channel_id=1, source_target_pairs={{0,16},{1,65},{2,18},{3,67},{4,20},{5,69},{6,22},{7,71},{8,24},{9,... | collective-permute-start | bytes 393224 | tf_op jit(solution)/shard_map/ppermute | solution.py:42
  25.6 5.0 %collective-permute-start = (bf16[256,256]{1,0:T(8,128)(2,1)S(1)}, bf16[256,256]{1,0:T(8,128)(2,1)S(1)}, u32[]{:S(2)}, u32[]{:S(2)}) collective-permute-start(bf16[256,256]{1,0:T(8,128)(2,1)S(1)} %get-tuple-element.30), channel_id=1, source_target_pairs={{0,8},{1,33},{2,10},{3,35},{4,12},{5,37},{6,14},{7,39},{8,16},{9,4... | collective-permute-start | bytes 393224 | tf_op jit(solution)/shard_map/ppermute | solution.py:42
  26.0 4.6 %collective-permute-start.2 = (bf16[256,256]{1,0:T(8,128)(2,1)S(1)}, bf16[256,256]{1,0:T(8,128)(2,1)S(1)}, u32[]{:S(2)}, u32[]{:S(2)}) collective-permute-start(bf16[256,256]{1,0:T(8,128)(2,1)S(1)} %get-tuple-element.30), channel_id=1, source_target_pairs={{0,24},{1,97},{2,26},{3,99},{4,28},{5,101},{6,30},{7,103},{8,0},{9... | collective-permute-start | bytes 393224 | tf_op jit(solution)/shard_map/ppermute | solution.py:42
  30.7 19.4 %copy-start.5 = (bf16[4,256,256]{2,1,0:T(8,128)(2,1)}, bf16[4,256,256]{2,1,0:T(8,128)(2,1)S(1)}, u32[]{:S(2)}) copy-start(bf16[4,256,256]{2,1,0:T(8,128)(2,1)S(1)} %pad_maximum_fusion.a0) | copy-start | bytes 1572868
  30.7 15.9 %collective-permute-start.5 = (bf16[4,256,256]{2,1,0:T(8,128)(2,1)S(1)}, bf16[4,256,256]{2,1,0:T(8,128)(2,1)S(1)}, u32[]{:S(2)}, u32[]{:S(2)}) collective-permute-start(bf16[4,256,256]{2,1,0:T(8,128)(2,1)S(1)} %pad_maximum_fusion.a0), channel_id=1, source_target_pairs={{0,96},{1,25},{2,98},{3,27},{4,100},{5,29},{6,102},{7,31},{8,104},... | collective-permute-start | bytes 1572872 | tf_op jit(solution)/shard_map/ppermute | solution.py:42
  34.9 11.7 %collective-permute-start.4 = (bf16[4,256,256]{2,1,0:T(8,128)(2,1)S(1)}, bf16[4,256,256]{2,1,0:T(8,128)(2,1)S(1)}, u32[]{:S(2)}, u32[]{:S(2)}) collective-permute-start(bf16[4,256,256]{2,1,0:T(8,128)(2,1)S(1)} %pad_maximum_fusion.a0), channel_id=1, source_target_pairs={{0,64},{1,17},{2,66},{3,19},{4,68},{5,21},{6,70},{7,23},{8,72},{9,... | collective-permute-start | bytes 1572872 | tf_op jit(solution)/shard_map/ppermute | solution.py:42
  34.9 15.3 %collective-permute-start.3 = (bf16[4,256,256]{2,1,0:T(8,128)(2,1)S(1)}, bf16[4,256,256]{2,1,0:T(8,128)(2,1)}, u32[]{:S(2)}, u32[]{:S(2)}) collective-permute-start(bf16[4,256,256]{2,1,0:T(8,128)(2,1)S(1)} %pad_maximum_fusion.a0), channel_id=1, source_target_pairs={{0,32},{1,9},{2,34},{3,11},{4,36},{5,13},{6,38},{7,15},{8,40},{9,1... | collective-permute-start | bytes 1572872 | tf_op jit(solution)/shard_map/ppermute | solution.py:42
  46.6 3.5 %copy-start.8 = (bf16[4,256,256]{2,1,0:T(8,128)(2,1)}, bf16[4,256,256]{2,1,0:T(8,128)(2,1)S(1)}, u32[]{:S(2)}) copy-start(bf16[4,256,256]{2,1,0:T(8,128)(2,1)S(1)} %collective-permute-done.5.a3) | copy-start | bytes 1572868
  46.6 3.5 %copy-start.9 = (bf16[4,256,256]{2,1,0:T(8,128)(2,1)}, bf16[4,256,256]{2,1,0:T(8,128)(2,1)S(1)}, u32[]{:S(2)}) copy-start(bf16[4,256,256]{2,1,0:T(8,128)(2,1)S(1)} %collective-permute-done.4.a2) | copy-start | bytes 1572868
  50.1 1.2 copy-start.1
  72.4 15.4 %collective-permute-start.6 = (bf16[4,256,256]{2,1,0:T(8,128)(2,1)}, bf16[4,256,256]{2,1,0:T(8,128)(2,1)S(1)}, u32[]{:S(2)}, u32[]{:S(2)}) collective-permute-start(bf16[4,256,256]{2,1,0:T(8,128)(2,1)} %get-tuple-element.15), channel_id=1, source_target_pairs={{0,32},{1,9},{2,34},{3,11},{4,36},{5,13},{6,38},{7,15},{8,40},{9,1... | collective-permute-start | bytes 1572872 | tf_op jit(solution)/shard_map/ppermute | solution.py:42
  72.4 15.4 %collective-permute-start.7 = (bf16[4,256,256]{2,1,0:T(8,128)(2,1)}, bf16[4,256,256]{2,1,0:T(8,128)(2,1)S(1)}, u32[]{:S(2)}, u32[]{:S(2)}) collective-permute-start(bf16[4,256,256]{2,1,0:T(8,128)(2,1)} %get-tuple-element.16), channel_id=1, source_target_pairs={{0,64},{1,17},{2,66},{3,19},{4,68},{5,21},{6,70},{7,23},{8,72},{9,... | collective-permute-start | bytes 1572872 | tf_op jit(solution)/shard_map/ppermute | solution.py:42
  74.3 14.2 %collective-permute-start.8 = (bf16[4,256,256]{2,1,0:T(8,128)(2,1)}, bf16[4,256,256]{2,1,0:T(8,128)(2,1)}, u32[]{:S(2)}, u32[]{:S(2)}) collective-permute-start(bf16[4,256,256]{2,1,0:T(8,128)(2,1)} %get-tuple-element.17), channel_id=1, source_target_pairs={{0,96},{1,25},{2,98},{3,27},{4,100},{5,29},{6,102},{7,31},{8,104},... | collective-permute-start | bytes 1572872 | tf_op jit(solution)/shard_map/ppermute | solution.py:42
  75.1 13.4 %copy-start.4 = (bf16[4,256,256]{2,1,0:T(8,128)(2,1)S(1)}, bf16[4,256,256]{2,1,0:T(8,128)(2,1)}, u32[]{:S(2)}) copy-start(bf16[4,256,256]{2,1,0:T(8,128)(2,1)} %get-tuple-element.14) | copy-start | bytes 1572868
  75.1 28.5 %all-to-all-start.2 = ((bf16[8,96,1024]{2,1,0:T(8,128)(2,1)}), bf16[8,96,1024]{2,1,0:T(8,128)(2,1)S(1)}, u32[]{:S(2)}, u32[]{:S(2)}) async-start(bf16[8,96,1024]{2,1,0:T(8,128)(2,1)} %bitcast.70), calls=%async_computation.2 | async-start | bytes 3145728 | tf_op jit(solution)/shard_map/all_to_all | solution.py:229
  88.5 5.1 %copy-start.6 = (f32[768,256]{1,0:T(8,128)S(1)}, f32[768,256]{1,0:T(8,128)}, u32[]{:S(2)}) copy-start(f32[768,256]{1,0:T(8,128)} %get-tuple-element.13) | copy-start | bytes 2359300
  90.0 5.4 %collective-permute-start.9 = (bf16[256,256]{1,0:T(8,128)(2,1)S(1)}, bf16[256,256]{1,0:T(8,128)(2,1)S(1)}, u32[]{:S(2)}, u32[]{:S(2)}) collective-permute-start(bf16[256,256]{1,0:T(8,128)(2,1)S(1)} %get-tuple-element.24), channel_id=1, source_target_pairs={{0,8},{1,33},{2,10},{3,35},{4,12},{5,37},{6,14},{7,39},{8,16},{9,4... | collective-permute-start | bytes 393224 | tf_op jit(solution)/shard_map/ppermute | solution.py:42
  90.1 5.3 %collective-permute-start.11 = (bf16[256,256]{1,0:T(8,128)(2,1)S(1)}, bf16[256,256]{1,0:T(8,128)(2,1)S(1)}, u32[]{:S(2)}, u32[]{:S(2)}) collective-permute-start(bf16[256,256]{1,0:T(8,128)(2,1)S(1)} %get-tuple-element.25), channel_id=1, source_target_pairs={{0,24},{1,97},{2,26},{3,99},{4,28},{5,101},{6,30},{7,103},{8,0},{9... | collective-permute-start | bytes 393224 | tf_op jit(solution)/shard_map/ppermute | solution.py:42
  92.7 5.3 %collective-permute-start.10 = (bf16[256,256]{1,0:T(8,128)(2,1)S(1)}, bf16[256,256]{1,0:T(8,128)(2,1)S(1)}, u32[]{:S(2)}, u32[]{:S(2)}) collective-permute-start(bf16[256,256]{1,0:T(8,128)(2,1)S(1)} %get-tuple-element.26), channel_id=1, source_target_pairs={{0,16},{1,65},{2,18},{3,67},{4,20},{5,69},{6,22},{7,71},{8,24},{9,... | collective-permute-start | bytes 393224 | tf_op jit(solution)/shard_map/ppermute | solution.py:42
  103.6 13.4 %all-to-all-start.3 = ((bf16[8,96,256]{2,1,0:T(8,128)(2,1)}), bf16[8,96,256]{2,1,0:T(8,128)(2,1)S(1)}, u32[]{:S(2)}, u32[]{:S(2)}) async-start(bf16[8,96,256]{2,1,0:T(8,128)(2,1)} %bitcast.16), calls=%async_computation.3 | async-start | bytes 786432 | tf_op jit(solution)/shard_map/all_to_all | solution.py:229

commit v4 on v2

v4 whole, which is shorter than its diff:
```python
import functools

import jax
import jax.numpy as jnp
from jax import lax
from jax.experimental import pallas as pl
from jax.experimental.pallas import tpu as pltpu
from jax.sharding import PartitionSpec as P

HQ = 32
KVH = 8
HD = 128
BLK = 256
DMAX = 4
GROUP = HQ // KVH
SIDE = 4
SCALE = HD**-0.5
SCALE2 = SCALE * 1.4426950408889634
F32 = jnp.float32
BF16 = jnp.bfloat16


def dot(a, b, ca, cb):
    return lax.dot_general(a, b, (((ca,), (cb,)), ((), ())), preferred_element_type=F32)


def ring_pairs(side, cores, along, by):
    pairs = []
    for y in range(side):
        for z in range(side):
            for h in range(cores):
                if (along + h) % 2:
                    to = y * side + (z + by) % side
                else:
                    to = (y + by) % side * side + z
                pairs.append(((y * side + z) * cores + h, to * cores + h))
    return pairs


def shifted(x, along, by):
    pairs = ring_pairs(SIDE, lax.axis_size("head"), along, by)
    return lax.ppermute(x, ("ctx", "head"), pairs)


def offsets(here, device):
    dy = (here[0] // SIDE - device // SIDE) % SIDE
    dz = (here[0] % SIDE - device % SIDE) % SIDE
    odd = here[1] % 2 == 1
    return jnp.where(odd, dz, dy), jnp.where(odd, dy, dz)


def attention_kernel(
    nb, here, parent, end_ref, qg_ref, kv_ref, a0, a1, a2, a3,
    out_ref, dfirst_ref, drest_ref, t0, t1, t2, t3,
    ks, vs, dks, dvs, bias, held, outs, terms, dfirst, drest, blank,
    kv_sem, in_sem, fetch_sem, out_sem, blank_sem, term_sem, rest_sem,
):
    nr = DMAX * BLK
    arrived = (a0, a1, a2, a3)
    term_refs = (t0, t1, t2, t3)
    found = []
    current = here[0] * nb
    for _ in range(DMAX):
        current = jnp.where(current >= 0, parent[jnp.maximum(current, 0)], -1)
        found.append(current)
    places = [offsets(here, jnp.maximum(f, 0) // nb) for f in found]

    def kv_copy(which):
        to = (ks, vs)[which].at[nr:, :]
        return pltpu.make_async_copy(kv_ref.at[:, which * HD : (which + 1) * HD], to, kv_sem.at[which])

    def fetch(j, r, at, which):
        to = (ks, vs)[which].at[j * BLK : (j + 1) * BLK, :]
        src = r.at[at, :, which * HD : (which + 1) * HD]
        return pltpu.make_async_copy(src, to, fetch_sem.at[j, which])

    def head_in(h, which):
        src = qg_ref.at[:, (which * GROUP + h) * HD : (which * GROUP + h + 1) * HD]
        return pltpu.make_async_copy(src, held.at[h, which], in_sem.at[h, which])

    def head_out(h, which):
        at = pl.ds(pl.multiple_of((which * GROUP + h) * HD, HD), HD)
        return pltpu.make_async_copy(outs.at[h, which], out_ref.at[:, at], out_sem.at[h, which])

    def blank_copy(s, at):
        return pltpu.make_async_copy(blank, term_refs[s].at[at], blank_sem.at[s * SIDE + at])

    for which in range(2):
        kv_copy(which).start()
        for j, (second, first) in enumerate(places):
            for s, r in enumerate(arrived):

                @pl.when(second == s)
                def _():
                    fetch(j, r, first, which).start()

        head_in(0, which).start()
    for h in range(1, GROUP):
        for which in range(2):
            head_in(h, which).start()
    i = lax.broadcasted_iota(jnp.int32, (BLK, BLK), 0)
    p = lax.broadcasted_iota(jnp.int32, (BLK, BLK), 1)
    for b in range(nb):
        ok = (p <= i) & (i <= end_ref[b : b + 1, :])
        bias[b] = jnp.where(ok, 0.0, -1e30)
    dks[...] = jnp.zeros_like(dks)
    dvs[...] = jnp.zeros_like(dvs)
    blank[...] = jnp.zeros_like(blank)
    for s in range(SIDE):
        for at in range(SIDE):
            blank_copy(s, at).start()
    for which in range(2):
        kv_copy(which).wait()
        for j in range(DMAX):
            fetch(j, a0, 0, which).wait()

    def width(b):
        return nr + (b + 1) * BLK

    def chunk(x, j):
        return x[:, j * BLK : (j + 1) * BLK]

    def one_head(h, carry):
        for which in range(2):
            pltpu.make_async_copy(
                qg_ref.at[:, :HD], held.at[h, which], in_sem.at[h, which]
            ).wait()

        def load(which, b):
            return held[h, which, b * BLK : (b + 1) * BLK, :]

        def store(which, b, x):
            outs[h, which, b * BLK : (b + 1) * BLK, :] = x.astype(BF16)

        def scores(n):
            b = n
            s = dot(load(0, n), ks[: width(b), :], 1, 1)
            parts = [chunk(s, j) for j in range(DMAX + b + 1)]
            parts[-1] = parts[-1] + bias[b]
            peak = None
            for j, x in enumerate(parts):
                t = jnp.maximum(x[:, :HD], x[:, HD:])
                if j < DMAX:
                    t = jnp.where(found[j] >= 0, t, -3e38)
                peak = t if peak is None else jnp.maximum(peak, t)
            return parts, peak

        def softmax(parts, peak):
            peak = jnp.max(peak, axis=1, keepdims=True)
            weights = []
            total = None
            for j, x in enumerate(parts):
                shift = jnp.where(found[j] >= 0, peak, 1e30) if j < DMAX else peak
                w = jnp.exp2((x - shift) * SCALE2)
                t = w[:, :HD] + w[:, HD:]
                total = t if total is None else total + t
                weights.append(w.astype(BF16))
            return weights, total, jnp.concatenate(weights, axis=1)

        def attend(n, w_b, total):
            inv = 1.0 / jnp.sum(total, axis=1, keepdims=True)
            out = dot(w_b, vs[: width(n), :], 1, 0) * inv
            store(0, n, out)
            g_b = (load(1, n).astype(F32) * inv).astype(BF16)
            return g_b, jnp.sum(g_b.astype(F32) * out, axis=1, keepdims=True)

        def grad_probs(n, g_b):
            return dot(g_b, vs[: width(n), :], 1, 1)

        def grad_scores(weights, grad_p, dot_out):
            each = [w * (chunk(grad_p, j) - dot_out).astype(BF16) for j, w in enumerate(weights)]
            return jnp.concatenate(each, axis=1)

        def grads(n, grad_s, w_b, g_b):
            keys = width(n)
            store(1, n, dot(grad_s, ks[:keys, :], 1, 0) * SCALE)
            dks[:, :keys] += dot(load(0, n).T, grad_s, 1, 0)
            dvs[:, :keys] += dot(g_b.T, w_b, 1, 0)

        s, w, o, d, t = {}, {}, {}, {}, {}
        s[0] = scores(0)
        for n in range(nb + 1):
            if n < nb:
                w[n] = softmax(*s.pop(n))
            if n + 1 < nb:
                s[n + 1] = scores(n + 1)
            if n >= 1:
                t[n - 1] = grad_scores(w[n - 1][0], d.pop(n - 1), o[n - 1][1])
            if n < nb:
                o[n] = attend(n, w[n][2], w[n][1])
            if n >= 1:
                grads(n - 1, t.pop(n - 1), w.pop(n - 1)[2], o.pop(n - 1)[0])
            if n < nb:
                d[n] = grad_probs(n, o[n][0])
        for which in range(2):
            head_out(h, which).start()
        return carry

    lax.fori_loop(0, GROUP, one_head, 0)
    for s in range(SIDE):
        for at in range(SIDE):
            blank_copy(s, at).wait()
    dk = dks[:, :nr].T * SCALE
    dv = dvs[:, :nr].T
    for j, (second, first) in enumerate(places):
        terms[j, :, :HD] = dk[j * BLK : (j + 1) * BLK, :].astype(BF16)
        terms[j, :, HD:] = dv[j * BLK : (j + 1) * BLK, :].astype(BF16)
        for s, r in enumerate(term_refs):

            @pl.when((found[j] >= 0) & ((SIDE - second) % SIDE == s))
            def _():
                at = (SIDE - first) % SIDE
                pltpu.make_async_copy(terms.at[j], r.at[at], term_sem.at[j]).start()

    dk = dks[:, nr:].T * SCALE
    dv = dvs[:, nr:].T
    dfirst[:, :HD] = dk[:BLK, :]
    dfirst[:, HD:] = dv[:BLK, :]
    drest[:, :HD] = dk[BLK:, :].astype(BF16)
    drest[:, HD:] = dv[BLK:, :].astype(BF16)
    last = (
        pltpu.make_async_copy(dfirst, dfirst_ref, rest_sem.at[0]),
        pltpu.make_async_copy(drest, drest_ref, rest_sem.at[1]),
    )
    for c in last:
        c.start()
    for h in range(GROUP):
        for which in range(2):
            head_out(h, which).wait()
    for j in range(DMAX):

        @pl.when(found[j] >= 0)
        def _():
            pltpu.make_async_copy(terms.at[j], t0.at[0], term_sem.at[j]).wait()

    for c in last:
        c.wait()


def attention(here, parent, qg, kv, arrived, ends):
    span = qg.shape[0]
    nb = span // BLK
    keys = (DMAX + nb) * BLK

    anywhere = pl.BlockSpec(memory_space=pl.ANY)
    spec = pltpu.PrefetchScalarGridSpec(
        num_scalar_prefetch=2,
        grid=(),
        in_specs=[pl.BlockSpec(memory_space=pltpu.VMEM)] + [anywhere] * (2 + SIDE),
        out_specs=[anywhere] * (3 + SIDE),
        scratch_shapes=[
            pltpu.VMEM((keys, HD), BF16),
            pltpu.VMEM((keys, HD), BF16),
            pltpu.VMEM((HD, keys), F32),
            pltpu.VMEM((HD, keys), F32),
            pltpu.VMEM((nb, BLK, BLK), F32),
            pltpu.VMEM((GROUP, 2, span, HD), BF16),
            pltpu.VMEM((GROUP, 2, span, HD), BF16),
            pltpu.VMEM((DMAX, BLK, 2 * HD), BF16),
            pltpu.VMEM((BLK, 2 * HD), F32),
            pltpu.VMEM((span - BLK, 2 * HD), BF16),
            pltpu.VMEM((BLK, 2 * HD), BF16),
            pltpu.SemaphoreType.DMA((2,)),
            pltpu.SemaphoreType.DMA((GROUP, 2)),
            pltpu.SemaphoreType.DMA((DMAX, 2)),
            pltpu.SemaphoreType.DMA((GROUP, 2)),
            pltpu.SemaphoreType.DMA((SIDE * SIDE,)),
            pltpu.SemaphoreType.DMA((DMAX,)),
            pltpu.SemaphoreType.DMA((2,)),
        ],
    )
    pairs = GROUP * sum(DMAX + b + 1 for b in range(nb)) * BLK * BLK
    return pl.pallas_call(
        functools.partial(attention_kernel, nb),
        grid_spec=spec,
        out_shape=[
            jax.ShapeDtypeStruct(qg.shape, BF16),
            jax.ShapeDtypeStruct((BLK, 2 * HD), F32),
            jax.ShapeDtypeStruct((span - BLK, 2 * HD), BF16),
        ]
        + [jax.ShapeDtypeStruct((SIDE, BLK, 2 * HD), BF16)] * SIDE,
        compiler_params=pltpu.CompilerParams(vmem_limit_bytes=24 * 2**20),
        cost_estimate=pl.CostEstimate(
            flops=12 * pairs * HD, bytes_accessed=8 * span * 4 * HD, transcendentals=pairs
        ),
        name="tree_attention",
    )(here, parent, ends, qg, kv, *arrived)


def swap(x):
    return lax.all_to_all(x, "head", split_axis=0, concat_axis=0, tiled=True)


def local(queries, keys, values, grad_out, parent, subtree_end):
    n_head = lax.axis_size("head")
    here = jnp.stack([lax.axis_index("ctx"), lax.axis_index("head")]).astype(jnp.int32)
    rows = queries.shape[0]
    span = rows * n_head
    nb = span // BLK

    def by_head(x, y):
        both = [a.reshape(rows, n_head, -1) for a in (x, y)]
        return swap(jnp.concatenate(both, axis=2).transpose(1, 0, 2)).reshape(span, -1)

    kv = by_head(keys, values)
    first = kv[:BLK]
    line = jnp.stack([first] + [shifted(first, 1, s) for s in range(1, SIDE)])
    arrived = [line] + [shifted(line, 0, s) for s in range(1, SIDE)]
    qg = by_head(queries, grad_out)
    out, dfirst, drest, *terms = attention(here, parent, qg, kv, arrived, subtree_end.reshape(nb, BLK))

    def send_back(x):
        return swap(x.reshape(n_head, rows, -1))

    def by_token(x):
        return [a.reshape(rows, -1) for a in jnp.split(x.transpose(1, 0, 2), 2, axis=2)]

    out = send_back(out)

    got = [terms[0]] + [shifted(terms[s], 0, s) for s in range(1, SIDE)]
    summed = sum(x[0].astype(F32) for x in got)
    part = sum(x[1:].astype(F32) for x in got).astype(BF16)
    for s in range(1, SIDE):
        summed = summed + shifted(part[s - 1], 1, s).astype(F32)
    dkv = jnp.concatenate([(dfirst + summed).astype(BF16), drest], axis=0)
    out, dkv = lax.optimization_barrier((out, dkv))
    attn_out, grad_q = by_token(out)
    grad_k, grad_v = by_token(send_back(dkv))
    return attn_out, grad_q, grad_k, grad_v


def solution(mesh):
    placed = P(("ctx", "head"), None)
    return jax.shard_map(
        local,
        mesh=mesh,
        in_specs=(placed, placed, placed, placed, P(), P("ctx")),
        out_specs=(placed, placed, placed, placed),
        check_vma=False,
    )
```

time: 125 us -> 117 us (0.936)
  Pallas kernels: 25.3 us -> 17.9 us
  starting transfers between devices: 39.1 us -> 41.9 us
  local copies, waits for them, and re-layouts: 10.9 us -> 8.21 us
    pallas_call x1, Pallas kernels: 25.3 us -> 17.9 us  [attention(): pl.pallas_call(functools.partial(attention_kernel, nb), grid_spec=spec, o...]
    all_to_all x4, starting transfers between devices: 22.3 us -> 24.9 us  [swap(): return lax.all_to_all(x, 'head', split_axis=0, concat_axis=0, tiled=True)]
    slice x2 -> x0, local copies, waits for them, and re-layouts: 2.57 us -> none  [the longest x1 2.54 us: local(): part = part + shifted(terms[s], 0, s).astype(F32)]
    all_to_all x4, waiting for transfers between devices: 18 us -> 16.4 us  [swap(): return lax.all_to_all(x, 'head', split_axis=0, concat_axis=0, tiled=True)]
    unnamed x20, local copies, waits for them, and re-layouts: 2.3 us -> 3.66 us
  transfers between devices with their start and end apart: 16 -> 16, of which waited for: 9 -> 10; matrix products, arithmetic and copies ran while one was open for 6% -> 6% of each run, Pallas kernels for 0% -> 0%
where the time goes in v4:
time: 117 us; the launch traced here: 116 us
  waiting for transfers between devices  42.2 us (36%)
  starting transfers between devices  41.9 us (36%)
  Pallas kernels  17.9 us (15%)
  local copies, waits for them, and re-layouts  8.21 us (7%)
  other arithmetic  5.54 us (5%)
    ppermute x12, waiting for transfers between devices, shifted(): return lax.ppermute(x, ('ctx', 'head'), pairs)  25.8 us
    all_to_all x4, starting transfers between devices, swap(): return lax.all_to_all(x, 'head', split_axis=0, concat_axis=0, tiled=True)  24.9 us
    pallas_call x1, Pallas kernels, attention(): pl.pallas_call(functools.partial(attention_kernel, nb), grid_spec=spec, o...  17.9 us
    ppermute x12, starting transfers between devices, shifted(): return lax.ppermute(x, ('ctx', 'head'), pairs)  17 us
    all_to_all x4, waiting for transfers between devices, swap(): return lax.all_to_all(x, 'head', split_axis=0, concat_axis=0, tiled=True)  16.4 us
    unnamed x20, local copies, waits for them, and re-layouts  3.66 us
    reshape x4, local copies, waits for them, and re-layouts, by_token(): a.reshape(rows, -1)  3.34 us
  transfers between devices with their start and end apart: 16, of which 10 were waited for; matrix products, arithmetic and copies ran while one was open for 6% of the time, Pallas kernels for 0%

profile of v4, /device:TPU:1, one launch (start us, length us, event | category | flops | bytes accessed | tf_op | source)
XLA Modules:
  0.0 116.5 jit_solution(5303721161640883988)
XLA Ops:
  0.6 0.0 copy-start
  0.6 0.0 copy-start.6
  0.7 0.0 copy-start.7
  0.7 0.9 copy-done
  1.6 1.0 copy_bitcast_fusion.4
  2.6 0.8 maximum_bitcast_fusion.1
  3.4 5.8 %all-to-all-start.1 = ((bf16[8,96,256]{2,1,0:T(8,128)(2,1)}), bf16[8,96,256]{2,1,0:T(8,128)(2,1)S(1)}, u32[]{:S(2)}, u32[]{:S(2)}) async-start(bf16[8,96,256]{2,1,0:T(8,128)(2,1)} %maximum_bitcast_fusion.1), calls=%async_computation.1 | async-start | bytes 786432 | tf_op jit(solution)/shard_map/all_to_all | solution.py:291
  9.2 0.0 copy-done.6
  9.2 0.0 copy-done.7
  9.2 0.2 copy_bitcast_fusion
  9.3 1.4 %maximum_bitcast_fusion = bf16[8,96,1024]{2,1,0:T(8,128)(2,1)} fusion(bf16[96,8,512]{2,0,1:T(8,128)(2,1)S(1)} %get-tuple-element.31, bf16[96,8,512]{2,0,1:T(8,128)(2,1)S(1)} %get-tuple-element.32), kind=kLoop, calls=%fused_computation | loop fusion | flops 3145728 | bytes 3145728 | tf_op jit(solution)/shard_map/transpose | solution.py:303
  10.7 0.0 copy-start.8
  10.7 0.0 copy-start.5
  10.7 6.5 %all-to-all-done.1 = bf16[8,96,256]{2,1,0:T(8,128)(2,1)S(1)} async-done(((bf16[8,96,256]{2,1,0:T(8,128)(2,1)}), bf16[8,96,256]{2,1,0:T(8,128)(2,1)S(1)}, u32[]{:S(2)}, u32[]{:S(2)}) %all-to-all-start.1) | async-done | bytes 393248 | tf_op jit(solution)/shard_map/all_to_all | solution.py:291
  17.2 4.4 %all-to-all-start = ((bf16[8,96,1024]{2,1,0:T(8,128)(2,1)}), bf16[8,96,1024]{2,1,0:T(8,128)(2,1)S(1)}, u32[]{:S(2)}, u32[]{:S(2)}) async-start(bf16[8,96,1024]{2,1,0:T(8,128)(2,1)} %maximum_bitcast_fusion), calls=%async_computation | async-start | bytes 3145728 | tf_op jit(solution)/shard_map/all_to_all | solution.py:291
  21.6 3.0 %collective-permute-start.1 = (bf16[256,256]{1,0:T(8,128)(2,1)S(1)}, bf16[256,256]{1,0:T(8,128)(2,1)S(1)}, u32[]{:S(2)}, u32[]{:S(2)}) collective-permute-start(bf16[256,256]{1,0:T(8,128)(2,1)S(1)} %get-tuple-element.30), channel_id=1, source_target_pairs={{0,16},{1,65},{2,18},{3,67},{4,20},{5,69},{6,22},{7,71},{8,24},{9,... | collective-permute-start | bytes 393224 | tf_op jit(solution)/shard_map/ppermute | solution.py:42
  24.6 0.4 collective-permute-start
  25.0 2.3 %collective-permute-start.2 = (bf16[256,256]{1,0:T(8,128)(2,1)S(1)}, bf16[256,256]{1,0:T(8,128)(2,1)S(1)}, u32[]{:S(2)}, u32[]{:S(2)}) collective-permute-start(bf16[256,256]{1,0:T(8,128)(2,1)S(1)} %get-tuple-element.30), channel_id=1, source_target_pairs={{0,24},{1,97},{2,26},{3,99},{4,28},{5,101},{6,30},{7,103},{8,0},{9... | collective-permute-start | bytes 393224 | tf_op jit(solution)/shard_map/ppermute | solution.py:42
  27.3 0.0 collective-permute-done.1
  27.3 2.4 %collective-permute-done = bf16[256,256]{1,0:T(8,128)(2,1)S(1)} collective-permute-done((bf16[256,256]{1,0:T(8,128)(2,1)S(1)}, bf16[256,256]{1,0:T(8,128)(2,1)S(1)}, u32[]{:S(2)}, u32[]{:S(2)}) %collective-permute-start) | collective-permute-done | bytes 131104 | tf_op jit(solution)/shard_map/ppermute | solution.py:42
  29.7 0.0 collective-permute-done.2
  29.7 0.1 pad_maximum_fusion.a0
  29.8 4.1 %collective-permute-start.5 = (bf16[4,256,256]{2,1,0:T(8,128)(2,1)S(1)}, bf16[4,256,256]{2,1,0:T(8,128)(2,1)S(1)}, u32[]{:S(2)}, u32[]{:S(2)}) collective-permute-start(bf16[4,256,256]{2,1,0:T(8,128)(2,1)S(1)} %pad_maximum_fusion.a0), channel_id=1, source_target_pairs={{0,96},{1,25},{2,98},{3,27},{4,100},{5,29},{6,102},{7,31},{8,104},... | collective-permute-start | bytes 1572872 | tf_op jit(solution)/shard_map/ppermute | solution.py:42
  33.8 0.0 collective-permute-start.4
  33.8 0.7 collective-permute-start.3
  34.5 0.0 copy-done.8
  34.5 0.1 pad_add_fusion.here
  34.6 11.0 %collective-permute-done.5.a3 = bf16[4,256,256]{2,1,0:T(8,128)(2,1)S(1)} collective-permute-done((bf16[4,256,256]{2,1,0:T(8,128)(2,1)S(1)}, bf16[4,256,256]{2,1,0:T(8,128)(2,1)S(1)}, u32[]{:S(2)}, u32[]{:S(2)}) %collective-permute-start.5) | collective-permute-done | bytes 524320 | tf_op jit(solution)/shard_map/ppermute | solution.py:42
  45.6 0.0 copy-start.3
  45.6 0.8 copy-done.3
  46.4 0.0 collective-permute-done.4.a2
  46.4 2.7 %collective-permute-done.3.a1 = bf16[4,256,256]{2,1,0:T(8,128)(2,1)} collective-permute-done((bf16[4,256,256]{2,1,0:T(8,128)(2,1)S(1)}, bf16[4,256,256]{2,1,0:T(8,128)(2,1)}, u32[]{:S(2)}, u32[]{:S(2)}) %collective-permute-start.3) | collective-permute-done | bytes 524320 | tf_op jit(solution)/shard_map/ppermute | solution.py:42
  49.1 0.0 all-to-all-done
  49.1 0.0 copy-done.5
  49.1 1.0 copy-done.4
  50.1 17.9 %tree_attention.1 = (bf16[768,1024]{1,0:T(8,128)(2,1)}, f32[256,256]{1,0:T(8,128)S(1)}, bf16[512,256]{1,0:T(8,128)(2,1)S(1)}, bf16[4,256,256]{2,1,0:T(8,128)(2,1...) custom-call(s32[2]{0:T(128)S(1)} %pad_add_fusion.here, ...), custom_call_target="tpu_custom_call" | custom-call | flops 7247757312 | bytes 3145728 | tf_op jit(solution)/shard_map/tree_attention/pallas_call | solution.py:273
  68.0 0.0 copy-start.1
  68.0 0.7 copy-done.1
  68.7 0.0 collective-permute-start.6
  68.7 2.3 %collective-permute-start.7 = (bf16[4,256,256]{2,1,0:T(8,128)(2,1)}, bf16[4,256,256]{2,1,0:T(8,128)(2,1)}, u32[]{:S(2)}, u32[]{:S(2)}) collective-permute-start(bf16[4,256,256]{2,1,0:T(8,128)(2,1)} %get-tuple-element.17), channel_id=1, source_target_pairs={{0,64},{1,17},{2,66},{3,19},{4,68},{5,21},{6,70},{7,23},{8,72},{9,... | collective-permute-start | bytes 1572872 | tf_op jit(solution)/shard_map/ppermute | solution.py:42
  71.0 0.4 collective-permute-start.8
  71.4 8.0 %all-to-all-start.2 = ((bf16[8,96,1024]{2,1,0:T(8,128)(2,1)}), bf16[8,96,1024]{2,1,0:T(8,128)(2,1)S(1)}, u32[]{:S(2)}, u32[]{:S(2)}) async-start(bf16[8,96,1024]{2,1,0:T(8,128)(2,1)} %bitcast.10), calls=%async_computation.2 | async-start | bytes 3145728 | tf_op jit(solution)/shard_map/all_to_all | solution.py:291
  79.4 4.8 %collective-permute-done.6 = bf16[4,256,256]{2,1,0:T(8,128)(2,1)S(1)} collective-permute-done((bf16[4,256,256]{2,1,0:T(8,128)(2,1)}, bf16[4,256,256]{2,1,0:T(8,128)(2,1)S(1)}, u32[]{:S(2)}, u32[]{:S(2)}) %collective-permute-start.6) | collective-permute-done | bytes 524320 | tf_op jit(solution)/shard_map/ppermute | solution.py:42
  84.2 0.0 collective-permute-done.7
  84.2 0.6 collective-permute-done.8
  84.8 1.3 %add_convert_fusion = bf16[3,256,256]{2,1,0:T(8,128)(2,1)S(1)} fusion(bf16[4,256,256]{2,1,0:T(8,128)(2,1)} %collective-permute-done.8, bf16[4,256,256]{2,1,0:T(8,128)(2,1)} %collective-permute-done.7, bf16[4,256,256]{2,1,0:T(8,128)(2,1)S(1)} %collective-permute-done.6, bf16[4,256,256]{2,1,0:T(8,128)(2,1)S(1)} %get-tuple-element.15), kind=kLoop, calls=%fused_computation.5 | loop fusion | flops 1572864 | bytes 1966080 | tf_op jit(solution)/shard_map/convert_element_type | solution.py:322
  86.2 0.3 collective-permute-start.9
  86.5 2.5 %collective-permute-start.11 = (bf16[256,256]{1,0:T(8,128)(2,1)S(1)}, bf16[256,256]{1,0:T(8,128)(2,1)S(1)}, u32[]{:S(2)}, u32[]{:S(2)}) collective-permute-start(bf16[256,256]{1,0:T(8,128)(2,1)S(1)} %get-tuple-element.27), channel_id=1, source_target_pairs={{0,24},{1,97},{2,26},{3,99},{4,28},{5,101},{6,30},{7,103},{8,0},{9... | collective-permute-start | bytes 393224 | tf_op jit(solution)/shard_map/ppermute | solution.py:42
  89.0 1.1 collective-permute-start.10
  90.1 1.5 %collective-permute-done.9 = bf16[256,256]{1,0:T(8,128)(2,1)S(1)} collective-permute-done((bf16[256,256]{1,0:T(8,128)(2,1)S(1)}, bf16[256,256]{1,0:T(8,128)(2,1)S(1)}, u32[]{:S(2)}, u32[]{:S(2)}) %collective-permute-start.9) | collective-permute-done | bytes 131104 | tf_op jit(solution)/shard_map/ppermute | solution.py:42
  91.6 0.0 collective-permute-done.11
  91.6 2.7 %collective-permute-done.10 = bf16[256,256]{1,0:T(8,128)(2,1)S(1)} collective-permute-done((bf16[256,256]{1,0:T(8,128)(2,1)S(1)}, bf16[256,256]{1,0:T(8,128)(2,1)S(1)}, u32[]{:S(2)}, u32[]{:S(2)}) %collective-permute-start.10) | collective-permute-done | bytes 131104 | tf_op jit(solution)/shard_map/ppermute | solution.py:42
  94.3 0.0 copy-done.2
  94.3 1.1 fusion.3
  95.5 0.8 pad_maximum_fusion.1
  96.2 3.9 %all-to-all-done.2 = bf16[8,96,1024]{2,1,0:T(8,128)(2,1)S(1)} async-done(((bf16[8,96,1024]{2,1,0:T(8,128)(2,1)}), bf16[8,96,1024]{2,1,0:T(8,128)(2,1)S(1)}, u32[]{:S(2)}, u32[]{:S(2)}) %all-to-all-start.2) | async-done | bytes 1572896 | tf_op jit(solution)/shard_map/all_to_all | solution.py:291
  100.1 6.8 %all-to-all-start.3 = ((bf16[8,96,256]{2,1,0:T(8,128)(2,1)}), bf16[8,96,256]{2,1,0:T(8,128)(2,1)S(1)}, u32[]{:S(2)}, u32[]{:S(2)}) async-start(bf16[8,96,256]{2,1,0:T(8,128)(2,1)} %bitcast.16), calls=%async_computation.3 | async-start | bytes 786432 | tf_op jit(solution)/shard_map/all_to_all | solution.py:291
  106.9 0.1 slice_bitcast_fusion
  107.0 0.9 copy.23
  108.0 0.9 copy.22
  108.9 6.0 %all-to-all-done.3 = bf16[8,96,256]{2,1,0:T(8,128)(2,1)S(1)} async-done(((bf16[8,96,256]{2,1,0:T(8,128)(2,1)}), bf16[8,96,256]{2,1,0:T(8,128)(2,1)S(1)}, u32[]{:S(2)}, u32[]{:S(2)}) %all-to-all-start.3) | async-done | bytes 393248 | tf_op jit(solution)/shard_map/all_to_all | solution.py:291
  114.9 0.1 slice_bitcast_fusion.2
  115.0 0.7 copy.32
  115.7 0.7 copy.33
  (5 shorter events, 0.1 us)
Async XLA Ops:
  0.6 0.9 copy-start
  0.6 8.5 %copy-start.6 = (bf16[96,4096]{1,0:T(8,128)(2,1)S(1)}, bf16[96,4096]{1,0:T(8,128)(2,1)}, u32[]{:S(2)}) copy-start(bf16[96,4096]{1,0:T(8,128)(2,1)} %param.9) | copy-start | bytes 2359300
  0.7 8.5 %copy-start.7 = (bf16[96,4096]{1,0:T(8,128)(2,1)S(1)}, bf16[96,4096]{1,0:T(8,128)(2,1)}, u32[]{:S(2)}) copy-start(bf16[96,4096]{1,0:T(8,128)(2,1)} %param.6) | copy-start | bytes 2359300
  3.4 13.9 %all-to-all-start.1 = ((bf16[8,96,256]{2,1,0:T(8,128)(2,1)}), bf16[8,96,256]{2,1,0:T(8,128)(2,1)S(1)}, u32[]{:S(2)}, u32[]{:S(2)}) async-start(bf16[8,96,256]{2,1,0:T(8,128)(2,1)} %maximum_bitcast_fusion.1), calls=%async_computation.1 | async-start | bytes 786432 | tf_op jit(solution)/shard_map/all_to_all | solution.py:291
  10.7 23.8 %copy-start.8 = (s32[768]{0:T(1024)S(1)}, s32[768]{0:T(1024)}, u32[]{:S(2)}) copy-start(s32[768]{0:T(1024)} %param.11) | copy-start | bytes 9220
  10.7 38.4 %copy-start.5 = (s32[48]{0:T(128)S(1)}, s32[48]{0:T(128)}, u32[]{:S(2)}) copy-start(s32[48]{0:T(128)} %parent.1) | copy-start | bytes 580
  17.2 31.9 %all-to-all-start = ((bf16[8,96,1024]{2,1,0:T(8,128)(2,1)}), bf16[8,96,1024]{2,1,0:T(8,128)(2,1)S(1)}, u32[]{:S(2)}, u32[]{:S(2)}) async-start(bf16[8,96,1024]{2,1,0:T(8,128)(2,1)} %maximum_bitcast_fusion), calls=%async_computation | async-start | bytes 3145728 | tf_op jit(solution)/shard_map/all_to_all | solution.py:291
  21.6 5.7 %collective-permute-start.1 = (bf16[256,256]{1,0:T(8,128)(2,1)S(1)}, bf16[256,256]{1,0:T(8,128)(2,1)S(1)}, u32[]{:S(2)}, u32[]{:S(2)}) collective-permute-start(bf16[256,256]{1,0:T(8,128)(2,1)S(1)} %get-tuple-element.30), channel_id=1, source_target_pairs={{0,16},{1,65},{2,18},{3,67},{4,20},{5,69},{6,22},{7,71},{8,24},{9,... | collective-permute-start | bytes 393224 | tf_op jit(solution)/shard_map/ppermute | solution.py:42
  24.6 5.1 %collective-permute-start = (bf16[256,256]{1,0:T(8,128)(2,1)S(1)}, bf16[256,256]{1,0:T(8,128)(2,1)S(1)}, u32[]{:S(2)}, u32[]{:S(2)}) collective-permute-start(bf16[256,256]{1,0:T(8,128)(2,1)S(1)} %get-tuple-element.30), channel_id=1, source_target_pairs={{0,8},{1,33},{2,10},{3,35},{4,12},{5,37},{6,14},{7,39},{8,16},{9,4... | collective-permute-start | bytes 393224 | tf_op jit(solution)/shard_map/ppermute | solution.py:42
  25.0 4.7 %collective-permute-start.2 = (bf16[256,256]{1,0:T(8,128)(2,1)S(1)}, bf16[256,256]{1,0:T(8,128)(2,1)S(1)}, u32[]{:S(2)}, u32[]{:S(2)}) collective-permute-start(bf16[256,256]{1,0:T(8,128)(2,1)S(1)} %get-tuple-element.30), channel_id=1, source_target_pairs={{0,24},{1,97},{2,26},{3,99},{4,28},{5,101},{6,30},{7,103},{8,0},{9... | collective-permute-start | bytes 393224 | tf_op jit(solution)/shard_map/ppermute | solution.py:42
  29.8 15.8 %collective-permute-start.5 = (bf16[4,256,256]{2,1,0:T(8,128)(2,1)S(1)}, bf16[4,256,256]{2,1,0:T(8,128)(2,1)S(1)}, u32[]{:S(2)}, u32[]{:S(2)}) collective-permute-start(bf16[4,256,256]{2,1,0:T(8,128)(2,1)S(1)} %pad_maximum_fusion.a0), channel_id=1, source_target_pairs={{0,96},{1,25},{2,98},{3,27},{4,100},{5,29},{6,102},{7,31},{8,104},... | collective-permute-start | bytes 1572872 | tf_op jit(solution)/shard_map/ppermute | solution.py:42
  33.8 12.5 %collective-permute-start.4 = (bf16[4,256,256]{2,1,0:T(8,128)(2,1)S(1)}, bf16[4,256,256]{2,1,0:T(8,128)(2,1)}, u32[]{:S(2)}, u32[]{:S(2)}) collective-permute-start(bf16[4,256,256]{2,1,0:T(8,128)(2,1)S(1)} %pad_maximum_fusion.a0), channel_id=1, source_target_pairs={{0,64},{1,17},{2,66},{3,19},{4,68},{5,21},{6,70},{7,23},{8,72},{9,... | collective-permute-start | bytes 1572872 | tf_op jit(solution)/shard_map/ppermute | solution.py:42
  33.8 15.3 %collective-permute-start.3 = (bf16[4,256,256]{2,1,0:T(8,128)(2,1)S(1)}, bf16[4,256,256]{2,1,0:T(8,128)(2,1)}, u32[]{:S(2)}, u32[]{:S(2)}) collective-permute-start(bf16[4,256,256]{2,1,0:T(8,128)(2,1)S(1)} %pad_maximum_fusion.a0), channel_id=1, source_target_pairs={{0,32},{1,9},{2,34},{3,11},{4,36},{5,13},{6,38},{7,15},{8,40},{9,1... | collective-permute-start | bytes 1572872 | tf_op jit(solution)/shard_map/ppermute | solution.py:42
  45.6 0.8 copy-start.3
  49.1 1.0 copy-start.4
  68.0 0.7 copy-start.1
  68.7 15.5 %collective-permute-start.6 = (bf16[4,256,256]{2,1,0:T(8,128)(2,1)}, bf16[4,256,256]{2,1,0:T(8,128)(2,1)S(1)}, u32[]{:S(2)}, u32[]{:S(2)}) collective-permute-start(bf16[4,256,256]{2,1,0:T(8,128)(2,1)} %get-tuple-element.16), channel_id=1, source_target_pairs={{0,32},{1,9},{2,34},{3,11},{4,36},{5,13},{6,38},{7,15},{8,40},{9,1... | collective-permute-start | bytes 1572872 | tf_op jit(solution)/shard_map/ppermute | solution.py:42
  68.7 15.5 %collective-permute-start.7 = (bf16[4,256,256]{2,1,0:T(8,128)(2,1)}, bf16[4,256,256]{2,1,0:T(8,128)(2,1)}, u32[]{:S(2)}, u32[]{:S(2)}) collective-permute-start(bf16[4,256,256]{2,1,0:T(8,128)(2,1)} %get-tuple-element.17), channel_id=1, source_target_pairs={{0,64},{1,17},{2,66},{3,19},{4,68},{5,21},{6,70},{7,23},{8,72},{9,... | collective-permute-start | bytes 1572872 | tf_op jit(solution)/shard_map/ppermute | solution.py:42
  71.0 13.8 %collective-permute-start.8 = (bf16[4,256,256]{2,1,0:T(8,128)(2,1)}, bf16[4,256,256]{2,1,0:T(8,128)(2,1)}, u32[]{:S(2)}, u32[]{:S(2)}) collective-permute-start(bf16[4,256,256]{2,1,0:T(8,128)(2,1)} %get-tuple-element.18), channel_id=1, source_target_pairs={{0,96},{1,25},{2,98},{3,27},{4,100},{5,29},{6,102},{7,31},{8,104},... | collective-permute-start | bytes 1572872 | tf_op jit(solution)/shard_map/ppermute | solution.py:42
  71.4 28.7 %all-to-all-start.2 = ((bf16[8,96,1024]{2,1,0:T(8,128)(2,1)}), bf16[8,96,1024]{2,1,0:T(8,128)(2,1)S(1)}, u32[]{:S(2)}, u32[]{:S(2)}) async-start(bf16[8,96,1024]{2,1,0:T(8,128)(2,1)} %bitcast.10), calls=%async_computation.2 | async-start | bytes 3145728 | tf_op jit(solution)/shard_map/all_to_all | solution.py:291
  79.4 15.0 %copy-start.2 = (f32[256,256]{1,0:T(8,128)S(1)}, f32[256,256]{1,0:T(8,128)}, u32[]{:S(2)}) copy-start(f32[256,256]{1,0:T(8,128)} %copy-done.1) | copy-start | bytes 786436
  86.2 5.4 %collective-permute-start.9 = (bf16[256,256]{1,0:T(8,128)(2,1)S(1)}, bf16[256,256]{1,0:T(8,128)(2,1)S(1)}, u32[]{:S(2)}, u32[]{:S(2)}) collective-permute-start(bf16[256,256]{1,0:T(8,128)(2,1)S(1)} %get-tuple-element.26), channel_id=1, source_target_pairs={{0,8},{1,33},{2,10},{3,35},{4,12},{5,37},{6,14},{7,39},{8,16},{9,4... | collective-permute-start | bytes 393224 | tf_op jit(solution)/shard_map/ppermute | solution.py:42
  86.5 5.1 %collective-permute-start.11 = (bf16[256,256]{1,0:T(8,128)(2,1)S(1)}, bf16[256,256]{1,0:T(8,128)(2,1)S(1)}, u32[]{:S(2)}, u32[]{:S(2)}) collective-permute-start(bf16[256,256]{1,0:T(8,128)(2,1)S(1)} %get-tuple-element.27), channel_id=1, source_target_pairs={{0,24},{1,97},{2,26},{3,99},{4,28},{5,101},{6,30},{7,103},{8,0},{9... | collective-permute-start | bytes 393224 | tf_op jit(solution)/shard_map/ppermute | solution.py:42
  89.0 5.3 %collective-permute-start.10 = (bf16[256,256]{1,0:T(8,128)(2,1)S(1)}, bf16[256,256]{1,0:T(8,128)(2,1)S(1)}, u32[]{:S(2)}, u32[]{:S(2)}) collective-permute-start(bf16[256,256]{1,0:T(8,128)(2,1)S(1)} %get-tuple-element.28), channel_id=1, source_target_pairs={{0,16},{1,65},{2,18},{3,67},{4,20},{5,69},{6,22},{7,71},{8,24},{9,... | collective-permute-start | bytes 393224 | tf_op jit(solution)/shard_map/ppermute | solution.py:42
  100.1 14.9 %all-to-all-start.3 = ((bf16[8,96,256]{2,1,0:T(8,128)(2,1)}), bf16[8,96,256]{2,1,0:T(8,128)(2,1)S(1)}, u32[]{:S(2)}, u32[]{:S(2)}) async-start(bf16[8,96,256]{2,1,0:T(8,128)(2,1)} %bitcast.16), calls=%async_computation.3 | async-start | bytes 786432 | tf_op jit(solution)/shard_map/all_to_all | solution.py:291

commit v5 on v4

--- a/solution.py
+++ b/solution.py
@@ -304,8 +304,10 @@
 
     kv = by_head(keys, values)
     first = kv[:BLK]
-    line = jnp.stack([first] + [shifted(first, 1, s) for s in range(1, SIDE)])
-    arrived = [line] + [shifted(line, 0, s) for s in range(1, SIDE)]
+    by = {s: shifted(first, 1, s) for s in (2, 1, 3)}
+    line = jnp.stack([first] + [by[s] for s in range(1, SIDE)])
+    by = {s: shifted(line, 0, s) for s in (2, 1, 3)}
+    arrived = [line] + [by[s] for s in range(1, SIDE)]
     qg = by_head(queries, grad_out)
     out, dfirst, drest, *terms = attention(here, parent, qg, kv, arrived, subtree_end.reshape(nb, BLK))
 
@@ -317,12 +319,13 @@
 
     out = send_back(out)
 
-    got = [terms[0]] + [shifted(terms[s], 0, s) for s in range(1, SIDE)]
-    summed = sum(x[0].astype(F32) for x in got)
+    by = {s: shifted(terms[s], 0, s) for s in (2, 1, 3)}
+    got = [terms[0]] + [by[s] for s in range(1, SIDE)]
+    own = lax.optimization_barrier(dfirst + sum(x[0].astype(F32) for x in got))
     part = sum(x[1:].astype(F32) for x in got).astype(BF16)
-    for s in range(1, SIDE):
-        summed = summed + shifted(part[s - 1], 1, s).astype(F32)
-    dkv = jnp.concatenate([(dfirst + summed).astype(BF16), drest], axis=0)
+    for s in (2, 1, 3):
+        own = own + shifted(part[s - 1], 1, s).astype(F32)
+    dkv = jnp.concatenate([own.astype(BF16), drest], axis=0)
     out, dkv = lax.optimization_barrier((out, dkv))
     attn_out, grad_q = by_token(out)
     grad_k, grad_v = by_token(send_back(dkv))

time: 117 us -> 115 us (0.983)
  starting transfers between devices: 41.9 us -> 39.7 us
    all_to_all x4, starting transfers between devices: 24.9 us -> 23.3 us  [swap(): return lax.all_to_all(x, 'head', split_axis=0, concat_axis=0, tiled=True)]
  transfers between devices with their start and end apart: 16 -> 16, of which waited for: 10 -> 11; matrix products, arithmetic and copies ran while one was open for 6% -> 6% of each run, Pallas kernels for 0% -> 0%
where the time goes in v5:
time: 115 us
  waiting for transfers between devices  42.8 us (37%)
  starting transfers between devices  39.7 us (35%)
  Pallas kernels  17.9 us (16%)
  local copies, waits for them, and re-layouts  8.21 us (7%)
  other arithmetic  5.55 us (5%)
    ppermute x12, waiting for transfers between devices, shifted(): return lax.ppermute(x, ('ctx', 'head'), pairs)  25.3 us
    all_to_all x4, starting transfers between devices, swap(): return lax.all_to_all(x, 'head', split_axis=0, concat_axis=0, tiled=True)  23.3 us
    pallas_call x1, Pallas kernels, attention(): pl.pallas_call(functools.partial(attention_kernel, nb), grid_spec=spec, o...  17.9 us
    all_to_all x4, waiting for transfers between devices, swap(): return lax.all_to_all(x, 'head', split_axis=0, concat_axis=0, tiled=True)  17.5 us
    ppermute x12, starting transfers between devices, shifted(): return lax.ppermute(x, ('ctx', 'head'), pairs)  16.4 us
    unnamed x20, local copies, waits for them, and re-layouts  3.66 us
    reshape x4, local copies, waits for them, and re-layouts, by_token(): a.reshape(rows, -1)  3.34 us
  transfers between devices with their start and end apart: 16, of which 11 were waited for; matrix products, arithmetic and copies ran while one was open for 6% of the time, Pallas kernels for 0%

profile of v5, /device:TPU:1, one launch (start us, length us, event | category | flops | bytes accessed | tf_op | source)
XLA Modules:
  0.0 114.9 jit_solution(6097371310462467199)
XLA Ops:
  0.6 0.0 copy-start
  0.6 0.0 copy-start.6
  0.7 0.0 copy-start.7
  0.7 0.9 copy-done
  1.6 1.0 copy_bitcast_fusion.4
  2.6 0.8 maximum_bitcast_fusion.1
  3.4 5.8 %all-to-all-start.1 = ((bf16[8,96,256]{2,1,0:T(8,128)(2,1)}), bf16[8,96,256]{2,1,0:T(8,128)(2,1)S(1)}, u32[]{:S(2)}, u32[]{:S(2)}) async-start(bf16[8,96,256]{2,1,0:T(8,128)(2,1)} %maximum_bitcast_fusion.1), calls=%async_computation.1 | async-start | bytes 786432 | tf_op jit(solution)/shard_map/all_to_all | solution.py:291
  9.2 0.0 copy-done.6
  9.2 0.0 copy-done.7
  9.2 0.2 copy_bitcast_fusion
  9.3 1.4 %maximum_bitcast_fusion = bf16[8,96,1024]{2,1,0:T(8,128)(2,1)} fusion(bf16[96,8,512]{2,0,1:T(8,128)(2,1)S(1)} %get-tuple-element.31, bf16[96,8,512]{2,0,1:T(8,128)(2,1)S(1)} %get-tuple-element.32), kind=kLoop, calls=%fused_computation | loop fusion | flops 3145728 | bytes 3145728 | tf_op jit(solution)/shard_map/transpose | solution.py:303
  10.7 0.0 copy-start.8
  10.7 0.0 copy-start.5
  10.7 6.5 %all-to-all-done.1 = bf16[8,96,256]{2,1,0:T(8,128)(2,1)S(1)} async-done(((bf16[8,96,256]{2,1,0:T(8,128)(2,1)}), bf16[8,96,256]{2,1,0:T(8,128)(2,1)S(1)}, u32[]{:S(2)}, u32[]{:S(2)}) %all-to-all-start.1) | async-done | bytes 393248 | tf_op jit(solution)/shard_map/all_to_all | solution.py:291
  17.2 4.4 %all-to-all-start = ((bf16[8,96,1024]{2,1,0:T(8,128)(2,1)}), bf16[8,96,1024]{2,1,0:T(8,128)(2,1)S(1)}, u32[]{:S(2)}, u32[]{:S(2)}) async-start(bf16[8,96,1024]{2,1,0:T(8,128)(2,1)} %maximum_bitcast_fusion), calls=%async_computation | async-start | bytes 3145728 | tf_op jit(solution)/shard_map/all_to_all | solution.py:291
  21.6 3.0 %collective-permute-start.1 = (bf16[256,256]{1,0:T(8,128)(2,1)S(1)}, bf16[256,256]{1,0:T(8,128)(2,1)S(1)}, u32[]{:S(2)}, u32[]{:S(2)}) collective-permute-start(bf16[256,256]{1,0:T(8,128)(2,1)S(1)} %get-tuple-element.30), channel_id=1, source_target_pairs={{0,16},{1,65},{2,18},{3,67},{4,20},{5,69},{6,22},{7,71},{8,24},{9,... | collective-permute-start | bytes 393224 | tf_op jit(solution)/shard_map/ppermute | solution.py:42
  24.6 0.4 collective-permute-start
  25.0 2.3 %collective-permute-start.2 = (bf16[256,256]{1,0:T(8,128)(2,1)S(1)}, bf16[256,256]{1,0:T(8,128)(2,1)S(1)}, u32[]{:S(2)}, u32[]{:S(2)}) collective-permute-start(bf16[256,256]{1,0:T(8,128)(2,1)S(1)} %get-tuple-element.30), channel_id=1, source_target_pairs={{0,24},{1,97},{2,26},{3,99},{4,28},{5,101},{6,30},{7,103},{8,0},{9... | collective-permute-start | bytes 393224 | tf_op jit(solution)/shard_map/ppermute | solution.py:42
  27.3 0.0 collective-permute-done.1
  27.3 2.4 %collective-permute-done = bf16[256,256]{1,0:T(8,128)(2,1)S(1)} collective-permute-done((bf16[256,256]{1,0:T(8,128)(2,1)S(1)}, bf16[256,256]{1,0:T(8,128)(2,1)S(1)}, u32[]{:S(2)}, u32[]{:S(2)}) %collective-permute-start) | collective-permute-done | bytes 131104 | tf_op jit(solution)/shard_map/ppermute | solution.py:42
  29.7 0.0 collective-permute-done.2
  29.7 0.1 pad_maximum_fusion.a0
  29.8 4.1 %collective-permute-start.5 = (bf16[4,256,256]{2,1,0:T(8,128)(2,1)S(1)}, bf16[4,256,256]{2,1,0:T(8,128)(2,1)S(1)}, u32[]{:S(2)}, u32[]{:S(2)}) collective-permute-start(bf16[4,256,256]{2,1,0:T(8,128)(2,1)S(1)} %pad_maximum_fusion.a0), channel_id=1, source_target_pairs={{0,96},{1,25},{2,98},{3,27},{4,100},{5,29},{6,102},{7,31},{8,104},... | collective-permute-start | bytes 1572872 | tf_op jit(solution)/shard_map/ppermute | solution.py:42
  33.8 0.0 collective-permute-start.4
  33.8 0.7 collective-permute-start.3
  34.5 0.0 copy-done.8
  34.5 0.1 pad_add_fusion.here
  34.6 11.0 %collective-permute-done.5.a3 = bf16[4,256,256]{2,1,0:T(8,128)(2,1)S(1)} collective-permute-done((bf16[4,256,256]{2,1,0:T(8,128)(2,1)S(1)}, bf16[4,256,256]{2,1,0:T(8,128)(2,1)S(1)}, u32[]{:S(2)}, u32[]{:S(2)}) %collective-permute-start.5) | collective-permute-done | bytes 524320 | tf_op jit(solution)/shard_map/ppermute | solution.py:42
  45.6 0.8 copy-done.3
  46.4 0.0 collective-permute-done.4.a2
  46.4 2.7 %collective-permute-done.3.a1 = bf16[4,256,256]{2,1,0:T(8,128)(2,1)} collective-permute-done((bf16[4,256,256]{2,1,0:T(8,128)(2,1)S(1)}, bf16[4,256,256]{2,1,0:T(8,128)(2,1)}, u32[]{:S(2)}, u32[]{:S(2)}) %collective-permute-start.3) | collective-permute-done | bytes 524320 | tf_op jit(solution)/shard_map/ppermute | solution.py:42
  49.1 0.0 all-to-all-done
  49.1 0.0 copy-done.5
  49.1 1.0 copy-done.4
  50.1 17.9 %tree_attention.1 = (bf16[768,1024]{1,0:T(8,128)(2,1)}, f32[256,256]{1,0:T(8,128)S(1)}, bf16[512,256]{1,0:T(8,128)(2,1)S(1)}, bf16[4,256,256]{2,1,0:T(8,128)(2,1...) custom-call(s32[2]{0:T(128)S(1)} %pad_add_fusion.here, ...), custom_call_target="tpu_custom_call" | custom-call | flops 7247757312 | bytes 3145728 | tf_op jit(solution)/shard_map/tree_attention/pallas_call | solution.py:273
  68.0 0.0 copy-start.1
  68.0 0.7 copy-done.1
  68.7 0.0 collective-permute-start.6
  68.7 2.3 %collective-permute-start.7 = (bf16[4,256,256]{2,1,0:T(8,128)(2,1)}, bf16[4,256,256]{2,1,0:T(8,128)(2,1)}, u32[]{:S(2)}, u32[]{:S(2)}) collective-permute-start(bf16[4,256,256]{2,1,0:T(8,128)(2,1)} %get-tuple-element.17), channel_id=1, source_target_pairs={{0,64},{1,17},{2,66},{3,19},{4,68},{5,21},{6,70},{7,23},{8,72},{9,... | collective-permute-start | bytes 1572872 | tf_op jit(solution)/shard_map/ppermute | solution.py:42
  71.0 0.4 collective-permute-start.8
  71.4 8.0 %all-to-all-start.2 = ((bf16[8,96,1024]{2,1,0:T(8,128)(2,1)}), bf16[8,96,1024]{2,1,0:T(8,128)(2,1)S(1)}, u32[]{:S(2)}, u32[]{:S(2)}) async-start(bf16[8,96,1024]{2,1,0:T(8,128)(2,1)} %bitcast.10), calls=%async_computation.2 | async-start | bytes 3145728 | tf_op jit(solution)/shard_map/all_to_all | solution.py:291
  79.4 4.8 %collective-permute-done.6 = bf16[4,256,256]{2,1,0:T(8,128)(2,1)S(1)} collective-permute-done((bf16[4,256,256]{2,1,0:T(8,128)(2,1)}, bf16[4,256,256]{2,1,0:T(8,128)(2,1)S(1)}, u32[]{:S(2)}, u32[]{:S(2)}) %collective-permute-start.6) | collective-permute-done | bytes 524320 | tf_op jit(solution)/shard_map/ppermute | solution.py:42
  84.2 0.0 collective-permute-done.7
  84.2 0.6 collective-permute-done.8
  84.8 1.3 %add_convert_fusion = bf16[3,256,256]{2,1,0:T(8,128)(2,1)S(1)} fusion(bf16[4,256,256]{2,1,0:T(8,128)(2,1)} %collective-permute-done.8, bf16[4,256,256]{2,1,0:T(8,128)(2,1)} %collective-permute-done.7, bf16[4,256,256]{2,1,0:T(8,128)(2,1)S(1)} %collective-permute-done.6, bf16[4,256,256]{2,1,0:T(8,128)(2,1)S(1)} %get-tuple-element.15), kind=kLoop, calls=%fused_computation.5 | loop fusion | flops 1572864 | bytes 1966080 | tf_op jit(solution)/shard_map/convert_element_type | solution.py:325
  86.2 1.3 %collective-permute-start.9 = (bf16[256,256]{1,0:T(8,128)(2,1)S(1)}, bf16[256,256]{1,0:T(8,128)(2,1)S(1)}, u32[]{:S(2)}, u32[]{:S(2)}) collective-permute-start(bf16[256,256]{1,0:T(8,128)(2,1)S(1)} %get-tuple-element.26), channel_id=1, source_target_pairs={{0,16},{1,65},{2,18},{3,67},{4,20},{5,69},{6,22},{7,71},{8,24},{9,... | collective-permute-start | bytes 393224 | tf_op jit(solution)/shard_map/ppermute | solution.py:42
  87.5 1.5 %collective-permute-start.11 = (bf16[256,256]{1,0:T(8,128)(2,1)S(1)}, bf16[256,256]{1,0:T(8,128)(2,1)S(1)}, u32[]{:S(2)}, u32[]{:S(2)}) collective-permute-start(bf16[256,256]{1,0:T(8,128)(2,1)S(1)} %get-tuple-element.27), channel_id=1, source_target_pairs={{0,24},{1,97},{2,26},{3,99},{4,28},{5,101},{6,30},{7,103},{8,0},{9... | collective-permute-start | bytes 393224 | tf_op jit(solution)/shard_map/ppermute | solution.py:42
  89.0 0.5 collective-permute-start.10
  89.5 0.0 copy-done.2
  89.5 1.1 bitcast_add_fusion
  90.5 1.1 collective-permute-done.9
  91.6 2.0 %collective-permute-done.11 = bf16[256,256]{1,0:T(8,128)(2,1)S(1)} collective-permute-done((bf16[256,256]{1,0:T(8,128)(2,1)S(1)}, bf16[256,256]{1,0:T(8,128)(2,1)S(1)}, u32[]{:S(2)}, u32[]{:S(2)}) %collective-permute-start.11) | collective-permute-done | bytes 131104 | tf_op jit(solution)/shard_map/ppermute | solution.py:42
  93.6 0.7 collective-permute-done.10
  94.3 0.1 add_convert_fusion.1
  94.4 0.8 pad_maximum_fusion.1
  95.1 4.9 %all-to-all-done.2 = bf16[8,96,1024]{2,1,0:T(8,128)(2,1)S(1)} async-done(((bf16[8,96,1024]{2,1,0:T(8,128)(2,1)}), bf16[8,96,1024]{2,1,0:T(8,128)(2,1)S(1)}, u32[]{:S(2)}, u32[]{:S(2)}) %all-to-all-start.2) | async-done | bytes 1572896 | tf_op jit(solution)/shard_map/all_to_all | solution.py:291
  100.1 5.2 %all-to-all-start.3 = ((bf16[8,96,256]{2,1,0:T(8,128)(2,1)}), bf16[8,96,256]{2,1,0:T(8,128)(2,1)S(1)}, u32[]{:S(2)}, u32[]{:S(2)}) async-start(bf16[8,96,256]{2,1,0:T(8,128)(2,1)} %bitcast.16), calls=%async_computation.3 | async-start | bytes 786432 | tf_op jit(solution)/shard_map/all_to_all | solution.py:291
  105.3 0.1 slice_bitcast_fusion
  105.4 0.9 copy.23
  106.4 0.9 copy.22
  107.3 6.0 %all-to-all-done.3 = bf16[8,96,256]{2,1,0:T(8,128)(2,1)S(1)} async-done(((bf16[8,96,256]{2,1,0:T(8,128)(2,1)}), bf16[8,96,256]{2,1,0:T(8,128)(2,1)S(1)}, u32[]{:S(2)}, u32[]{:S(2)}) %all-to-all-start.3) | async-done | bytes 393248 | tf_op jit(solution)/shard_map/all_to_all | solution.py:291
  113.4 0.1 slice_bitcast_fusion.2
  113.4 0.7 copy.32
  114.2 0.7 copy.33
  (6 shorter events, 0.1 us)
Async XLA Ops:
  0.6 0.9 copy-start
  0.6 8.5 %copy-start.6 = (bf16[96,4096]{1,0:T(8,128)(2,1)S(1)}, bf16[96,4096]{1,0:T(8,128)(2,1)}, u32[]{:S(2)}) copy-start(bf16[96,4096]{1,0:T(8,128)(2,1)} %param.9) | copy-start | bytes 2359300
  0.7 8.5 %copy-start.7 = (bf16[96,4096]{1,0:T(8,128)(2,1)S(1)}, bf16[96,4096]{1,0:T(8,128)(2,1)}, u32[]{:S(2)}) copy-start(bf16[96,4096]{1,0:T(8,128)(2,1)} %param.6) | copy-start | bytes 2359300
  3.4 13.9 %all-to-all-start.1 = ((bf16[8,96,256]{2,1,0:T(8,128)(2,1)}), bf16[8,96,256]{2,1,0:T(8,128)(2,1)S(1)}, u32[]{:S(2)}, u32[]{:S(2)}) async-start(bf16[8,96,256]{2,1,0:T(8,128)(2,1)} %maximum_bitcast_fusion.1), calls=%async_computation.1 | async-start | bytes 786432 | tf_op jit(solution)/shard_map/all_to_all | solution.py:291
  10.7 23.8 %copy-start.8 = (s32[768]{0:T(1024)S(1)}, s32[768]{0:T(1024)}, u32[]{:S(2)}) copy-start(s32[768]{0:T(1024)} %param.11) | copy-start | bytes 9220
  10.7 38.4 %copy-start.5 = (s32[48]{0:T(128)S(1)}, s32[48]{0:T(128)}, u32[]{:S(2)}) copy-start(s32[48]{0:T(128)} %parent.1) | copy-start | bytes 580
  17.2 31.9 %all-to-all-start = ((bf16[8,96,1024]{2,1,0:T(8,128)(2,1)}), bf16[8,96,1024]{2,1,0:T(8,128)(2,1)S(1)}, u32[]{:S(2)}, u32[]{:S(2)}) async-start(bf16[8,96,1024]{2,1,0:T(8,128)(2,1)} %maximum_bitcast_fusion), calls=%async_computation | async-start | bytes 3145728 | tf_op jit(solution)/shard_map/all_to_all | solution.py:291
  21.6 5.7 %collective-permute-start.1 = (bf16[256,256]{1,0:T(8,128)(2,1)S(1)}, bf16[256,256]{1,0:T(8,128)(2,1)S(1)}, u32[]{:S(2)}, u32[]{:S(2)}) collective-permute-start(bf16[256,256]{1,0:T(8,128)(2,1)S(1)} %get-tuple-element.30), channel_id=1, source_target_pairs={{0,16},{1,65},{2,18},{3,67},{4,20},{5,69},{6,22},{7,71},{8,24},{9,... | collective-permute-start | bytes 393224 | tf_op jit(solution)/shard_map/ppermute | solution.py:42
  24.6 5.1 %collective-permute-start = (bf16[256,256]{1,0:T(8,128)(2,1)S(1)}, bf16[256,256]{1,0:T(8,128)(2,1)S(1)}, u32[]{:S(2)}, u32[]{:S(2)}) collective-permute-start(bf16[256,256]{1,0:T(8,128)(2,1)S(1)} %get-tuple-element.30), channel_id=1, source_target_pairs={{0,8},{1,33},{2,10},{3,35},{4,12},{5,37},{6,14},{7,39},{8,16},{9,4... | collective-permute-start | bytes 393224 | tf_op jit(solution)/shard_map/ppermute | solution.py:42
  25.0 4.7 %collective-permute-start.2 = (bf16[256,256]{1,0:T(8,128)(2,1)S(1)}, bf16[256,256]{1,0:T(8,128)(2,1)S(1)}, u32[]{:S(2)}, u32[]{:S(2)}) collective-permute-start(bf16[256,256]{1,0:T(8,128)(2,1)S(1)} %get-tuple-element.30), channel_id=1, source_target_pairs={{0,24},{1,97},{2,26},{3,99},{4,28},{5,101},{6,30},{7,103},{8,0},{9... | collective-permute-start | bytes 393224 | tf_op jit(solution)/shard_map/ppermute | solution.py:42
  29.8 15.8 %collective-permute-start.5 = (bf16[4,256,256]{2,1,0:T(8,128)(2,1)S(1)}, bf16[4,256,256]{2,1,0:T(8,128)(2,1)S(1)}, u32[]{:S(2)}, u32[]{:S(2)}) collective-permute-start(bf16[4,256,256]{2,1,0:T(8,128)(2,1)S(1)} %pad_maximum_fusion.a0), channel_id=1, source_target_pairs={{0,96},{1,25},{2,98},{3,27},{4,100},{5,29},{6,102},{7,31},{8,104},... | collective-permute-start | bytes 1572872 | tf_op jit(solution)/shard_map/ppermute | solution.py:42
  33.8 12.5 %collective-permute-start.4 = (bf16[4,256,256]{2,1,0:T(8,128)(2,1)S(1)}, bf16[4,256,256]{2,1,0:T(8,128)(2,1)}, u32[]{:S(2)}, u32[]{:S(2)}) collective-permute-start(bf16[4,256,256]{2,1,0:T(8,128)(2,1)S(1)} %pad_maximum_fusion.a0), channel_id=1, source_target_pairs={{0,64},{1,17},{2,66},{3,19},{4,68},{5,21},{6,70},{7,23},{8,72},{9,... | collective-permute-start | bytes 1572872 | tf_op jit(solution)/shard_map/ppermute | solution.py:42
  33.8 15.3 %collective-permute-start.3 = (bf16[4,256,256]{2,1,0:T(8,128)(2,1)S(1)}, bf16[4,256,256]{2,1,0:T(8,128)(2,1)}, u32[]{:S(2)}, u32[]{:S(2)}) collective-permute-start(bf16[4,256,256]{2,1,0:T(8,128)(2,1)S(1)} %pad_maximum_fusion.a0), channel_id=1, source_target_pairs={{0,32},{1,9},{2,34},{3,11},{4,36},{5,13},{6,38},{7,15},{8,40},{9,1... | collective-permute-start | bytes 1572872 | tf_op jit(solution)/shard_map/ppermute | solution.py:42
  45.6 0.8 copy-start.3
  49.1 1.0 copy-start.4
  68.0 0.7 copy-start.1
  68.7 15.5 %collective-permute-start.6 = (bf16[4,256,256]{2,1,0:T(8,128)(2,1)}, bf16[4,256,256]{2,1,0:T(8,128)(2,1)S(1)}, u32[]{:S(2)}, u32[]{:S(2)}) collective-permute-start(bf16[4,256,256]{2,1,0:T(8,128)(2,1)} %get-tuple-element.16), channel_id=1, source_target_pairs={{0,32},{1,9},{2,34},{3,11},{4,36},{5,13},{6,38},{7,15},{8,40},{9,1... | collective-permute-start | bytes 1572872 | tf_op jit(solution)/shard_map/ppermute | solution.py:42
  68.7 15.5 %collective-permute-start.7 = (bf16[4,256,256]{2,1,0:T(8,128)(2,1)}, bf16[4,256,256]{2,1,0:T(8,128)(2,1)}, u32[]{:S(2)}, u32[]{:S(2)}) collective-permute-start(bf16[4,256,256]{2,1,0:T(8,128)(2,1)} %get-tuple-element.17), channel_id=1, source_target_pairs={{0,64},{1,17},{2,66},{3,19},{4,68},{5,21},{6,70},{7,23},{8,72},{9,... | collective-permute-start | bytes 1572872 | tf_op jit(solution)/shard_map/ppermute | solution.py:42
  71.0 13.8 %collective-permute-start.8 = (bf16[4,256,256]{2,1,0:T(8,128)(2,1)}, bf16[4,256,256]{2,1,0:T(8,128)(2,1)}, u32[]{:S(2)}, u32[]{:S(2)}) collective-permute-start(bf16[4,256,256]{2,1,0:T(8,128)(2,1)} %get-tuple-element.18), channel_id=1, source_target_pairs={{0,96},{1,25},{2,98},{3,27},{4,100},{5,29},{6,102},{7,31},{8,104},... | collective-permute-start | bytes 1572872 | tf_op jit(solution)/shard_map/ppermute | solution.py:42
  71.4 28.7 %all-to-all-start.2 = ((bf16[8,96,1024]{2,1,0:T(8,128)(2,1)}), bf16[8,96,1024]{2,1,0:T(8,128)(2,1)S(1)}, u32[]{:S(2)}, u32[]{:S(2)}) async-start(bf16[8,96,1024]{2,1,0:T(8,128)(2,1)} %bitcast.10), calls=%async_computation.2 | async-start | bytes 3145728 | tf_op jit(solution)/shard_map/all_to_all | solution.py:291
  79.4 10.1 %copy-start.2 = (f32[256,256]{1,0:T(8,128)S(1)}, f32[256,256]{1,0:T(8,128)}, u32[]{:S(2)}) copy-start(f32[256,256]{1,0:T(8,128)} %copy-done.1) | copy-start | bytes 786436
  86.2 5.4 %collective-permute-start.9 = (bf16[256,256]{1,0:T(8,128)(2,1)S(1)}, bf16[256,256]{1,0:T(8,128)(2,1)S(1)}, u32[]{:S(2)}, u32[]{:S(2)}) collective-permute-start(bf16[256,256]{1,0:T(8,128)(2,1)S(1)} %get-tuple-element.26), channel_id=1, source_target_pairs={{0,16},{1,65},{2,18},{3,67},{4,20},{5,69},{6,22},{7,71},{8,24},{9,... | collective-permute-start | bytes 393224 | tf_op jit(solution)/shard_map/ppermute | solution.py:42
  87.5 6.1 %collective-permute-start.11 = (bf16[256,256]{1,0:T(8,128)(2,1)S(1)}, bf16[256,256]{1,0:T(8,128)(2,1)S(1)}, u32[]{:S(2)}, u32[]{:S(2)}) collective-permute-start(bf16[256,256]{1,0:T(8,128)(2,1)S(1)} %get-tuple-element.27), channel_id=1, source_target_pairs={{0,24},{1,97},{2,26},{3,99},{4,28},{5,101},{6,30},{7,103},{8,0},{9... | collective-permute-start | bytes 393224 | tf_op jit(solution)/shard_map/ppermute | solution.py:42
  89.0 5.3 %collective-permute-start.10 = (bf16[256,256]{1,0:T(8,128)(2,1)S(1)}, bf16[256,256]{1,0:T(8,128)(2,1)S(1)}, u32[]{:S(2)}, u32[]{:S(2)}) collective-permute-start(bf16[256,256]{1,0:T(8,128)(2,1)S(1)} %get-tuple-element.28), channel_id=1, source_target_pairs={{0,8},{1,33},{2,10},{3,35},{4,12},{5,37},{6,14},{7,39},{8,16},{9,4... | collective-permute-start | bytes 393224 | tf_op jit(solution)/shard_map/ppermute | solution.py:42
  100.1 13.3 %all-to-all-start.3 = ((bf16[8,96,256]{2,1,0:T(8,128)(2,1)}), bf16[8,96,256]{2,1,0:T(8,128)(2,1)S(1)}, u32[]{:S(2)}, u32[]{:S(2)}) async-start(bf16[8,96,256]{2,1,0:T(8,128)(2,1)} %bitcast.16), calls=%async_computation.3 | async-start | bytes 786432 | tf_op jit(solution)/shard_map/all_to_all | solution.py:291

commit v6 on v5

--- a/solution.py
+++ b/solution.py
@@ -24,7 +24,7 @@
     return lax.dot_general(a, b, (((ca,), (cb,)), ((), ())), preferred_element_type=F32)
 
 
-def ring_pairs(side, cores, along, by):
+def ring_pairs(side, cores, along, by, up):
     pairs = []
     for y in range(side):
         for z in range(side):
@@ -32,13 +32,16 @@
                 if (along + h) % 2:
                     to = y * side + (z + by) % side
                 else:
-                    to = (y + by) % side * side + z
+                    to_y = (y + by) % side
+                    if up and 2 * by == side == 4 and to_y < y:
+                        to_y = (0, 1)[to_y == 0]
+                    to = to_y * side + z
                 pairs.append(((y * side + z) * cores + h, to * cores + h))
     return pairs
 
 
-def shifted(x, along, by):
-    pairs = ring_pairs(SIDE, lax.axis_size("head"), along, by)
+def shifted(x, along, by, up):
+    pairs = ring_pairs(SIDE, lax.axis_size("head"), along, by, up)
     return lax.ppermute(x, ("ctx", "head"), pairs)
 
 
@@ -304,9 +307,9 @@
 
     kv = by_head(keys, values)
     first = kv[:BLK]
-    by = {s: shifted(first, 1, s) for s in (2, 1, 3)}
+    by = {s: shifted(first, 1, s, True) for s in (2, 1, 3)}
     line = jnp.stack([first] + [by[s] for s in range(1, SIDE)])
-    by = {s: shifted(line, 0, s) for s in (2, 1, 3)}
+    by = {s: shifted(line, 0, s, True) for s in (2, 1, 3)}
     arrived = [line] + [by[s] for s in range(1, SIDE)]
     qg = by_head(queries, grad_out)
     out, dfirst, drest, *terms = attention(here, parent, qg, kv, arrived, subtree_end.reshape(nb, BLK))
@@ -319,12 +322,12 @@
 
     out = send_back(out)
 
-    by = {s: shifted(terms[s], 0, s) for s in (2, 1, 3)}
+    by = {s: shifted(terms[s], 0, s, False) for s in (2, 1, 3)}
     got = [terms[0]] + [by[s] for s in range(1, SIDE)]
     own = lax.optimization_barrier(dfirst + sum(x[0].astype(F32) for x in got))
     part = sum(x[1:].astype(F32) for x in got).astype(BF16)
     for s in (2, 1, 3):
-        own = own + shifted(part[s - 1], 1, s).astype(F32)
+        own = own + shifted(part[s - 1], 1, s, False).astype(F32)
     dkv = jnp.concatenate([own.astype(BF16), drest], axis=0)
     out, dkv = lax.optimization_barrier((out, dkv))
     attn_out, grad_q = by_token(out)

time: 115 us -> 115 us (level)
  no operation moved by 1% of the time
where the time goes in v6:
time: 115 us
  waiting for transfers between devices  42.8 us (37%)
  starting transfers between devices  39.4 us (34%)
  Pallas kernels  17.9 us (16%)
  local copies, waits for them, and re-layouts  8.21 us (7%)
  other arithmetic  5.55 us (5%)
    ppermute x12, waiting for transfers between devices, shifted(): return lax.ppermute(x, ('ctx', 'head'), pairs)  25.7 us
    all_to_all x4, starting transfers between devices, swap(): return lax.all_to_all(x, 'head', split_axis=0, concat_axis=0, tiled=True)  23 us
    pallas_call x1, Pallas kernels, attention(): pl.pallas_call(functools.partial(attention_kernel, nb), grid_spec=spec, o...  17.9 us
    all_to_all x4, waiting for transfers between devices, swap(): return lax.all_to_all(x, 'head', split_axis=0, concat_axis=0, tiled=True)  17.1 us
    ppermute x12, starting transfers between devices, shifted(): return lax.ppermute(x, ('ctx', 'head'), pairs)  16.4 us
    unnamed x20, local copies, waits for them, and re-layouts  3.66 us
    reshape x4, local copies, waits for them, and re-layouts, by_token(): a.reshape(rows, -1)  3.34 us
  transfers between devices with their start and end apart: 16, of which 11 were waited for; matrix products, arithmetic and copies ran while one was open for 6% of the time, Pallas kernels for 0%

profile of v6, /device:TPU:1, one launch (start us, length us, event | category | flops | bytes accessed | tf_op | source)
XLA Modules:
  0.0 114.6 jit_solution(12615371128071828381)
XLA Ops:
  0.6 0.0 copy-start
  0.6 0.0 copy-start.6
  0.7 0.0 copy-start.7
  0.7 0.9 copy-done
  1.6 1.0 copy_bitcast_fusion.4
  2.6 0.8 maximum_bitcast_fusion.1
  3.4 5.8 %all-to-all-start.1 = ((bf16[8,96,256]{2,1,0:T(8,128)(2,1)}), bf16[8,96,256]{2,1,0:T(8,128)(2,1)S(1)}, u32[]{:S(2)}, u32[]{:S(2)}) async-start(bf16[8,96,256]{2,1,0:T(8,128)(2,1)} %maximum_bitcast_fusion.1), calls=%async_computation.1 | async-start | bytes 786432 | tf_op jit(solution)/shard_map/all_to_all | solution.py:294
  9.2 0.0 copy-done.6
  9.2 0.0 copy-done.7
  9.2 0.2 copy_bitcast_fusion
  9.3 1.4 %maximum_bitcast_fusion = bf16[8,96,1024]{2,1,0:T(8,128)(2,1)} fusion(bf16[96,8,512]{2,0,1:T(8,128)(2,1)S(1)} %get-tuple-element.31, bf16[96,8,512]{2,0,1:T(8,128)(2,1)S(1)} %get-tuple-element.32), kind=kLoop, calls=%fused_computation | loop fusion | flops 3145728 | bytes 3145728 | tf_op jit(solution)/shard_map/transpose | solution.py:306
  10.7 0.0 copy-start.8
  10.7 0.0 copy-start.5
  10.7 6.5 %all-to-all-done.1 = bf16[8,96,256]{2,1,0:T(8,128)(2,1)S(1)} async-done(((bf16[8,96,256]{2,1,0:T(8,128)(2,1)}), bf16[8,96,256]{2,1,0:T(8,128)(2,1)S(1)}, u32[]{:S(2)}, u32[]{:S(2)}) %all-to-all-start.1) | async-done | bytes 393248 | tf_op jit(solution)/shard_map/all_to_all | solution.py:294
  17.2 4.4 %all-to-all-start = ((bf16[8,96,1024]{2,1,0:T(8,128)(2,1)}), bf16[8,96,1024]{2,1,0:T(8,128)(2,1)S(1)}, u32[]{:S(2)}, u32[]{:S(2)}) async-start(bf16[8,96,1024]{2,1,0:T(8,128)(2,1)} %maximum_bitcast_fusion), calls=%async_computation | async-start | bytes 3145728 | tf_op jit(solution)/shard_map/all_to_all | solution.py:294
  21.6 3.0 %collective-permute-start.1 = (bf16[256,256]{1,0:T(8,128)(2,1)S(1)}, bf16[256,256]{1,0:T(8,128)(2,1)S(1)}, u32[]{:S(2)}, u32[]{:S(2)}) collective-permute-start(bf16[256,256]{1,0:T(8,128)(2,1)S(1)} %get-tuple-element.30), channel_id=1, source_target_pairs={{0,16},{1,65},{2,18},{3,67},{4,20},{5,69},{6,22},{7,71},{8,24},{9,... | collective-permute-start | bytes 393224 | tf_op jit(solution)/shard_map/ppermute | solution.py:45
  24.6 0.4 collective-permute-start
  25.0 2.3 %collective-permute-start.2 = (bf16[256,256]{1,0:T(8,128)(2,1)S(1)}, bf16[256,256]{1,0:T(8,128)(2,1)S(1)}, u32[]{:S(2)}, u32[]{:S(2)}) collective-permute-start(bf16[256,256]{1,0:T(8,128)(2,1)S(1)} %get-tuple-element.30), channel_id=1, source_target_pairs={{0,24},{1,97},{2,26},{3,99},{4,28},{5,101},{6,30},{7,103},{8,0},{9... | collective-permute-start | bytes 393224 | tf_op jit(solution)/shard_map/ppermute | solution.py:45
  27.3 0.0 collective-permute-done.1
  27.3 2.4 %collective-permute-done = bf16[256,256]{1,0:T(8,128)(2,1)S(1)} collective-permute-done((bf16[256,256]{1,0:T(8,128)(2,1)S(1)}, bf16[256,256]{1,0:T(8,128)(2,1)S(1)}, u32[]{:S(2)}, u32[]{:S(2)}) %collective-permute-start) | collective-permute-done | bytes 131104 | tf_op jit(solution)/shard_map/ppermute | solution.py:45
  29.7 0.0 collective-permute-done.2
  29.7 0.1 pad_maximum_fusion.a0
  29.8 4.1 %collective-permute-start.5 = (bf16[4,256,256]{2,1,0:T(8,128)(2,1)S(1)}, bf16[4,256,256]{2,1,0:T(8,128)(2,1)S(1)}, u32[]{:S(2)}, u32[]{:S(2)}) collective-permute-start(bf16[4,256,256]{2,1,0:T(8,128)(2,1)S(1)} %pad_maximum_fusion.a0), channel_id=1, source_target_pairs={{0,96},{1,25},{2,98},{3,27},{4,100},{5,29},{6,102},{7,31},{8,104},... | collective-permute-start | bytes 1572872 | tf_op jit(solution)/shard_map/ppermute | solution.py:45
  33.8 0.0 collective-permute-start.4
  33.8 0.7 collective-permute-start.3
  34.5 0.0 copy-done.8
  34.5 0.1 pad_add_fusion.here
  34.6 11.0 %collective-permute-done.5.a3 = bf16[4,256,256]{2,1,0:T(8,128)(2,1)S(1)} collective-permute-done((bf16[4,256,256]{2,1,0:T(8,128)(2,1)S(1)}, bf16[4,256,256]{2,1,0:T(8,128)(2,1)S(1)}, u32[]{:S(2)}, u32[]{:S(2)}) %collective-permute-start.5) | collective-permute-done | bytes 524320 | tf_op jit(solution)/shard_map/ppermute | solution.py:45
  45.6 0.8 copy-done.3
  46.4 0.0 collective-permute-done.4.a2
  46.4 2.7 %collective-permute-done.3.a1 = bf16[4,256,256]{2,1,0:T(8,128)(2,1)} collective-permute-done((bf16[4,256,256]{2,1,0:T(8,128)(2,1)S(1)}, bf16[4,256,256]{2,1,0:T(8,128)(2,1)}, u32[]{:S(2)}, u32[]{:S(2)}) %collective-permute-start.3) | collective-permute-done | bytes 524320 | tf_op jit(solution)/shard_map/ppermute | solution.py:45
  49.1 0.0 all-to-all-done
  49.1 0.0 copy-done.5
  49.1 1.0 copy-done.4
  50.1 17.9 %tree_attention.1 = (bf16[768,1024]{1,0:T(8,128)(2,1)}, f32[256,256]{1,0:T(8,128)S(1)}, bf16[512,256]{1,0:T(8,128)(2,1)S(1)}, bf16[4,256,256]{2,1,0:T(8,128)(2,1...) custom-call(s32[2]{0:T(128)S(1)} %pad_add_fusion.here, ...), custom_call_target="tpu_custom_call" | custom-call | flops 7247757312 | bytes 3145728 | tf_op jit(solution)/shard_map/tree_attention/pallas_call | solution.py:276
  68.0 0.0 copy-start.1
  68.0 0.7 copy-done.1
  68.7 0.0 collective-permute-start.6
  68.7 2.3 %collective-permute-start.7 = (bf16[4,256,256]{2,1,0:T(8,128)(2,1)}, bf16[4,256,256]{2,1,0:T(8,128)(2,1)}, u32[]{:S(2)}, u32[]{:S(2)}) collective-permute-start(bf16[4,256,256]{2,1,0:T(8,128)(2,1)} %get-tuple-element.17), channel_id=1, source_target_pairs={{0,64},{1,17},{2,66},{3,19},{4,68},{5,21},{6,70},{7,23},{8,72},{9,... | collective-permute-start | bytes 1572872 | tf_op jit(solution)/shard_map/ppermute | solution.py:45
  71.0 0.4 collective-permute-start.8
  71.4 7.6 %all-to-all-start.2 = ((bf16[8,96,1024]{2,1,0:T(8,128)(2,1)}), bf16[8,96,1024]{2,1,0:T(8,128)(2,1)S(1)}, u32[]{:S(2)}, u32[]{:S(2)}) async-start(bf16[8,96,1024]{2,1,0:T(8,128)(2,1)} %bitcast.10), calls=%async_computation.2 | async-start | bytes 3145728 | tf_op jit(solution)/shard_map/all_to_all | solution.py:294
  79.0 5.2 %collective-permute-done.6 = bf16[4,256,256]{2,1,0:T(8,128)(2,1)S(1)} collective-permute-done((bf16[4,256,256]{2,1,0:T(8,128)(2,1)}, bf16[4,256,256]{2,1,0:T(8,128)(2,1)S(1)}, u32[]{:S(2)}, u32[]{:S(2)}) %collective-permute-start.6) | collective-permute-done | bytes 524320 | tf_op jit(solution)/shard_map/ppermute | solution.py:45
  84.2 0.0 collective-permute-done.7
  84.2 0.6 collective-permute-done.8
  84.8 1.3 %add_convert_fusion = bf16[3,256,256]{2,1,0:T(8,128)(2,1)S(1)} fusion(bf16[4,256,256]{2,1,0:T(8,128)(2,1)} %collective-permute-done.8, bf16[4,256,256]{2,1,0:T(8,128)(2,1)} %collective-permute-done.7, bf16[4,256,256]{2,1,0:T(8,128)(2,1)S(1)} %collective-permute-done.6, bf16[4,256,256]{2,1,0:T(8,128)(2,1)S(1)} %get-tuple-element.15), kind=kLoop, calls=%fused_computation.5 | loop fusion | flops 1572864 | bytes 1966080 | tf_op jit(solution)/shard_map/convert_element_type | solution.py:328
  86.2 1.3 %collective-permute-start.9 = (bf16[256,256]{1,0:T(8,128)(2,1)S(1)}, bf16[256,256]{1,0:T(8,128)(2,1)S(1)}, u32[]{:S(2)}, u32[]{:S(2)}) collective-permute-start(bf16[256,256]{1,0:T(8,128)(2,1)S(1)} %get-tuple-element.26), channel_id=1, source_target_pairs={{0,16},{1,65},{2,18},{3,67},{4,20},{5,69},{6,22},{7,71},{8,24},{9,... | collective-permute-start | bytes 393224 | tf_op jit(solution)/shard_map/ppermute | solution.py:45
  87.5 1.6 %collective-permute-start.11 = (bf16[256,256]{1,0:T(8,128)(2,1)S(1)}, bf16[256,256]{1,0:T(8,128)(2,1)S(1)}, u32[]{:S(2)}, u32[]{:S(2)}) collective-permute-start(bf16[256,256]{1,0:T(8,128)(2,1)S(1)} %get-tuple-element.27), channel_id=1, source_target_pairs={{0,24},{1,97},{2,26},{3,99},{4,28},{5,101},{6,30},{7,103},{8,0},{9... | collective-permute-start | bytes 393224 | tf_op jit(solution)/shard_map/ppermute | solution.py:45
  89.0 0.5 collective-permute-start.10
  89.5 0.0 copy-done.2
  89.5 1.1 bitcast_add_fusion
  90.6 1.0 collective-permute-done.9
  91.6 2.0 %collective-permute-done.11 = bf16[256,256]{1,0:T(8,128)(2,1)S(1)} collective-permute-done((bf16[256,256]{1,0:T(8,128)(2,1)S(1)}, bf16[256,256]{1,0:T(8,128)(2,1)S(1)}, u32[]{:S(2)}, u32[]{:S(2)}) %collective-permute-start.11) | collective-permute-done | bytes 131104 | tf_op jit(solution)/shard_map/ppermute | solution.py:45
  93.6 0.7 collective-permute-done.10
  94.4 0.1 add_convert_fusion.1
  94.4 0.8 pad_maximum_fusion.1
  95.2 4.5 %all-to-all-done.2 = bf16[8,96,1024]{2,1,0:T(8,128)(2,1)S(1)} async-done(((bf16[8,96,1024]{2,1,0:T(8,128)(2,1)}), bf16[8,96,1024]{2,1,0:T(8,128)(2,1)S(1)}, u32[]{:S(2)}, u32[]{:S(2)}) %all-to-all-start.2) | async-done | bytes 1572896 | tf_op jit(solution)/shard_map/all_to_all | solution.py:294
  99.7 5.2 %all-to-all-start.3 = ((bf16[8,96,256]{2,1,0:T(8,128)(2,1)}), bf16[8,96,256]{2,1,0:T(8,128)(2,1)S(1)}, u32[]{:S(2)}, u32[]{:S(2)}) async-start(bf16[8,96,256]{2,1,0:T(8,128)(2,1)} %bitcast.16), calls=%async_computation.3 | async-start | bytes 786432 | tf_op jit(solution)/shard_map/all_to_all | solution.py:294
  105.0 0.1 slice_bitcast_fusion
  105.1 0.9 copy.23
  106.1 0.9 copy.22
  107.0 6.0 %all-to-all-done.3 = bf16[8,96,256]{2,1,0:T(8,128)(2,1)S(1)} async-done(((bf16[8,96,256]{2,1,0:T(8,128)(2,1)}), bf16[8,96,256]{2,1,0:T(8,128)(2,1)S(1)}, u32[]{:S(2)}, u32[]{:S(2)}) %all-to-all-start.3) | async-done | bytes 393248 | tf_op jit(solution)/shard_map/all_to_all | solution.py:294
  113.1 0.1 slice_bitcast_fusion.2
  113.1 0.7 copy.32
  113.9 0.7 copy.33
  (6 shorter events, 0.1 us)
Async XLA Ops:
  0.6 0.9 copy-start
  0.6 8.5 %copy-start.6 = (bf16[96,4096]{1,0:T(8,128)(2,1)S(1)}, bf16[96,4096]{1,0:T(8,128)(2,1)}, u32[]{:S(2)}) copy-start(bf16[96,4096]{1,0:T(8,128)(2,1)} %param.9) | copy-start | bytes 2359300
  0.7 8.5 %copy-start.7 = (bf16[96,4096]{1,0:T(8,128)(2,1)S(1)}, bf16[96,4096]{1,0:T(8,128)(2,1)}, u32[]{:S(2)}) copy-start(bf16[96,4096]{1,0:T(8,128)(2,1)} %param.6) | copy-start | bytes 2359300
  3.4 13.9 %all-to-all-start.1 = ((bf16[8,96,256]{2,1,0:T(8,128)(2,1)}), bf16[8,96,256]{2,1,0:T(8,128)(2,1)S(1)}, u32[]{:S(2)}, u32[]{:S(2)}) async-start(bf16[8,96,256]{2,1,0:T(8,128)(2,1)} %maximum_bitcast_fusion.1), calls=%async_computation.1 | async-start | bytes 786432 | tf_op jit(solution)/shard_map/all_to_all | solution.py:294
  10.7 23.8 %copy-start.8 = (s32[768]{0:T(1024)S(1)}, s32[768]{0:T(1024)}, u32[]{:S(2)}) copy-start(s32[768]{0:T(1024)} %param.11) | copy-start | bytes 9220
  10.7 38.4 %copy-start.5 = (s32[48]{0:T(128)S(1)}, s32[48]{0:T(128)}, u32[]{:S(2)}) copy-start(s32[48]{0:T(128)} %parent.1) | copy-start | bytes 580
  17.2 31.9 %all-to-all-start = ((bf16[8,96,1024]{2,1,0:T(8,128)(2,1)}), bf16[8,96,1024]{2,1,0:T(8,128)(2,1)S(1)}, u32[]{:S(2)}, u32[]{:S(2)}) async-start(bf16[8,96,1024]{2,1,0:T(8,128)(2,1)} %maximum_bitcast_fusion), calls=%async_computation | async-start | bytes 3145728 | tf_op jit(solution)/shard_map/all_to_all | solution.py:294
  21.6 5.7 %collective-permute-start.1 = (bf16[256,256]{1,0:T(8,128)(2,1)S(1)}, bf16[256,256]{1,0:T(8,128)(2,1)S(1)}, u32[]{:S(2)}, u32[]{:S(2)}) collective-permute-start(bf16[256,256]{1,0:T(8,128)(2,1)S(1)} %get-tuple-element.30), channel_id=1, source_target_pairs={{0,16},{1,65},{2,18},{3,67},{4,20},{5,69},{6,22},{7,71},{8,24},{9,... | collective-permute-start | bytes 393224 | tf_op jit(solution)/shard_map/ppermute | solution.py:45
  24.6 5.1 %collective-permute-start = (bf16[256,256]{1,0:T(8,128)(2,1)S(1)}, bf16[256,256]{1,0:T(8,128)(2,1)S(1)}, u32[]{:S(2)}, u32[]{:S(2)}) collective-permute-start(bf16[256,256]{1,0:T(8,128)(2,1)S(1)} %get-tuple-element.30), channel_id=1, source_target_pairs={{0,8},{1,33},{2,10},{3,35},{4,12},{5,37},{6,14},{7,39},{8,16},{9,4... | collective-permute-start | bytes 393224 | tf_op jit(solution)/shard_map/ppermute | solution.py:45
  25.0 4.7 %collective-permute-start.2 = (bf16[256,256]{1,0:T(8,128)(2,1)S(1)}, bf16[256,256]{1,0:T(8,128)(2,1)S(1)}, u32[]{:S(2)}, u32[]{:S(2)}) collective-permute-start(bf16[256,256]{1,0:T(8,128)(2,1)S(1)} %get-tuple-element.30), channel_id=1, source_target_pairs={{0,24},{1,97},{2,26},{3,99},{4,28},{5,101},{6,30},{7,103},{8,0},{9... | collective-permute-start | bytes 393224 | tf_op jit(solution)/shard_map/ppermute | solution.py:45
  29.8 15.8 %collective-permute-start.5 = (bf16[4,256,256]{2,1,0:T(8,128)(2,1)S(1)}, bf16[4,256,256]{2,1,0:T(8,128)(2,1)S(1)}, u32[]{:S(2)}, u32[]{:S(2)}) collective-permute-start(bf16[4,256,256]{2,1,0:T(8,128)(2,1)S(1)} %pad_maximum_fusion.a0), channel_id=1, source_target_pairs={{0,96},{1,25},{2,98},{3,27},{4,100},{5,29},{6,102},{7,31},{8,104},... | collective-permute-start | bytes 1572872 | tf_op jit(solution)/shard_map/ppermute | solution.py:45
  33.8 12.5 %collective-permute-start.4 = (bf16[4,256,256]{2,1,0:T(8,128)(2,1)S(1)}, bf16[4,256,256]{2,1,0:T(8,128)(2,1)}, u32[]{:S(2)}, u32[]{:S(2)}) collective-permute-start(bf16[4,256,256]{2,1,0:T(8,128)(2,1)S(1)} %pad_maximum_fusion.a0), channel_id=1, source_target_pairs={{0,64},{1,17},{2,66},{3,19},{4,68},{5,21},{6,70},{7,23},{8,72},{9,... | collective-permute-start | bytes 1572872 | tf_op jit(solution)/shard_map/ppermute | solution.py:45
  33.8 15.3 %collective-permute-start.3 = (bf16[4,256,256]{2,1,0:T(8,128)(2,1)S(1)}, bf16[4,256,256]{2,1,0:T(8,128)(2,1)}, u32[]{:S(2)}, u32[]{:S(2)}) collective-permute-start(bf16[4,256,256]{2,1,0:T(8,128)(2,1)S(1)} %pad_maximum_fusion.a0), channel_id=1, source_target_pairs={{0,32},{1,9},{2,34},{3,11},{4,36},{5,13},{6,38},{7,15},{8,40},{9,1... | collective-permute-start | bytes 1572872 | tf_op jit(solution)/shard_map/ppermute | solution.py:45
  45.6 0.8 copy-start.3
  49.1 1.0 copy-start.4
  68.0 0.7 copy-start.1
  68.7 15.5 %collective-permute-start.6 = (bf16[4,256,256]{2,1,0:T(8,128)(2,1)}, bf16[4,256,256]{2,1,0:T(8,128)(2,1)S(1)}, u32[]{:S(2)}, u32[]{:S(2)}) collective-permute-start(bf16[4,256,256]{2,1,0:T(8,128)(2,1)} %get-tuple-element.16), channel_id=1, source_target_pairs={{0,32},{1,9},{2,34},{3,11},{4,36},{5,13},{6,38},{7,15},{8,40},{9,1... | collective-permute-start | bytes 1572872 | tf_op jit(solution)/shard_map/ppermute | solution.py:45
  68.7 15.5 %collective-permute-start.7 = (bf16[4,256,256]{2,1,0:T(8,128)(2,1)}, bf16[4,256,256]{2,1,0:T(8,128)(2,1)}, u32[]{:S(2)}, u32[]{:S(2)}) collective-permute-start(bf16[4,256,256]{2,1,0:T(8,128)(2,1)} %get-tuple-element.17), channel_id=1, source_target_pairs={{0,64},{1,17},{2,66},{3,19},{4,68},{5,21},{6,70},{7,23},{8,72},{9,... | collective-permute-start | bytes 1572872 | tf_op jit(solution)/shard_map/ppermute | solution.py:45
  71.0 13.8 %collective-permute-start.8 = (bf16[4,256,256]{2,1,0:T(8,128)(2,1)}, bf16[4,256,256]{2,1,0:T(8,128)(2,1)}, u32[]{:S(2)}, u32[]{:S(2)}) collective-permute-start(bf16[4,256,256]{2,1,0:T(8,128)(2,1)} %get-tuple-element.18), channel_id=1, source_target_pairs={{0,96},{1,25},{2,98},{3,27},{4,100},{5,29},{6,102},{7,31},{8,104},... | collective-permute-start | bytes 1572872 | tf_op jit(solution)/shard_map/ppermute | solution.py:45
  71.4 28.3 %all-to-all-start.2 = ((bf16[8,96,1024]{2,1,0:T(8,128)(2,1)}), bf16[8,96,1024]{2,1,0:T(8,128)(2,1)S(1)}, u32[]{:S(2)}, u32[]{:S(2)}) async-start(bf16[8,96,1024]{2,1,0:T(8,128)(2,1)} %bitcast.10), calls=%async_computation.2 | async-start | bytes 3145728 | tf_op jit(solution)/shard_map/all_to_all | solution.py:294
  79.0 10.5 %copy-start.2 = (f32[256,256]{1,0:T(8,128)S(1)}, f32[256,256]{1,0:T(8,128)}, u32[]{:S(2)}) copy-start(f32[256,256]{1,0:T(8,128)} %copy-done.1) | copy-start | bytes 786436
  86.2 5.4 %collective-permute-start.9 = (bf16[256,256]{1,0:T(8,128)(2,1)S(1)}, bf16[256,256]{1,0:T(8,128)(2,1)S(1)}, u32[]{:S(2)}, u32[]{:S(2)}) collective-permute-start(bf16[256,256]{1,0:T(8,128)(2,1)S(1)} %get-tuple-element.26), channel_id=1, source_target_pairs={{0,16},{1,65},{2,18},{3,67},{4,20},{5,69},{6,22},{7,71},{8,24},{9,... | collective-permute-start | bytes 393224 | tf_op jit(solution)/shard_map/ppermute | solution.py:45
  87.5 6.1 %collective-permute-start.11 = (bf16[256,256]{1,0:T(8,128)(2,1)S(1)}, bf16[256,256]{1,0:T(8,128)(2,1)S(1)}, u32[]{:S(2)}, u32[]{:S(2)}) collective-permute-start(bf16[256,256]{1,0:T(8,128)(2,1)S(1)} %get-tuple-element.27), channel_id=1, source_target_pairs={{0,24},{1,97},{2,26},{3,99},{4,28},{5,101},{6,30},{7,103},{8,0},{9... | collective-permute-start | bytes 393224 | tf_op jit(solution)/shard_map/ppermute | solution.py:45
  89.0 5.3 %collective-permute-start.10 = (bf16[256,256]{1,0:T(8,128)(2,1)S(1)}, bf16[256,256]{1,0:T(8,128)(2,1)S(1)}, u32[]{:S(2)}, u32[]{:S(2)}) collective-permute-start(bf16[256,256]{1,0:T(8,128)(2,1)S(1)} %get-tuple-element.28), channel_id=1, source_target_pairs={{0,8},{1,33},{2,10},{3,35},{4,12},{5,37},{6,14},{7,39},{8,16},{9,4... | collective-permute-start | bytes 393224 | tf_op jit(solution)/shard_map/ppermute | solution.py:45
  99.7 13.3 %all-to-all-start.3 = ((bf16[8,96,256]{2,1,0:T(8,128)(2,1)}), bf16[8,96,256]{2,1,0:T(8,128)(2,1)S(1)}, u32[]{:S(2)}, u32[]{:S(2)}) async-start(bf16[8,96,256]{2,1,0:T(8,128)(2,1)} %bitcast.16), calls=%async_computation.3 | async-start | bytes 786432 | tf_op jit(solution)/shard_map/all_to_all | solution.py:294

commit v7 on v6

--- a/solution.py
+++ b/solution.py
@@ -33,8 +33,8 @@
                     to = y * side + (z + by) % side
                 else:
                     to_y = (y + by) % side
-                    if up and 2 * by == side == 4 and to_y < y:
-                        to_y = (0, 1)[to_y == 0]
+                    if 2 * by == side == 4 and (to_y < y) == up:
+                        to_y = to_y ^ 1
                     to = to_y * side + z
                 pairs.append(((y * side + z) * cores + h, to * cores + h))
     return pairs

time: 115 us -> 114 us (level)
  no operation moved by 1% of the time
where the time goes in v7:
time: 114 us
  waiting for transfers between devices  42 us (37%)
  starting transfers between devices  39.2 us (34%)
  Pallas kernels  17.9 us (16%)
  local copies, waits for them, and re-layouts  8.21 us (7%)
  other arithmetic  5.55 us (5%)
    ppermute x12, waiting for transfers between devices, shifted(): return lax.ppermute(x, ('ctx', 'head'), pairs)  24.8 us
    all_to_all x4, starting transfers between devices, swap(): return lax.all_to_all(x, 'head', split_axis=0, concat_axis=0, tiled=True)  22 us
    pallas_call x1, Pallas kernels, attention(): pl.pallas_call(functools.partial(attention_kernel, nb), grid_spec=spec, o...  17.9 us
    ppermute x12, starting transfers between devices, shifted(): return lax.ppermute(x, ('ctx', 'head'), pairs)  17.2 us
    all_to_all x4, waiting for transfers between devices, swap(): return lax.all_to_all(x, 'head', split_axis=0, concat_axis=0, tiled=True)  17.1 us
    unnamed x20, local copies, waits for them, and re-layouts  3.66 us
    reshape x4, local copies, waits for them, and re-layouts, by_token(): a.reshape(rows, -1)  3.34 us
  transfers between devices with their start and end apart: 16, of which 11 were waited for; matrix products, arithmetic and copies ran while one was open for 6% of the time, Pallas kernels for 0%

profile of v7, /device:TPU:1, one launch (start us, length us, event | category | flops | bytes accessed | tf_op | source)
XLA Modules:
  0.0 113.6 jit_solution(8383940940138557029)
XLA Ops:
  0.6 0.0 copy-start
  0.6 0.0 copy-start.6
  0.7 0.0 copy-start.7
  0.7 0.9 copy-done
  1.6 1.0 copy_bitcast_fusion.4
  2.6 0.8 maximum_bitcast_fusion.1
  3.4 5.8 %all-to-all-start.1 = ((bf16[8,96,256]{2,1,0:T(8,128)(2,1)}), bf16[8,96,256]{2,1,0:T(8,128)(2,1)S(1)}, u32[]{:S(2)}, u32[]{:S(2)}) async-start(bf16[8,96,256]{2,1,0:T(8,128)(2,1)} %maximum_bitcast_fusion.1), calls=%async_computation.1 | async-start | bytes 786432 | tf_op jit(solution)/shard_map/all_to_all | solution.py:294
  9.2 0.0 copy-done.6
  9.2 0.0 copy-done.7
  9.2 0.2 copy_bitcast_fusion
  9.3 1.4 %maximum_bitcast_fusion = bf16[8,96,1024]{2,1,0:T(8,128)(2,1)} fusion(bf16[96,8,512]{2,0,1:T(8,128)(2,1)S(1)} %get-tuple-element.31, bf16[96,8,512]{2,0,1:T(8,128)(2,1)S(1)} %get-tuple-element.32), kind=kLoop, calls=%fused_computation | loop fusion | flops 3145728 | bytes 3145728 | tf_op jit(solution)/shard_map/transpose | solution.py:306
  10.7 0.0 copy-start.5
  10.7 6.5 %all-to-all-done.1 = bf16[8,96,256]{2,1,0:T(8,128)(2,1)S(1)} async-done(((bf16[8,96,256]{2,1,0:T(8,128)(2,1)}), bf16[8,96,256]{2,1,0:T(8,128)(2,1)S(1)}, u32[]{:S(2)}, u32[]{:S(2)}) %all-to-all-start.1) | async-done | bytes 393248 | tf_op jit(solution)/shard_map/all_to_all | solution.py:294
  17.2 4.4 %all-to-all-start = ((bf16[8,96,1024]{2,1,0:T(8,128)(2,1)}), bf16[8,96,1024]{2,1,0:T(8,128)(2,1)S(1)}, u32[]{:S(2)}, u32[]{:S(2)}) async-start(bf16[8,96,1024]{2,1,0:T(8,128)(2,1)} %maximum_bitcast_fusion), calls=%async_computation | async-start | bytes 3145728 | tf_op jit(solution)/shard_map/all_to_all | solution.py:294
  21.6 3.0 %collective-permute-start.1 = (bf16[256,256]{1,0:T(8,128)(2,1)S(1)}, bf16[256,256]{1,0:T(8,128)(2,1)S(1)}, u32[]{:S(2)}, u32[]{:S(2)}) collective-permute-start(bf16[256,256]{1,0:T(8,128)(2,1)S(1)} %get-tuple-element.30), channel_id=1, source_target_pairs={{0,16},{1,65},{2,18},{3,67},{4,20},{5,69},{6,22},{7,71},{8,24},{9,... | collective-permute-start | bytes 393224 | tf_op jit(solution)/shard_map/ppermute | solution.py:45
  24.6 0.4 collective-permute-start
  25.0 2.3 %collective-permute-start.2 = (bf16[256,256]{1,0:T(8,128)(2,1)S(1)}, bf16[256,256]{1,0:T(8,128)(2,1)S(1)}, u32[]{:S(2)}, u32[]{:S(2)}) collective-permute-start(bf16[256,256]{1,0:T(8,128)(2,1)S(1)} %get-tuple-element.30), channel_id=1, source_target_pairs={{0,24},{1,97},{2,26},{3,99},{4,28},{5,101},{6,30},{7,103},{8,0},{9... | collective-permute-start | bytes 393224 | tf_op jit(solution)/shard_map/ppermute | solution.py:45
  27.3 0.0 collective-permute-done.1
  27.3 2.4 %collective-permute-done = bf16[256,256]{1,0:T(8,128)(2,1)S(1)} collective-permute-done((bf16[256,256]{1,0:T(8,128)(2,1)S(1)}, bf16[256,256]{1,0:T(8,128)(2,1)S(1)}, u32[]{:S(2)}, u32[]{:S(2)}) %collective-permute-start) | collective-permute-done | bytes 131104 | tf_op jit(solution)/shard_map/ppermute | solution.py:45
  29.7 0.0 collective-permute-done.2
  29.7 0.1 pad_maximum_fusion.a0
  29.8 4.1 %collective-permute-start.5 = (bf16[4,256,256]{2,1,0:T(8,128)(2,1)S(1)}, bf16[4,256,256]{2,1,0:T(8,128)(2,1)S(1)}, u32[]{:S(2)}, u32[]{:S(2)}) collective-permute-start(bf16[4,256,256]{2,1,0:T(8,128)(2,1)S(1)} %pad_maximum_fusion.a0), channel_id=1, source_target_pairs={{0,96},{1,25},{2,98},{3,27},{4,100},{5,29},{6,102},{7,31},{8,104},... | collective-permute-start | bytes 1572872 | tf_op jit(solution)/shard_map/ppermute | solution.py:45
  33.8 0.0 collective-permute-start.4
  33.8 0.7 collective-permute-start.3
  34.5 0.0 copy-done.8
  34.5 0.1 pad_add_fusion.here
  34.6 11.0 %collective-permute-done.5.a3 = bf16[4,256,256]{2,1,0:T(8,128)(2,1)S(1)} collective-permute-done((bf16[4,256,256]{2,1,0:T(8,128)(2,1)S(1)}, bf16[4,256,256]{2,1,0:T(8,128)(2,1)S(1)}, u32[]{:S(2)}, u32[]{:S(2)}) %collective-permute-start.5) | collective-permute-done | bytes 524320 | tf_op jit(solution)/shard_map/ppermute | solution.py:45
  45.6 0.0 copy-start.3
  45.6 0.8 copy-done.3
  46.4 0.0 collective-permute-done.4.a2
  46.4 2.7 %collective-permute-done.3.a1 = bf16[4,256,256]{2,1,0:T(8,128)(2,1)} collective-permute-done((bf16[4,256,256]{2,1,0:T(8,128)(2,1)S(1)}, bf16[4,256,256]{2,1,0:T(8,128)(2,1)}, u32[]{:S(2)}, u32[]{:S(2)}) %collective-permute-start.3) | collective-permute-done | bytes 524320 | tf_op jit(solution)/shard_map/ppermute | solution.py:45
  49.1 0.0 all-to-all-done
  49.1 0.0 copy-done.5
  49.1 1.0 copy-done.4
  50.1 17.9 %tree_attention.1 = (bf16[768,1024]{1,0:T(8,128)(2,1)}, f32[256,256]{1,0:T(8,128)S(1)}, bf16[512,256]{1,0:T(8,128)(2,1)S(1)}, bf16[4,256,256]{2,1,0:T(8,128)(2,1...) custom-call(s32[2]{0:T(128)S(1)} %pad_add_fusion.here, ...), custom_call_target="tpu_custom_call" | custom-call | flops 7247757312 | bytes 3145728 | tf_op jit(solution)/shard_map/tree_attention/pallas_call | solution.py:276
  68.0 0.0 copy-start.1
  68.0 0.7 copy-done.1
  68.7 0.0 collective-permute-start.6
  68.7 2.3 %collective-permute-start.7 = (bf16[4,256,256]{2,1,0:T(8,128)(2,1)}, bf16[4,256,256]{2,1,0:T(8,128)(2,1)}, u32[]{:S(2)}, u32[]{:S(2)}) collective-permute-start(bf16[4,256,256]{2,1,0:T(8,128)(2,1)} %get-tuple-element.17), channel_id=1, source_target_pairs={{0,96},{1,17},{2,98},{3,19},{4,100},{5,21},{6,102},{7,23},{8,104},... | collective-permute-start | bytes 1572872 | tf_op jit(solution)/shard_map/ppermute | solution.py:45
  71.0 0.4 collective-permute-start.8
  71.4 7.6 %all-to-all-start.2 = ((bf16[8,96,1024]{2,1,0:T(8,128)(2,1)}), bf16[8,96,1024]{2,1,0:T(8,128)(2,1)S(1)}, u32[]{:S(2)}, u32[]{:S(2)}) async-start(bf16[8,96,1024]{2,1,0:T(8,128)(2,1)} %bitcast.10), calls=%async_computation.2 | async-start | bytes 3145728 | tf_op jit(solution)/shard_map/all_to_all | solution.py:294
  79.0 5.2 %collective-permute-done.6 = bf16[4,256,256]{2,1,0:T(8,128)(2,1)S(1)} collective-permute-done((bf16[4,256,256]{2,1,0:T(8,128)(2,1)}, bf16[4,256,256]{2,1,0:T(8,128)(2,1)S(1)}, u32[]{:S(2)}, u32[]{:S(2)}) %collective-permute-start.6) | collective-permute-done | bytes 524320 | tf_op jit(solution)/shard_map/ppermute | solution.py:45
  84.2 0.0 collective-permute-done.7
  84.2 0.6 collective-permute-done.8
  84.8 1.3 %add_convert_fusion = bf16[3,256,256]{2,1,0:T(8,128)(2,1)S(1)} fusion(bf16[4,256,256]{2,1,0:T(8,128)(2,1)} %collective-permute-done.8, bf16[4,256,256]{2,1,0:T(8,128)(2,1)} %collective-permute-done.7, bf16[4,256,256]{2,1,0:T(8,128)(2,1)S(1)} %collective-permute-done.6, bf16[4,256,256]{2,1,0:T(8,128)(2,1)S(1)} %get-tuple-element.15), kind=kLoop, calls=%fused_computation.5 | loop fusion | flops 1572864 | bytes 1966080 | tf_op jit(solution)/shard_map/convert_element_type | solution.py:328
  86.2 2.7 %collective-permute-start.9 = (bf16[256,256]{1,0:T(8,128)(2,1)S(1)}, bf16[256,256]{1,0:T(8,128)(2,1)S(1)}, u32[]{:S(2)}, u32[]{:S(2)}) collective-permute-start(bf16[256,256]{1,0:T(8,128)(2,1)S(1)} %get-tuple-element.26), channel_id=1, source_target_pairs={{0,16},{1,97},{2,18},{3,99},{4,20},{5,101},{6,22},{7,103},{8,24},{... | collective-permute-start | bytes 393224 | tf_op jit(solution)/shard_map/ppermute | solution.py:45
  88.9 0.1 collective-permute-start.11
  89.0 1.4 %collective-permute-start.10 = (bf16[256,256]{1,0:T(8,128)(2,1)S(1)}, bf16[256,256]{1,0:T(8,128)(2,1)S(1)}, u32[]{:S(2)}, u32[]{:S(2)}) collective-permute-start(bf16[256,256]{1,0:T(8,128)(2,1)S(1)} %get-tuple-element.28), channel_id=1, source_target_pairs={{0,8},{1,33},{2,10},{3,35},{4,12},{5,37},{6,14},{7,39},{8,16},{9,4... | collective-permute-start | bytes 393224 | tf_op jit(solution)/shard_map/ppermute | solution.py:45
  90.4 0.0 copy-done.2
  90.4 1.1 bitcast_add_fusion
  91.4 0.2 collective-permute-done.9
  91.6 1.4 %collective-permute-done.11 = bf16[256,256]{1,0:T(8,128)(2,1)S(1)} collective-permute-done((bf16[256,256]{1,0:T(8,128)(2,1)S(1)}, bf16[256,256]{1,0:T(8,128)(2,1)S(1)}, u32[]{:S(2)}, u32[]{:S(2)}) %collective-permute-start.11) | collective-permute-done | bytes 131104 | tf_op jit(solution)/shard_map/ppermute | solution.py:45
  93.0 1.3 %collective-permute-done.10 = bf16[256,256]{1,0:T(8,128)(2,1)S(1)} collective-permute-done((bf16[256,256]{1,0:T(8,128)(2,1)S(1)}, bf16[256,256]{1,0:T(8,128)(2,1)S(1)}, u32[]{:S(2)}, u32[]{:S(2)}) %collective-permute-start.10) | collective-permute-done | bytes 131104 | tf_op jit(solution)/shard_map/ppermute | solution.py:45
  94.3 0.1 add_convert_fusion.1
  94.4 0.8 pad_maximum_fusion.1
  95.1 4.6 %all-to-all-done.2 = bf16[8,96,1024]{2,1,0:T(8,128)(2,1)S(1)} async-done(((bf16[8,96,1024]{2,1,0:T(8,128)(2,1)}), bf16[8,96,1024]{2,1,0:T(8,128)(2,1)S(1)}, u32[]{:S(2)}, u32[]{:S(2)}) %all-to-all-start.2) | async-done | bytes 1572896 | tf_op jit(solution)/shard_map/all_to_all | solution.py:294
  99.7 4.2 %all-to-all-start.3 = ((bf16[8,96,256]{2,1,0:T(8,128)(2,1)}), bf16[8,96,256]{2,1,0:T(8,128)(2,1)S(1)}, u32[]{:S(2)}, u32[]{:S(2)}) async-start(bf16[8,96,256]{2,1,0:T(8,128)(2,1)} %bitcast.16), calls=%async_computation.3 | async-start | bytes 786432 | tf_op jit(solution)/shard_map/all_to_all | solution.py:294
  104.0 0.1 slice_bitcast_fusion
  104.1 0.9 copy.23
  105.1 0.9 copy.22
  106.0 6.0 %all-to-all-done.3 = bf16[8,96,256]{2,1,0:T(8,128)(2,1)S(1)} async-done(((bf16[8,96,256]{2,1,0:T(8,128)(2,1)}), bf16[8,96,256]{2,1,0:T(8,128)(2,1)S(1)}, u32[]{:S(2)}, u32[]{:S(2)}) %all-to-all-start.3) | async-done | bytes 393248 | tf_op jit(solution)/shard_map/all_to_all | solution.py:294
  112.1 0.1 slice_bitcast_fusion.2
  112.1 0.7 copy.32
  112.9 0.7 copy.33
  (6 shorter events, 0.1 us)
Async XLA Ops:
  0.6 0.9 copy-start
  0.6 8.5 %copy-start.6 = (bf16[96,4096]{1,0:T(8,128)(2,1)S(1)}, bf16[96,4096]{1,0:T(8,128)(2,1)}, u32[]{:S(2)}) copy-start(bf16[96,4096]{1,0:T(8,128)(2,1)} %param.9) | copy-start | bytes 2359300
  0.7 8.5 %copy-start.7 = (bf16[96,4096]{1,0:T(8,128)(2,1)S(1)}, bf16[96,4096]{1,0:T(8,128)(2,1)}, u32[]{:S(2)}) copy-start(bf16[96,4096]{1,0:T(8,128)(2,1)} %param.6) | copy-start | bytes 2359300
  3.4 13.9 %all-to-all-start.1 = ((bf16[8,96,256]{2,1,0:T(8,128)(2,1)}), bf16[8,96,256]{2,1,0:T(8,128)(2,1)S(1)}, u32[]{:S(2)}, u32[]{:S(2)}) async-start(bf16[8,96,256]{2,1,0:T(8,128)(2,1)} %maximum_bitcast_fusion.1), calls=%async_computation.1 | async-start | bytes 786432 | tf_op jit(solution)/shard_map/all_to_all | solution.py:294
  10.7 23.8 %copy-start.8 = (s32[768]{0:T(1024)S(1)}, s32[768]{0:T(1024)}, u32[]{:S(2)}) copy-start(s32[768]{0:T(1024)} %param.11) | copy-start | bytes 9220
  10.7 38.4 %copy-start.5 = (s32[48]{0:T(128)S(1)}, s32[48]{0:T(128)}, u32[]{:S(2)}) copy-start(s32[48]{0:T(128)} %parent.1) | copy-start | bytes 580
  17.2 31.9 %all-to-all-start = ((bf16[8,96,1024]{2,1,0:T(8,128)(2,1)}), bf16[8,96,1024]{2,1,0:T(8,128)(2,1)S(1)}, u32[]{:S(2)}, u32[]{:S(2)}) async-start(bf16[8,96,1024]{2,1,0:T(8,128)(2,1)} %maximum_bitcast_fusion), calls=%async_computation | async-start | bytes 3145728 | tf_op jit(solution)/shard_map/all_to_all | solution.py:294
  21.6 5.7 %collective-permute-start.1 = (bf16[256,256]{1,0:T(8,128)(2,1)S(1)}, bf16[256,256]{1,0:T(8,128)(2,1)S(1)}, u32[]{:S(2)}, u32[]{:S(2)}) collective-permute-start(bf16[256,256]{1,0:T(8,128)(2,1)S(1)} %get-tuple-element.30), channel_id=1, source_target_pairs={{0,16},{1,65},{2,18},{3,67},{4,20},{5,69},{6,22},{7,71},{8,24},{9,... | collective-permute-start | bytes 393224 | tf_op jit(solution)/shard_map/ppermute | solution.py:45
  24.6 5.1 %collective-permute-start = (bf16[256,256]{1,0:T(8,128)(2,1)S(1)}, bf16[256,256]{1,0:T(8,128)(2,1)S(1)}, u32[]{:S(2)}, u32[]{:S(2)}) collective-permute-start(bf16[256,256]{1,0:T(8,128)(2,1)S(1)} %get-tuple-element.30), channel_id=1, source_target_pairs={{0,8},{1,33},{2,10},{3,35},{4,12},{5,37},{6,14},{7,39},{8,16},{9,4... | collective-permute-start | bytes 393224 | tf_op jit(solution)/shard_map/ppermute | solution.py:45
  25.0 4.7 %collective-permute-start.2 = (bf16[256,256]{1,0:T(8,128)(2,1)S(1)}, bf16[256,256]{1,0:T(8,128)(2,1)S(1)}, u32[]{:S(2)}, u32[]{:S(2)}) collective-permute-start(bf16[256,256]{1,0:T(8,128)(2,1)S(1)} %get-tuple-element.30), channel_id=1, source_target_pairs={{0,24},{1,97},{2,26},{3,99},{4,28},{5,101},{6,30},{7,103},{8,0},{9... | collective-permute-start | bytes 393224 | tf_op jit(solution)/shard_map/ppermute | solution.py:45
  29.8 15.8 %collective-permute-start.5 = (bf16[4,256,256]{2,1,0:T(8,128)(2,1)S(1)}, bf16[4,256,256]{2,1,0:T(8,128)(2,1)S(1)}, u32[]{:S(2)}, u32[]{:S(2)}) collective-permute-start(bf16[4,256,256]{2,1,0:T(8,128)(2,1)S(1)} %pad_maximum_fusion.a0), channel_id=1, source_target_pairs={{0,96},{1,25},{2,98},{3,27},{4,100},{5,29},{6,102},{7,31},{8,104},... | collective-permute-start | bytes 1572872 | tf_op jit(solution)/shard_map/ppermute | solution.py:45
  33.8 12.5 %collective-permute-start.4 = (bf16[4,256,256]{2,1,0:T(8,128)(2,1)S(1)}, bf16[4,256,256]{2,1,0:T(8,128)(2,1)}, u32[]{:S(2)}, u32[]{:S(2)}) collective-permute-start(bf16[4,256,256]{2,1,0:T(8,128)(2,1)S(1)} %pad_maximum_fusion.a0), channel_id=1, source_target_pairs={{0,64},{1,17},{2,66},{3,19},{4,68},{5,21},{6,70},{7,23},{8,72},{9,... | collective-permute-start | bytes 1572872 | tf_op jit(solution)/shard_map/ppermute | solution.py:45
  33.8 15.3 %collective-permute-start.3 = (bf16[4,256,256]{2,1,0:T(8,128)(2,1)S(1)}, bf16[4,256,256]{2,1,0:T(8,128)(2,1)}, u32[]{:S(2)}, u32[]{:S(2)}) collective-permute-start(bf16[4,256,256]{2,1,0:T(8,128)(2,1)S(1)} %pad_maximum_fusion.a0), channel_id=1, source_target_pairs={{0,32},{1,9},{2,34},{3,11},{4,36},{5,13},{6,38},{7,15},{8,40},{9,1... | collective-permute-start | bytes 1572872 | tf_op jit(solution)/shard_map/ppermute | solution.py:45
  45.6 0.8 copy-start.3
  49.1 1.0 copy-start.4
  68.0 0.7 copy-start.1
  68.7 15.5 %collective-permute-start.6 = (bf16[4,256,256]{2,1,0:T(8,128)(2,1)}, bf16[4,256,256]{2,1,0:T(8,128)(2,1)S(1)}, u32[]{:S(2)}, u32[]{:S(2)}) collective-permute-start(bf16[4,256,256]{2,1,0:T(8,128)(2,1)} %get-tuple-element.16), channel_id=1, source_target_pairs={{0,32},{1,9},{2,34},{3,11},{4,36},{5,13},{6,38},{7,15},{8,40},{9,1... | collective-permute-start | bytes 1572872 | tf_op jit(solution)/shard_map/ppermute | solution.py:45
  68.7 15.5 %collective-permute-start.7 = (bf16[4,256,256]{2,1,0:T(8,128)(2,1)}, bf16[4,256,256]{2,1,0:T(8,128)(2,1)}, u32[]{:S(2)}, u32[]{:S(2)}) collective-permute-start(bf16[4,256,256]{2,1,0:T(8,128)(2,1)} %get-tuple-element.17), channel_id=1, source_target_pairs={{0,96},{1,17},{2,98},{3,19},{4,100},{5,21},{6,102},{7,23},{8,104},... | collective-permute-start | bytes 1572872 | tf_op jit(solution)/shard_map/ppermute | solution.py:45
  71.0 13.8 %collective-permute-start.8 = (bf16[4,256,256]{2,1,0:T(8,128)(2,1)}, bf16[4,256,256]{2,1,0:T(8,128)(2,1)}, u32[]{:S(2)}, u32[]{:S(2)}) collective-permute-start(bf16[4,256,256]{2,1,0:T(8,128)(2,1)} %get-tuple-element.18), channel_id=1, source_target_pairs={{0,96},{1,25},{2,98},{3,27},{4,100},{5,29},{6,102},{7,31},{8,104},... | collective-permute-start | bytes 1572872 | tf_op jit(solution)/shard_map/ppermute | solution.py:45
  71.4 28.3 %all-to-all-start.2 = ((bf16[8,96,1024]{2,1,0:T(8,128)(2,1)}), bf16[8,96,1024]{2,1,0:T(8,128)(2,1)S(1)}, u32[]{:S(2)}, u32[]{:S(2)}) async-start(bf16[8,96,1024]{2,1,0:T(8,128)(2,1)} %bitcast.10), calls=%async_computation.2 | async-start | bytes 3145728 | tf_op jit(solution)/shard_map/all_to_all | solution.py:294
  79.0 11.3 %copy-start.2 = (f32[256,256]{1,0:T(8,128)S(1)}, f32[256,256]{1,0:T(8,128)}, u32[]{:S(2)}) copy-start(f32[256,256]{1,0:T(8,128)} %copy-done.1) | copy-start | bytes 786436
  86.2 5.4 %collective-permute-start.9 = (bf16[256,256]{1,0:T(8,128)(2,1)S(1)}, bf16[256,256]{1,0:T(8,128)(2,1)S(1)}, u32[]{:S(2)}, u32[]{:S(2)}) collective-permute-start(bf16[256,256]{1,0:T(8,128)(2,1)S(1)} %get-tuple-element.26), channel_id=1, source_target_pairs={{0,16},{1,97},{2,18},{3,99},{4,20},{5,101},{6,22},{7,103},{8,24},{... | collective-permute-start | bytes 393224 | tf_op jit(solution)/shard_map/ppermute | solution.py:45
  88.9 4.1 %collective-permute-start.11 = (bf16[256,256]{1,0:T(8,128)(2,1)S(1)}, bf16[256,256]{1,0:T(8,128)(2,1)S(1)}, u32[]{:S(2)}, u32[]{:S(2)}) collective-permute-start(bf16[256,256]{1,0:T(8,128)(2,1)S(1)} %get-tuple-element.27), channel_id=1, source_target_pairs={{0,24},{1,97},{2,26},{3,99},{4,28},{5,101},{6,30},{7,103},{8,0},{9... | collective-permute-start | bytes 393224 | tf_op jit(solution)/shard_map/ppermute | solution.py:45
  89.0 5.3 %collective-permute-start.10 = (bf16[256,256]{1,0:T(8,128)(2,1)S(1)}, bf16[256,256]{1,0:T(8,128)(2,1)S(1)}, u32[]{:S(2)}, u32[]{:S(2)}) collective-permute-start(bf16[256,256]{1,0:T(8,128)(2,1)S(1)} %get-tuple-element.28), channel_id=1, source_target_pairs={{0,8},{1,33},{2,10},{3,35},{4,12},{5,37},{6,14},{7,39},{8,16},{9,4... | collective-permute-start | bytes 393224 | tf_op jit(solution)/shard_map/ppermute | solution.py:45
  99.7 12.3 %all-to-all-start.3 = ((bf16[8,96,256]{2,1,0:T(8,128)(2,1)}), bf16[8,96,256]{2,1,0:T(8,128)(2,1)S(1)}, u32[]{:S(2)}, u32[]{:S(2)}) async-start(bf16[8,96,256]{2,1,0:T(8,128)(2,1)} %bitcast.16), calls=%async_computation.3 | async-start | bytes 786432 | tf_op jit(solution)/shard_map/all_to_all | solution.py:294

commit v8 on v7

--- a/solution.py
+++ b/solution.py
@@ -325,9 +325,9 @@
     by = {s: shifted(terms[s], 0, s, False) for s in (2, 1, 3)}
     got = [terms[0]] + [by[s] for s in range(1, SIDE)]
     own = lax.optimization_barrier(dfirst + sum(x[0].astype(F32) for x in got))
-    part = sum(x[1:].astype(F32) for x in got).astype(BF16)
     for s in (2, 1, 3):
-        own = own + shifted(part[s - 1], 1, s, False).astype(F32)
+        part = sum(x[s].astype(F32) for x in got).astype(BF16)
+        own = own + shifted(part, 1, s, False).astype(F32)
     dkv = jnp.concatenate([own.astype(BF16), drest], axis=0)
     out, dkv = lax.optimization_barrier((out, dkv))
     attn_out, grad_q = by_token(out)

time: 114 us -> 114 us (level)
    add x0 -> x1, other arithmetic: none -> 1.42 us  [local(): part = sum((x[s].astype(F32) for x in got)).astype(BF16)]
    convert_element_type x1 -> x0, other arithmetic: 1.33 us -> none  [local(): part = sum((x[1:].astype(F32) for x in got)).astype(BF16)]
where the time goes in v8:
time: 114 us
  waiting for transfers between devices  41.9 us (37%)
  starting transfers between devices  39.3 us (34%)
  Pallas kernels  17.9 us (16%)
  local copies, waits for them, and re-layouts  8.18 us (7%)
  other arithmetic  5.63 us (5%)
    ppermute x12, waiting for transfers between devices, shifted(): return lax.ppermute(x, ('ctx', 'head'), pairs)  24.9 us
    all_to_all x4, starting transfers between devices, swap(): return lax.all_to_all(x, 'head', split_axis=0, concat_axis=0, tiled=True)  22.1 us
    pallas_call x1, Pallas kernels, attention(): pl.pallas_call(functools.partial(attention_kernel, nb), grid_spec=spec, o...  17.9 us
    ppermute x12, starting transfers between devices, shifted(): return lax.ppermute(x, ('ctx', 'head'), pairs)  17.3 us
    all_to_all x4, waiting for transfers between devices, swap(): return lax.all_to_all(x, 'head', split_axis=0, concat_axis=0, tiled=True)  16.9 us
    unnamed x20, local copies, waits for them, and re-layouts  3.66 us
    reshape x4, local copies, waits for them, and re-layouts, by_token(): a.reshape(rows, -1)  3.34 us
  transfers between devices with their start and end apart: 16, of which 11 were waited for; matrix products, arithmetic and copies ran while one was open for 6% of the time, Pallas kernels for 0%

profile of v8, /device:TPU:1, one launch (start us, length us, event | category | flops | bytes accessed | tf_op | source)
XLA Modules:
  0.0 113.6 jit_solution(15627565902075615837)
XLA Ops:
  0.6 0.0 copy-start
  0.6 0.0 copy-start.6
  0.7 0.0 copy-start.7
  0.7 0.9 copy-done
  1.6 1.0 copy_bitcast_fusion.4
  2.6 0.8 maximum_bitcast_fusion.1
  3.4 5.8 %all-to-all-start.1 = ((bf16[8,96,256]{2,1,0:T(8,128)(2,1)}), bf16[8,96,256]{2,1,0:T(8,128)(2,1)S(1)}, u32[]{:S(2)}, u32[]{:S(2)}) async-start(bf16[8,96,256]{2,1,0:T(8,128)(2,1)} %maximum_bitcast_fusion.1), calls=%async_computation.1 | async-start | bytes 786432 | tf_op jit(solution)/shard_map/all_to_all | solution.py:294
  9.2 0.0 copy-done.6
  9.2 0.0 copy-done.7
  9.2 0.2 copy_bitcast_fusion
  9.3 1.4 %maximum_bitcast_fusion = bf16[8,96,1024]{2,1,0:T(8,128)(2,1)} fusion(bf16[96,8,512]{2,0,1:T(8,128)(2,1)S(1)} %get-tuple-element.31, bf16[96,8,512]{2,0,1:T(8,128)(2,1)S(1)} %get-tuple-element.32), kind=kLoop, calls=%fused_computation | loop fusion | flops 3145728 | bytes 3145728 | tf_op jit(solution)/shard_map/transpose | solution.py:306
  10.7 0.0 copy-start.8
  10.7 0.0 copy-start.5
  10.7 6.5 %all-to-all-done.1 = bf16[8,96,256]{2,1,0:T(8,128)(2,1)S(1)} async-done(((bf16[8,96,256]{2,1,0:T(8,128)(2,1)}), bf16[8,96,256]{2,1,0:T(8,128)(2,1)S(1)}, u32[]{:S(2)}, u32[]{:S(2)}) %all-to-all-start.1) | async-done | bytes 393248 | tf_op jit(solution)/shard_map/all_to_all | solution.py:294
  17.2 4.4 %all-to-all-start = ((bf16[8,96,1024]{2,1,0:T(8,128)(2,1)}), bf16[8,96,1024]{2,1,0:T(8,128)(2,1)S(1)}, u32[]{:S(2)}, u32[]{:S(2)}) async-start(bf16[8,96,1024]{2,1,0:T(8,128)(2,1)} %maximum_bitcast_fusion), calls=%async_computation | async-start | bytes 3145728 | tf_op jit(solution)/shard_map/all_to_all | solution.py:294
  21.6 3.0 %collective-permute-start.1 = (bf16[256,256]{1,0:T(8,128)(2,1)S(1)}, bf16[256,256]{1,0:T(8,128)(2,1)S(1)}, u32[]{:S(2)}, u32[]{:S(2)}) collective-permute-start(bf16[256,256]{1,0:T(8,128)(2,1)S(1)} %get-tuple-element.30), channel_id=1, source_target_pairs={{0,16},{1,65},{2,18},{3,67},{4,20},{5,69},{6,22},{7,71},{8,24},{9,... | collective-permute-start | bytes 393224 | tf_op jit(solution)/shard_map/ppermute | solution.py:45
  24.6 0.4 collective-permute-start
  25.0 2.3 %collective-permute-start.2 = (bf16[256,256]{1,0:T(8,128)(2,1)S(1)}, bf16[256,256]{1,0:T(8,128)(2,1)S(1)}, u32[]{:S(2)}, u32[]{:S(2)}) collective-permute-start(bf16[256,256]{1,0:T(8,128)(2,1)S(1)} %get-tuple-element.30), channel_id=1, source_target_pairs={{0,24},{1,97},{2,26},{3,99},{4,28},{5,101},{6,30},{7,103},{8,0},{9... | collective-permute-start | bytes 393224 | tf_op jit(solution)/shard_map/ppermute | solution.py:45
  27.3 0.0 collective-permute-done.1
  27.3 2.4 %collective-permute-done = bf16[256,256]{1,0:T(8,128)(2,1)S(1)} collective-permute-done((bf16[256,256]{1,0:T(8,128)(2,1)S(1)}, bf16[256,256]{1,0:T(8,128)(2,1)S(1)}, u32[]{:S(2)}, u32[]{:S(2)}) %collective-permute-start) | collective-permute-done | bytes 131104 | tf_op jit(solution)/shard_map/ppermute | solution.py:45
  29.7 0.0 collective-permute-done.2
  29.7 0.1 pad_maximum_fusion.a0
  29.8 4.1 %collective-permute-start.5 = (bf16[4,256,256]{2,1,0:T(8,128)(2,1)S(1)}, bf16[4,256,256]{2,1,0:T(8,128)(2,1)S(1)}, u32[]{:S(2)}, u32[]{:S(2)}) collective-permute-start(bf16[4,256,256]{2,1,0:T(8,128)(2,1)S(1)} %pad_maximum_fusion.a0), channel_id=1, source_target_pairs={{0,96},{1,25},{2,98},{3,27},{4,100},{5,29},{6,102},{7,31},{8,104},... | collective-permute-start | bytes 1572872 | tf_op jit(solution)/shard_map/ppermute | solution.py:45
  33.8 0.0 collective-permute-start.4
  33.8 0.7 collective-permute-start.3
  34.5 0.0 copy-done.8
  34.5 0.1 pad_add_fusion.here
  34.6 11.0 %collective-permute-done.5.a3 = bf16[4,256,256]{2,1,0:T(8,128)(2,1)S(1)} collective-permute-done((bf16[4,256,256]{2,1,0:T(8,128)(2,1)S(1)}, bf16[4,256,256]{2,1,0:T(8,128)(2,1)S(1)}, u32[]{:S(2)}, u32[]{:S(2)}) %collective-permute-start.5) | collective-permute-done | bytes 524320 | tf_op jit(solution)/shard_map/ppermute | solution.py:45
  45.6 0.8 copy-done.3
  46.4 0.0 collective-permute-done.4.a2
  46.4 2.7 %collective-permute-done.3.a1 = bf16[4,256,256]{2,1,0:T(8,128)(2,1)} collective-permute-done((bf16[4,256,256]{2,1,0:T(8,128)(2,1)S(1)}, bf16[4,256,256]{2,1,0:T(8,128)(2,1)}, u32[]{:S(2)}, u32[]{:S(2)}) %collective-permute-start.3) | collective-permute-done | bytes 524320 | tf_op jit(solution)/shard_map/ppermute | solution.py:45
  49.1 0.0 all-to-all-done
  49.1 0.0 copy-done.5
  49.1 1.0 copy-done.4
  50.1 17.9 %tree_attention.1 = (bf16[768,1024]{1,0:T(8,128)(2,1)}, f32[256,256]{1,0:T(8,128)S(1)}, bf16[512,256]{1,0:T(8,128)(2,1)S(1)}, bf16[4,256,256]{2,1,0:T(8,128)(2,1...) custom-call(s32[2]{0:T(128)S(1)} %pad_add_fusion.here, ...), custom_call_target="tpu_custom_call" | custom-call | flops 7247757312 | bytes 3145728 | tf_op jit(solution)/shard_map/tree_attention/pallas_call | solution.py:276
  68.0 0.0 copy-start.1
  68.0 0.7 copy-done.1
  68.7 0.0 collective-permute-start.6
  68.7 2.3 %collective-permute-start.7 = (bf16[4,256,256]{2,1,0:T(8,128)(2,1)}, bf16[4,256,256]{2,1,0:T(8,128)(2,1)}, u32[]{:S(2)}, u32[]{:S(2)}) collective-permute-start(bf16[4,256,256]{2,1,0:T(8,128)(2,1)} %get-tuple-element.17), channel_id=1, source_target_pairs={{0,96},{1,17},{2,98},{3,19},{4,100},{5,21},{6,102},{7,23},{8,104},... | collective-permute-start | bytes 1572872 | tf_op jit(solution)/shard_map/ppermute | solution.py:45
  71.0 0.4 collective-permute-start.8
  71.4 7.5 %all-to-all-start.2 = ((bf16[8,96,1024]{2,1,0:T(8,128)(2,1)}), bf16[8,96,1024]{2,1,0:T(8,128)(2,1)S(1)}, u32[]{:S(2)}, u32[]{:S(2)}) async-start(bf16[8,96,1024]{2,1,0:T(8,128)(2,1)} %bitcast.10), calls=%async_computation.2 | async-start | bytes 3145728 | tf_op jit(solution)/shard_map/all_to_all | solution.py:294
  78.9 5.3 %collective-permute-done.6 = bf16[4,256,256]{2,1,0:T(8,128)(2,1)S(1)} collective-permute-done((bf16[4,256,256]{2,1,0:T(8,128)(2,1)}, bf16[4,256,256]{2,1,0:T(8,128)(2,1)S(1)}, u32[]{:S(2)}, u32[]{:S(2)}) %collective-permute-start.6) | collective-permute-done | bytes 524320 | tf_op jit(solution)/shard_map/ppermute | solution.py:45
  84.2 0.0 collective-permute-done.7
  84.2 0.6 collective-permute-done.8
  84.8 1.4 %fusion = (bf16[256,256]{1,0:T(8,128)(2,1)S(1)}, bf16[256,256]{1,0:T(8,128)(2,1)S(1)}, bf16[256,256]{1,0:T(8,128)(2,1)S(1)}) fusion(bf16[4,256,256]{2,1,0:T(8,128)(2,1)} %collective-permute-done.8, bf16[4,256,256]{2,1,0:T(8,128)(2,1)} %collective-permute-done.7, bf16[4,256,256]{2,1,0:T(8,128)(2,1)S(1)} %collective-permute-done.6, ...), kind=kLoop, calls=%fused_computation.19 | loop fusion | flops 1572864 | bytes 1966080 | tf_op jit(solution)/shard_map/add | solution.py:329
  86.2 2.7 %collective-permute-start.9 = (bf16[256,256]{1,0:T(8,128)(2,1)S(1)}, bf16[256,256]{1,0:T(8,128)(2,1)S(1)}, u32[]{:S(2)}, u32[]{:S(2)}) collective-permute-start(bf16[256,256]{1,0:T(8,128)(2,1)S(1)} %get-tuple-element.22), channel_id=1, source_target_pairs={{0,16},{1,97},{2,18},{3,99},{4,20},{5,101},{6,22},{7,103},{8,24},{... | collective-permute-start | bytes 393224 | tf_op jit(solution)/shard_map/ppermute | solution.py:45
  89.0 0.1 collective-permute-start.11
  89.0 1.4 %collective-permute-start.10 = (bf16[256,256]{1,0:T(8,128)(2,1)S(1)}, bf16[256,256]{1,0:T(8,128)(2,1)S(1)}, u32[]{:S(2)}, u32[]{:S(2)}) collective-permute-start(bf16[256,256]{1,0:T(8,128)(2,1)S(1)} %get-tuple-element.24), channel_id=1, source_target_pairs={{0,8},{1,33},{2,10},{3,35},{4,12},{5,37},{6,14},{7,39},{8,16},{9,4... | collective-permute-start | bytes 393224 | tf_op jit(solution)/shard_map/ppermute | solution.py:45
  90.4 0.0 copy-done.2
  90.4 1.1 bitcast_add_fusion
  91.5 0.1 collective-permute-done.9
  91.6 1.5 %collective-permute-done.11 = bf16[256,256]{1,0:T(8,128)(2,1)S(1)} collective-permute-done((bf16[256,256]{1,0:T(8,128)(2,1)S(1)}, bf16[256,256]{1,0:T(8,128)(2,1)S(1)}, u32[]{:S(2)}, u32[]{:S(2)}) %collective-permute-start.11) | collective-permute-done | bytes 131104 | tf_op jit(solution)/shard_map/ppermute | solution.py:45
  93.1 1.3 %collective-permute-done.10 = bf16[256,256]{1,0:T(8,128)(2,1)S(1)} collective-permute-done((bf16[256,256]{1,0:T(8,128)(2,1)S(1)}, bf16[256,256]{1,0:T(8,128)(2,1)S(1)}, u32[]{:S(2)}, u32[]{:S(2)}) %collective-permute-start.10) | collective-permute-done | bytes 131104 | tf_op jit(solution)/shard_map/ppermute | solution.py:45
  94.4 0.1 add_convert_fusion
  94.4 0.8 pad_maximum_fusion.1
  95.2 4.4 %all-to-all-done.2 = bf16[8,96,1024]{2,1,0:T(8,128)(2,1)S(1)} async-done(((bf16[8,96,1024]{2,1,0:T(8,128)(2,1)}), bf16[8,96,1024]{2,1,0:T(8,128)(2,1)S(1)}, u32[]{:S(2)}, u32[]{:S(2)}) %all-to-all-start.2) | async-done | bytes 1572896 | tf_op jit(solution)/shard_map/all_to_all | solution.py:294
  99.6 4.4 %all-to-all-start.3 = ((bf16[8,96,256]{2,1,0:T(8,128)(2,1)}), bf16[8,96,256]{2,1,0:T(8,128)(2,1)S(1)}, u32[]{:S(2)}, u32[]{:S(2)}) async-start(bf16[8,96,256]{2,1,0:T(8,128)(2,1)} %bitcast.16), calls=%async_computation.3 | async-start | bytes 786432 | tf_op jit(solution)/shard_map/all_to_all | solution.py:294
  104.0 0.1 slice_bitcast_fusion
  104.2 0.9 copy.23
  105.1 0.9 copy.22
  106.1 6.0 %all-to-all-done.3 = bf16[8,96,256]{2,1,0:T(8,128)(2,1)S(1)} async-done(((bf16[8,96,256]{2,1,0:T(8,128)(2,1)}), bf16[8,96,256]{2,1,0:T(8,128)(2,1)S(1)}, u32[]{:S(2)}, u32[]{:S(2)}) %all-to-all-start.3) | async-done | bytes 393248 | tf_op jit(solution)/shard_map/all_to_all | solution.py:294
  112.1 0.1 slice_bitcast_fusion.2
  112.2 0.7 copy.32
  112.9 0.7 copy.33
  (5 shorter events, 0.0 us)
Async XLA Ops:
  0.6 0.9 copy-start
  0.6 8.5 %copy-start.6 = (bf16[96,4096]{1,0:T(8,128)(2,1)S(1)}, bf16[96,4096]{1,0:T(8,128)(2,1)}, u32[]{:S(2)}) copy-start(bf16[96,4096]{1,0:T(8,128)(2,1)} %param.9) | copy-start | bytes 2359300
  0.7 8.5 %copy-start.7 = (bf16[96,4096]{1,0:T(8,128)(2,1)S(1)}, bf16[96,4096]{1,0:T(8,128)(2,1)}, u32[]{:S(2)}) copy-start(bf16[96,4096]{1,0:T(8,128)(2,1)} %param.6) | copy-start | bytes 2359300
  3.4 13.9 %all-to-all-start.1 = ((bf16[8,96,256]{2,1,0:T(8,128)(2,1)}), bf16[8,96,256]{2,1,0:T(8,128)(2,1)S(1)}, u32[]{:S(2)}, u32[]{:S(2)}) async-start(bf16[8,96,256]{2,1,0:T(8,128)(2,1)} %maximum_bitcast_fusion.1), calls=%async_computation.1 | async-start | bytes 786432 | tf_op jit(solution)/shard_map/all_to_all | solution.py:294
  10.7 23.8 %copy-start.8 = (s32[768]{0:T(1024)S(1)}, s32[768]{0:T(1024)}, u32[]{:S(2)}) copy-start(s32[768]{0:T(1024)} %param.11) | copy-start | bytes 9220
  10.7 38.4 %copy-start.5 = (s32[48]{0:T(128)S(1)}, s32[48]{0:T(128)}, u32[]{:S(2)}) copy-start(s32[48]{0:T(128)} %parent.1) | copy-start | bytes 580
  17.2 31.9 %all-to-all-start = ((bf16[8,96,1024]{2,1,0:T(8,128)(2,1)}), bf16[8,96,1024]{2,1,0:T(8,128)(2,1)S(1)}, u32[]{:S(2)}, u32[]{:S(2)}) async-start(bf16[8,96,1024]{2,1,0:T(8,128)(2,1)} %maximum_bitcast_fusion), calls=%async_computation | async-start | bytes 3145728 | tf_op jit(solution)/shard_map/all_to_all | solution.py:294
  21.6 5.7 %collective-permute-start.1 = (bf16[256,256]{1,0:T(8,128)(2,1)S(1)}, bf16[256,256]{1,0:T(8,128)(2,1)S(1)}, u32[]{:S(2)}, u32[]{:S(2)}) collective-permute-start(bf16[256,256]{1,0:T(8,128)(2,1)S(1)} %get-tuple-element.30), channel_id=1, source_target_pairs={{0,16},{1,65},{2,18},{3,67},{4,20},{5,69},{6,22},{7,71},{8,24},{9,... | collective-permute-start | bytes 393224 | tf_op jit(solution)/shard_map/ppermute | solution.py:45
  24.6 5.1 %collective-permute-start = (bf16[256,256]{1,0:T(8,128)(2,1)S(1)}, bf16[256,256]{1,0:T(8,128)(2,1)S(1)}, u32[]{:S(2)}, u32[]{:S(2)}) collective-permute-start(bf16[256,256]{1,0:T(8,128)(2,1)S(1)} %get-tuple-element.30), channel_id=1, source_target_pairs={{0,8},{1,33},{2,10},{3,35},{4,12},{5,37},{6,14},{7,39},{8,16},{9,4... | collective-permute-start | bytes 393224 | tf_op jit(solution)/shard_map/ppermute | solution.py:45
  25.0 4.7 %collective-permute-start.2 = (bf16[256,256]{1,0:T(8,128)(2,1)S(1)}, bf16[256,256]{1,0:T(8,128)(2,1)S(1)}, u32[]{:S(2)}, u32[]{:S(2)}) collective-permute-start(bf16[256,256]{1,0:T(8,128)(2,1)S(1)} %get-tuple-element.30), channel_id=1, source_target_pairs={{0,24},{1,97},{2,26},{3,99},{4,28},{5,101},{6,30},{7,103},{8,0},{9... | collective-permute-start | bytes 393224 | tf_op jit(solution)/shard_map/ppermute | solution.py:45
  29.8 15.8 %collective-permute-start.5 = (bf16[4,256,256]{2,1,0:T(8,128)(2,1)S(1)}, bf16[4,256,256]{2,1,0:T(8,128)(2,1)S(1)}, u32[]{:S(2)}, u32[]{:S(2)}) collective-permute-start(bf16[4,256,256]{2,1,0:T(8,128)(2,1)S(1)} %pad_maximum_fusion.a0), channel_id=1, source_target_pairs={{0,96},{1,25},{2,98},{3,27},{4,100},{5,29},{6,102},{7,31},{8,104},... | collective-permute-start | bytes 1572872 | tf_op jit(solution)/shard_map/ppermute | solution.py:45
  33.8 12.5 %collective-permute-start.4 = (bf16[4,256,256]{2,1,0:T(8,128)(2,1)S(1)}, bf16[4,256,256]{2,1,0:T(8,128)(2,1)}, u32[]{:S(2)}, u32[]{:S(2)}) collective-permute-start(bf16[4,256,256]{2,1,0:T(8,128)(2,1)S(1)} %pad_maximum_fusion.a0), channel_id=1, source_target_pairs={{0,64},{1,17},{2,66},{3,19},{4,68},{5,21},{6,70},{7,23},{8,72},{9,... | collective-permute-start | bytes 1572872 | tf_op jit(solution)/shard_map/ppermute | solution.py:45
  33.8 15.3 %collective-permute-start.3 = (bf16[4,256,256]{2,1,0:T(8,128)(2,1)S(1)}, bf16[4,256,256]{2,1,0:T(8,128)(2,1)}, u32[]{:S(2)}, u32[]{:S(2)}) collective-permute-start(bf16[4,256,256]{2,1,0:T(8,128)(2,1)S(1)} %pad_maximum_fusion.a0), channel_id=1, source_target_pairs={{0,32},{1,9},{2,34},{3,11},{4,36},{5,13},{6,38},{7,15},{8,40},{9,1... | collective-permute-start | bytes 1572872 | tf_op jit(solution)/shard_map/ppermute | solution.py:45
  45.6 0.8 copy-start.3
  49.1 1.0 copy-start.4
  68.0 0.7 copy-start.1
  68.7 15.5 %collective-permute-start.6 = (bf16[4,256,256]{2,1,0:T(8,128)(2,1)}, bf16[4,256,256]{2,1,0:T(8,128)(2,1)S(1)}, u32[]{:S(2)}, u32[]{:S(2)}) collective-permute-start(bf16[4,256,256]{2,1,0:T(8,128)(2,1)} %get-tuple-element.16), channel_id=1, source_target_pairs={{0,32},{1,9},{2,34},{3,11},{4,36},{5,13},{6,38},{7,15},{8,40},{9,1... | collective-permute-start | bytes 1572872 | tf_op jit(solution)/shard_map/ppermute | solution.py:45
  68.7 15.5 %collective-permute-start.7 = (bf16[4,256,256]{2,1,0:T(8,128)(2,1)}, bf16[4,256,256]{2,1,0:T(8,128)(2,1)}, u32[]{:S(2)}, u32[]{:S(2)}) collective-permute-start(bf16[4,256,256]{2,1,0:T(8,128)(2,1)} %get-tuple-element.17), channel_id=1, source_target_pairs={{0,96},{1,17},{2,98},{3,19},{4,100},{5,21},{6,102},{7,23},{8,104},... | collective-permute-start | bytes 1572872 | tf_op jit(solution)/shard_map/ppermute | solution.py:45
  71.0 13.8 %collective-permute-start.8 = (bf16[4,256,256]{2,1,0:T(8,128)(2,1)}, bf16[4,256,256]{2,1,0:T(8,128)(2,1)}, u32[]{:S(2)}, u32[]{:S(2)}) collective-permute-start(bf16[4,256,256]{2,1,0:T(8,128)(2,1)} %get-tuple-element.18), channel_id=1, source_target_pairs={{0,96},{1,25},{2,98},{3,27},{4,100},{5,29},{6,102},{7,31},{8,104},... | collective-permute-start | bytes 1572872 | tf_op jit(solution)/shard_map/ppermute | solution.py:45
  71.4 28.2 %all-to-all-start.2 = ((bf16[8,96,1024]{2,1,0:T(8,128)(2,1)}), bf16[8,96,1024]{2,1,0:T(8,128)(2,1)S(1)}, u32[]{:S(2)}, u32[]{:S(2)}) async-start(bf16[8,96,1024]{2,1,0:T(8,128)(2,1)} %bitcast.10), calls=%async_computation.2 | async-start | bytes 3145728 | tf_op jit(solution)/shard_map/all_to_all | solution.py:294
  78.9 11.5 %copy-start.2 = (f32[256,256]{1,0:T(8,128)S(1)}, f32[256,256]{1,0:T(8,128)}, u32[]{:S(2)}) copy-start(f32[256,256]{1,0:T(8,128)} %copy-done.1) | copy-start | bytes 786436
  86.2 5.4 %collective-permute-start.9 = (bf16[256,256]{1,0:T(8,128)(2,1)S(1)}, bf16[256,256]{1,0:T(8,128)(2,1)S(1)}, u32[]{:S(2)}, u32[]{:S(2)}) collective-permute-start(bf16[256,256]{1,0:T(8,128)(2,1)S(1)} %get-tuple-element.22), channel_id=1, source_target_pairs={{0,16},{1,97},{2,18},{3,99},{4,20},{5,101},{6,22},{7,103},{8,24},{... | collective-permute-start | bytes 393224 | tf_op jit(solution)/shard_map/ppermute | solution.py:45
  89.0 4.1 %collective-permute-start.11 = (bf16[256,256]{1,0:T(8,128)(2,1)S(1)}, bf16[256,256]{1,0:T(8,128)(2,1)S(1)}, u32[]{:S(2)}, u32[]{:S(2)}) collective-permute-start(bf16[256,256]{1,0:T(8,128)(2,1)S(1)} %get-tuple-element.23), channel_id=1, source_target_pairs={{0,24},{1,97},{2,26},{3,99},{4,28},{5,101},{6,30},{7,103},{8,0},{9... | collective-permute-start | bytes 393224 | tf_op jit(solution)/shard_map/ppermute | solution.py:45
  89.0 5.3 %collective-permute-start.10 = (bf16[256,256]{1,0:T(8,128)(2,1)S(1)}, bf16[256,256]{1,0:T(8,128)(2,1)S(1)}, u32[]{:S(2)}, u32[]{:S(2)}) collective-permute-start(bf16[256,256]{1,0:T(8,128)(2,1)S(1)} %get-tuple-element.24), channel_id=1, source_target_pairs={{0,8},{1,33},{2,10},{3,35},{4,12},{5,37},{6,14},{7,39},{8,16},{9,4... | collective-permute-start | bytes 393224 | tf_op jit(solution)/shard_map/ppermute | solution.py:45
  99.6 12.5 %all-to-all-start.3 = ((bf16[8,96,256]{2,1,0:T(8,128)(2,1)}), bf16[8,96,256]{2,1,0:T(8,128)(2,1)S(1)}, u32[]{:S(2)}, u32[]{:S(2)}) async-start(bf16[8,96,256]{2,1,0:T(8,128)(2,1)} %bitcast.16), calls=%async_computation.3 | async-start | bytes 786432 | tf_op jit(solution)/shard_map/all_to_all | solution.py:294
